TPU v7x, 32 devices: a whole 2x2x4 slice. The times are simulated.
32 devices in a mesh: vocab: 16 (over z, y, x), hid: 2 (over core).
Axes of the slice: x: 2, y: 2, z: 4, core: 2. Of those that a mesh axis runs over, the one named last changes fastest.
Arguments:
- hidden_states: bfloat16 [768, 8192], P('vocab', 'hid'), may hold values from -10 to 10
- head_weight: bfloat16 [8192, 20480], P('hid', 'vocab'), may hold values from -8 to 8
- focus_tiles: int32 [256, 2], P('vocab'), may hold values from 0 to 191, as said below
- focus_blocks: bfloat16 [256, 128, 128], P('vocab'), may hold values from -0.5 to 0.5
Outputs:
- student_target: float32 [768, 24576], P('hid', 'vocab')
Inputs may be any that keep to these rules, and one draw needn't show every extreme that they name: `focus_tiles`: rows k * 16 to (k + 1) * 16 - 1 name teacher tiles k * 10 to (k + 1) * 10 - 1 in column 0; column 1 is a student tile, whose owner is the tile divided by 12. Within each such block of rows no owner is named more than 2 times, and one owner, drawn from the seed, is named exactly 2 times in every block; other owners may be named 2 times as well.
All inputs are finite; a program needn't handle non-finite values.
Results may differ from a plain program's by a relative error of at most 0.0035.
Values may be sent and summed in bfloat16 or wider, within the bound.
No kernel may reach another device: no remote copies, remote signals or barrier semaphores. Data moves between devices by JAX's collectives and lax.ppermute only.
A program may use at most 64 MiB of HBM per device.

v0:
```python
import jax
import jax.numpy as jnp
from jax import lax
from jax.sharding import PartitionSpec as P

TILE = 128
STILES_DEV = 12
CAP = 2


def per_device(hidden_states, head_weight, focus_tiles, focus_blocks):
    hid_count = lax.axis_size("hid")
    vocab_count = lax.axis_size("vocab")
    gathered = lax.all_gather(hidden_states, "vocab", axis=0, tiled=True)
    row_count = gathered.shape[0] // hid_count
    logits = lax.psum_scatter(
        jnp.dot(gathered, head_weight, preferred_element_type=jnp.float32),
        "hid",
        scatter_dimension=0,
        tiled=True,
    )
    row_top = lax.pmax(jnp.max(logits, axis=1), "vocab")
    exp_values = jnp.exp(logits - row_top[:, None])
    denominator = lax.psum(jnp.sum(exp_values, axis=1), "vocab")
    weights = exp_values.astype(jnp.bfloat16)
    tiles_here = weights.shape[1] // TILE
    prob_tiles = weights.reshape(row_count, tiles_here, TILE)
    entry_count = focus_tiles.shape[0]
    local_teacher = focus_tiles[:, 0] - lax.axis_index("vocab") * tiles_here
    selector = (local_teacher[:, None] == jnp.arange(tiles_here, dtype=jnp.int32)[None, :]).astype(
        jnp.bfloat16
    )
    chosen = jnp.einsum(
        "et,rtk->erk", selector, prob_tiles, preferred_element_type=jnp.float32
    ).astype(jnp.bfloat16)
    partials = jnp.einsum("erk,ekc->erc", chosen, focus_blocks, preferred_element_type=jnp.float32)
    owner_index = focus_tiles[:, 1] // STILES_DEV
    target_tile = focus_tiles[:, 1] % STILES_DEV
    positions_idx = jnp.arange(entry_count, dtype=jnp.int32)
    same_owner = (owner_index[:, None] == owner_index[None, :]) & (
        positions_idx[None, :] < positions_idx[:, None]
    )
    slot_rank = jnp.sum(same_owner.astype(jnp.int32), axis=1)
    destination = owner_index * CAP + slot_rank
    placement_map = (
        destination[:, None] == jnp.arange(vocab_count * CAP, dtype=jnp.int32)[None, :]
    ).astype(jnp.float32)
    outgoing = jnp.einsum("ed,erc->drc", placement_map, partials, precision=lax.Precision.HIGHEST)
    outgoing = outgoing.reshape(vocab_count, CAP, row_count, TILE)
    tile_labels = jnp.einsum(
        "ed,e->d",
        placement_map,
        target_tile.astype(jnp.float32) + 1.0,
        precision=lax.Precision.HIGHEST,
    )
    tile_labels = tile_labels.reshape(vocab_count, CAP)
    arrived, arrived_labels = (
        lax.all_to_all(outgoing, "vocab", split_axis=0, concat_axis=0, tiled=True),
        lax.all_to_all(tile_labels, "vocab", split_axis=0, concat_axis=0, tiled=True),
    )
    received = arrived.reshape(vocab_count * CAP, row_count, TILE)
    tile_match = (
        arrived_labels.reshape(-1)[:, None]
        == (jnp.arange(STILES_DEV, dtype=jnp.float32) + 1.0)[None, :]
    ).astype(jnp.float32)
    mapped = jnp.einsum("sj,src->rjc", tile_match, received, precision=lax.Precision.HIGHEST)
    mapped = mapped.reshape(row_count, STILES_DEV * TILE)
    student_size = STILES_DEV * TILE * vocab_count
    return student_size * mapped / denominator[:, None]


def solution(mesh):
    return jax.shard_map(
        per_device,
        mesh=mesh,
        in_specs=(P("vocab", "hid"), P("hid", "vocab"), P("vocab", None), P("vocab", None, None)),
        out_specs=P("hid", "vocab"),
        check_vma=False,
    )
```

profile of v0, /device:TPU:10, one launch (start us, length us, event | category | flops | bytes accessed | tf_op | source)
XLA Modules:
  0.0 383.8 jit_solution(9110056030902153758)
XLA Ops:
  6.5 0.7 all-gather.2.cloned.1.call-update
  7.3 0.0 reduce-scatter.2.cloned.1.call-start
  7.3 97.5 %all-gather.2.cloned.1.call-done = bf16[768,4096]{1,0:T(8,128)(2,1)} async-done(((bf16[48,4096]{1,0:T(8,128)(2,1)}), bf16[768,4096]{1,0:T(8,128)(2,1)}) %all-gather.2.cloned.1.call-update) | async-done | bytes 6291472 | tf_op jit(solution)/shard_map/all_gather | solution.py:14
  104.8 13.8 %fusion.33 = f32[768,1280]{1,0:T(8,128)} fusion(bf16[768,4096]{1,0:T(8,128)(2,1)} %all-gather.2.cloned.1.call-done, bf16[4096,1280]{1,0:T(8,128)(2,1)} %param.5), kind=kOutput, calls=%fused_computation.48 | convolution fusion | flops 8053063680 | bytes 20709376 | tf_op jit(solution)/shard_map/dot_general | solution.py:17
  118.7 0.0 reduce-scatter.2.cloned.1.call-update
  118.7 0.6 copy-done.3
  119.4 0.2 convert_reduce_fusion
  119.6 0.1 broadcast_compare_fusion
  119.7 0.1 fusion.6
  119.8 0.8 copy.25
  120.5 5.0 %all-to-all-start.1 = ((f32[16,1,2]{2,1,0:T(1,128)}), f32[16,1,2]{2,1,0:T(1,128)S(1)}, u32[]{:S(2)}, u32[]{:S(2)}) async-start(f32[16,1,2]{2,1,0:T(1,128)} %copy.25), calls=%async_computation.2 | async-start | bytes 16384 | tf_op jit(solution)/shard_map/all_to_all | solution.py:59
  125.5 4.3 %reduce-scatter.2.cloned.1.call-done = f32[384,1280]{1,0:T(8,128)} async-done(((f32[768,1280]{1,0:T(8,128)}), f32[384,1280]{1,0:T(8,128)}) %reduce-scatter.2.cloned.1.call-update) | async-done | bytes 1966096 | tf_op jit(solution)/shard_map/reduce_scatter | solution.py:16
  129.9 1.9 reduce_max.9
  131.7 30.9 %pmax.7 = f32[384]{0:T(512)S(1)} all-reduce(f32[384]{0:T(512)S(1)} %reduce_max.9), channel_id=1, replica_groups=mesh['vocab'=16,'hid'=2] {'vocab'}, use_global_device_ids=true, to_apply=%region_3.0 | all-reduce | flops 384 | bytes 3072 | tf_op jit(solution)/shard_map/pmax | solution.py:22
  162.6 0.4 fusion.2
  163.1 1.3 copy.19
  164.4 2.3 copy.20
  166.7 0.6 convolution_convert_fusion
  167.3 0.6 fusion.4
  167.9 7.1 %fusion = f32[32,384,128]{2,0,1:T(8,128)} fusion(f32[16,384,128]{2,1,0:T(8,128)S(1)} %fusion.4, s32[16]{0:T(128)S(1)} %fusion.23), kind=kOutput, calls=%fused_computation | convolution fusion | flops 301990400 | bytes 9437248 | tf_op jit(solution)/shard_map/ed,erc->drc/dot_general | solution.py:48
  175.0 8.7 %copy.23 = f32[16,2,384,128]{3,1,2,0:T(2,128)} copy(f32[16,2,384,128]{3,1,0,2:T(2,128)} %bitcast.45) | data formatting | bytes 12582912 | tf_op jit(solution)/shard_map/reshape | solution.py:49
  183.7 0.0 all-to-all-done.1
  183.7 15.8 %all-to-all-start = ((f32[16,2,384,128]{3,1,2,0:T(2,128)}), f32[16,2,384,128]{3,1,2,0:T(2,128)}, u32[]{:S(2)}, u32[]{:S(2)}) async-start(f32[16,2,384,128]{3,1,2,0:T(2,128)} %copy.23), calls=%async_computation.1 | async-start | bytes 12582912 | tf_op jit(solution)/shard_map/all_to_all | solution.py:58
  199.5 0.5 broadcast.102
  200.0 0.7 reduce.3
  200.7 0.1 eq.104
  200.8 153.1 %psum.7 = f32[384]{0:T(512)S(1)} all-reduce(f32[384]{0:T(512)S(1)} %get-tuple-element.8), channel_id=1, replica_groups=mesh['vocab'=16,'hid'=2] {'vocab'}, use_global_device_ids=true, to_apply=%region_5.6 | all-reduce | flops 384 | bytes 3072 | tf_op jit(solution)/shard_map/psum | solution.py:24
  353.9 9.1 %copy.24 = f32[16,2,384,128]{3,1,0,2:T(2,128)} copy(f32[16,2,384,128]{3,1,2,0:T(2,128)} %all-to-all-done) | data formatting | bytes 12582912 | tf_op jit(solution)/shard_map/all_to_all | solution.py:58
  363.0 6.9 %multiply_bitcast_fusion = f32[384,12,128]{2,1,0:T(8,128)} fusion(f32[32,384,128]{2,0,1:T(8,128)} %bitcast.44, f32[32]{0:T(128)S(1)} %eq.104, f32[12]{0:T(128)S(1)} %iota_add_fusion), kind=kOutput, calls=%fused_computation.2 | convolution fusion | flops 227082624 | bytes 8650928 | tf_op jit(solution)/shard_map/sj,src->rjc/dot_general | solution.py:66
  369.9 3.3 copy.26
  373.1 1.9 bitcast_divide_fusion
  375.0 2.0 copy.27
  (14 shorter events, 0.1 us)
Async XLA Ops:
  6.5 160.8 %copy-start = (bf16[16,128,128]{2,1,0:T(8,128)(2,1)S(1)}, bf16[16,128,128]{2,1,0:T(8,128)(2,1)}, u32[]{:S(2)}) copy-start(bf16[16,128,128]{2,1,0:T(8,128)(2,1)} %param.7) | copy-start | bytes 1572868
  6.5 98.3 %all-gather.2.cloned.1.call-start = ((), (), s32[]{:S(2)}) async-start(), calls=%async_computation.3 | async-start | bytes 6684672 | tf_op jit(solution)/shard_map/all_gather | solution.py:14
  7.3 122.6 %reduce-scatter.2.cloned.1.call-start = ((), (), s32[]{:S(2)}) async-start(), calls=%async_computation.4 | async-start | bytes 5898240 | tf_op jit(solution)/shard_map/reduce_scatter | solution.py:16
  118.7 0.7 copy-start.3
  120.5 63.2 %all-to-all-start.1 = ((f32[16,1,2]{2,1,0:T(1,128)}), f32[16,1,2]{2,1,0:T(1,128)S(1)}, u32[]{:S(2)}, u32[]{:S(2)}) async-start(f32[16,1,2]{2,1,0:T(1,128)} %copy.25), calls=%async_computation.2 | async-start | bytes 16384 | tf_op jit(solution)/shard_map/all_to_all | solution.py:59
  129.9 32.7 %copy-start.2 = (f32[384,1280]{1,0:T(8,128)S(1)}, f32[384,1280]{1,0:T(8,128)}, u32[]{:S(2)}) copy-start(f32[384,1280]{1,0:T(8,128)} %reduce-scatter.2.cloned.1.call-done) | copy-start | bytes 5898244
  183.7 170.2 %all-to-all-start = ((f32[16,2,384,128]{3,1,2,0:T(2,128)}), f32[16,2,384,128]{3,1,2,0:T(2,128)}, u32[]{:S(2)}, u32[]{:S(2)}) async-start(f32[16,2,384,128]{3,1,2,0:T(2,128)} %copy.23), calls=%async_computation.1 | async-start | bytes 12582912 | tf_op jit(solution)/shard_map/all_to_all | solution.py:58
  373.1 3.8 %copy-start.1 = (bf16[16,128,128]{2,1,0:T(8,128)(2,1)S(1)}, bf16[16,128,128]{2,1,0:T(8,128)(2,1)}, u32[]{:S(2)}) copy-start(bf16[16,128,128]{2,1,0:T(8,128)(2,1)} %param.7) | copy-start | bytes 1572868
Sparse Core Ops, SparseCore 0:
  10.1 94.6 all-gather.1
  118.8 11.0 reduce-scatter.1
where the time goes:
time: 386 us; the launch traced here: 384 us
  blocking collectives  184 us (48%)
  waiting for transfers between devices  103 us (27%)
  matrix products  29.1 us (8%)
  local copies, waits for them, and re-layouts  28.6 us (7%)
  starting transfers between devices  20.8 us (5%)
  between operations  13.5 us (3%)
  other arithmetic  5.16 us (1%)
    psum x1, blocking collectives, per_device(): denominator = lax.psum(jnp.sum(exp_values, axis=1), 'vocab')  153 us
    all_gather x1, waiting for transfers between devices, per_device(): gathered = lax.all_gather(hidden_states, 'vocab', axis=0, tiled=True)  97.5 us
    pmax x1, blocking collectives, per_device(): row_top = lax.pmax(jnp.max(logits, axis=1), 'vocab')  30.9 us
    all_to_all x1, starting transfers between devices, per_device(): lax.all_to_all(outgoing, 'vocab', split_axis=0, concat_axis=0, tiled=True)  15.8 us
    dot_general x1, matrix products, per_device(): jnp.dot(gathered, head_weight, preferred_element_type=jnp.float32)  13.8 us
    all_to_all x1, local copies, waits for them, and re-layouts, per_device(): lax.all_to_all(outgoing, 'vocab', split_axis=0, concat_axis=0, tiled=True)  9.07 us
    reshape x1, local copies, waits for them, and re-layouts, per_device(): outgoing = outgoing.reshape(vocab_count, CAP, row_count, TILE)  8.69 us
  transfers between devices with their start and end apart: 4, of which 2 were waited for; matrix products, arithmetic and copies ran while one was open for 7% of the time, Pallas kernels for 0%

commit v1 on v0

v1 whole, which is shorter than its diff:
```python
import functools

import jax
import jax.numpy as jnp
from jax import lax
from jax.experimental import pallas as pl
from jax.experimental.pallas import tpu as pltpu
from jax.sharding import PartitionSpec as P

TILE = 128
STILES_DEV = 12
CAP = 2
VMEM = pl.BlockSpec(memory_space=pltpu.VMEM)
SMEM = pl.BlockSpec(memory_space=pltpu.SMEM)


def map_kernel(blocks, plan_ref, kept_ref, came_ref, focus_ref, out_ref, stat_ref, tiles_ref):
    rows = kept_ref.shape[0] // blocks
    turn = plan_ref[2, 0]
    for i in range(blocks):
        source = pl.ds(pl.multiple_of((turn ^ i) * rows, 8), rows)
        target = pl.ds(i * rows, rows)
        logits = kept_ref[source, :] + came_ref[source, :]
        top = jnp.max(logits, axis=1, keepdims=True)
        values = jnp.exp(logits - top)
        total = jnp.sum(values, axis=1, keepdims=True)
        lane = lax.broadcasted_iota(jnp.int32, (rows, TILE), 1)
        stat_ref[target, :] = jnp.where(lane == 0, top, total)
        weights = values.astype(jnp.bfloat16)
        for t in range(tiles_ref.shape[0]):
            tiles_ref[t, target, :] = weights[:, t * TILE : (t + 1) * TILE]

    @pl.loop(0, focus_ref.shape[0])
    def _(e):
        term = jnp.dot(
            tiles_ref[plan_ref[0, e]], focus_ref[e], preferred_element_type=jnp.float32
        )
        out_ref[plan_ref[1, e]] = term.astype(jnp.bfloat16)


def map_rows(plan, kept, came, focus_blocks, slots, blocks):
    rows, columns = kept.shape
    entries = focus_blocks.shape[0]
    return pl.pallas_call(
        functools.partial(map_kernel, blocks),
        out_shape=(
            jax.ShapeDtypeStruct((slots, rows, TILE), jnp.bfloat16),
            jax.ShapeDtypeStruct((rows, TILE), jnp.float32),
        ),
        in_specs=[SMEM, VMEM, VMEM, VMEM],
        out_specs=(VMEM, VMEM),
        scratch_shapes=[pltpu.VMEM((columns // TILE, rows, TILE), jnp.bfloat16)],
        compiler_params=pltpu.CompilerParams(vmem_limit_bytes=32 << 20),
        cost_estimate=pl.CostEstimate(
            flops=2 * entries * rows * TILE * TILE,
            bytes_accessed=8 * rows * columns + 2 * slots * rows * TILE,
            transcendentals=rows * columns,
        ),
    )(plan, kept, came, focus_blocks)


def sum_kernel(place, chunks, label_ref, factor_ref, *refs):
    out_ref = refs[chunks]
    rows = refs[0].shape[1]
    out_ref[...] = jnp.zeros_like(out_ref)
    for sender in range(refs[0].shape[0] // CAP):
        for c in range(chunks):
            target = pl.ds(place(sender, c) * rows, rows)
            factor = factor_ref[target, sender : sender + 1]
            for r in range(CAP):
                slot = sender * CAP + r
                label = label_ref[slot]

                @pl.when(label >= 0)
                def _(slot=slot, label=label, target=target, factor=factor, c=c):
                    columns = pl.ds(pl.multiple_of(label * TILE, TILE), TILE)
                    out_ref[target, columns] += refs[c][slot].astype(jnp.float32) * factor


def sum_slots(labels, factor, received, place):
    rows = factor.shape[0]
    slots = received[0].shape[0]
    return pl.pallas_call(
        functools.partial(sum_kernel, place, len(received)),
        out_shape=jax.ShapeDtypeStruct((rows, STILES_DEV * TILE), jnp.float32),
        in_specs=[SMEM] + [VMEM] * (1 + len(received)),
        out_specs=VMEM,
        compiler_params=pltpu.CompilerParams(vmem_limit_bytes=32 << 20),
        cost_estimate=pl.CostEstimate(
            flops=2 * slots * rows * TILE,
            bytes_accessed=2 * slots * rows * TILE + 4 * rows * STILES_DEV * TILE,
            transcendentals=0,
        ),
    )(labels, factor, *received)


def slot_plan(focus_tiles):
    owner = focus_tiles[..., 1] // STILES_DEV
    index = jnp.arange(focus_tiles.shape[-2], dtype=jnp.int32)
    same = (owner[..., :, None] == owner[..., None, :]) & (index[None, :] < index[:, None])
    rank = jnp.sum(same.astype(jnp.int32), axis=-1)
    return owner, focus_tiles[..., 1] % STILES_DEV, rank


def arriving_labels(all_tiles, senders, me):
    owner, tile, rank = slot_plan(all_tiles.reshape(senders, -1, 2))
    slot = jnp.arange(CAP, dtype=jnp.int32)
    hit = (owner[:, None, :] == me) & (rank[:, None, :] == slot[None, :, None])
    return (jnp.sum(jnp.where(hit, tile[:, None, :] + 1, 0), axis=-1) - 1).reshape(-1)


def per_device(hidden_states, head_weight, focus_tiles, focus_blocks):
    vocab, hid = lax.axis_size("vocab"), lax.axis_size("hid")
    me, core = lax.axis_index("vocab"), lax.axis_index("hid")
    tiles_here = head_weight.shape[1] // TILE
    slots = vocab * CAP
    staged = vocab == 16 and hid == 2

    def swap(x, k):
        return lax.ppermute(x, "vocab", [(i, i ^ k) for i in range(vocab)])

    def dot(x):
        return jnp.dot(x, head_weight, preferred_element_type=jnp.float32)

    owner, _, rank = slot_plan(focus_tiles)
    turn = jnp.broadcast_to(me & 3 if staged else 0, rank.shape)
    plan = jnp.stack([focus_tiles[:, 0] - me * tiles_here, owner * CAP + rank, turn])
    labels = arriving_labels(lax.all_gather(focus_tiles, "vocab"), vocab, me)

    def exchange(kept, came, blocks):
        out, stats = map_rows(plan, kept, came, focus_blocks, slots, blocks)
        rows = out.shape[1]
        out = out.reshape(vocab, CAP * rows, TILE)
        arrived = lax.all_to_all(out, "vocab", split_axis=0, concat_axis=0, tiled=True)
        stats = lax.all_gather(stats[:, :2].T, "vocab")
        return arrived.reshape(slots, rows, TILE), stats

    if staged:

        def spread(x, first):
            beside, above = swap(x, 1), swap(x, 2)
            far = swap(beside, 2) if first else swap(above, 1)
            return jnp.concatenate([x, beside, above, far])

        def chunk(near, away):
            mine = (me >> 3) == core
            other = dot(jnp.where(mine, away, near))
            came = lax.ppermute(other, "hid", [(0, 1), (1, 0)])
            return exchange(dot(jnp.where(mine, near, away)), came, 4)

        away = swap(hidden_states, 8)
        one, one_stats = chunk(spread(hidden_states, True), spread(away, False))
        two, two_stats = chunk(spread(swap(hidden_states, 4), True), spread(swap(away, 4), False))
        odd = (jnp.arange(vocab, dtype=jnp.int32) >> 2 & 1)[:, None, None] == 1
        stats = jnp.where(
            odd,
            jnp.concatenate([two_stats, one_stats], axis=-1),
            jnp.concatenate([one_stats, two_stats], axis=-1),
        )
        received = [one, two]

        def place(sender, c):
            return (sender >> 2 & 1) ^ c
    else:
        gathered = lax.all_gather(hidden_states, "vocab", axis=0, tiled=True)
        logits = lax.psum_scatter(dot(gathered), "hid", scatter_dimension=0, tiled=True)
        arrived, stats = exchange(logits, jnp.zeros_like(logits), 1)
        received = [arrived]

        def place(sender, c):
            return c

    top, total = stats[:, 0], stats[:, 1]
    scale = jnp.exp(top - jnp.max(top, axis=0))
    student_size = STILES_DEV * TILE * vocab
    factor = scale * (student_size / jnp.sum(scale * total, axis=0))
    return sum_slots(labels, factor.T, received, place)


def solution(mesh):
    return jax.shard_map(
        per_device,
        mesh=mesh,
        in_specs=(P("vocab", "hid"), P("hid", "vocab"), P("vocab", None), P("vocab", None, None)),
        out_specs=P("hid", "vocab"),
        check_vma=False,
    )
```

time: 386 us -> 250 us (0.65)
  the two profiles are of different devices: /device:TPU:10 before, /device:TPU:0 now
where the time goes in v1:
time: 250 us; the launch traced here: 248 us
  blocking collectives  141 us (56%)
  waiting for transfers between devices  34.6 us (14%)
  starting transfers between devices  31.5 us (13%)
  matrix products  18 us (7%)
  Pallas kernels  10.3 us (4%)
  local copies, waits for them, and re-layouts  9.58 us (4%)
    all_gather x2, blocking collectives, exchange(): stats = lax.all_gather(stats[:, :2].T, 'vocab')  92.7 us
    all_gather x1, blocking collectives, per_device(): labels = arriving_labels(lax.all_gather(focus_tiles, 'vocab'), vocab, me)  48.3 us
    ppermute x15, waiting for transfers between devices, swap(): return lax.ppermute(x, 'vocab', [(i, i ^ k) for i in range(vocab)])  34.6 us
    ppermute x15, starting transfers between devices, swap(): return lax.ppermute(x, 'vocab', [(i, i ^ k) for i in range(vocab)])  20.9 us
    dot_general x4, matrix products, dot(): return jnp.dot(x, head_weight, preferred_element_type=jnp.float32)  18 us
    all_to_all x2, starting transfers between devices, exchange(): lax.all_to_all(out, 'vocab', split_axis=0, concat_axis=0, tiled=True)  10.4 us
    pallas_call x2, Pallas kernels, map_rows(): pl.pallas_call(functools.partial(map_kernel, blocks), out_shape=(jax.Shap...  6.34 us
  transfers between devices with their start and end apart: 19, of which 5 were waited for; matrix products, arithmetic and copies ran while one was open for 11% of the time, Pallas kernels for 3%

profile of v1, /device:TPU:0, one launch (start us, length us, event | category | flops | bytes accessed | tf_op | source)
XLA Modules:
  0.0 247.8 jit_solution(10402921173393419306)
XLA Ops:
  0.0 4.0 %collective-permute-start.4 = (bf16[48,4096]{1,0:T(8,128)(2,1)}, bf16[48,4096]{1,0:T(8,128)(2,1)S(1)}, u32[]{:S(2)}, u32[]{:S(2)}) collective-permute-start(bf16[48,4096]{1,0:T(8,128)(2,1)} %param.4), channel_id=1, source_target_pairs={{0,16},{2,18},{4,20},{6,22},{8,24},{10,26},{12,28},{14,30},{16,0},... | collective-permute-start | bytes 1179656 | tf_op jit(solution)/shard_map/ppermute | solution.py:120
  4.0 1.6 collective-permute-start
  5.6 1.5 collective-permute-start.10
  7.1 1.5 collective-permute-start.11
  9.7 1.0 constant_dynamic-update-slice_fusion.11
  10.8 11.3 %collective-permute-done = bf16[48,4096]{1,0:T(8,128)(2,1)S(1)} collective-permute-done((bf16[48,4096]{1,0:T(8,128)(2,1)}, bf16[48,4096]{1,0:T(8,128)(2,1)S(1)}, u32[]{:S(2)}, u32[]{:S(2)}) %collective-permute-start) | collective-permute-done | bytes 393248 | tf_op jit(solution)/shard_map/ppermute | solution.py:120
  22.1 1.5 collective-permute-start.1
  23.6 1.5 collective-permute-start.2
  25.2 1.5 collective-permute-start.5
  28.0 6.4 %collective-permute-done.5 = bf16[48,4096]{1,0:T(8,128)(2,1)S(1)} collective-permute-done((bf16[48,4096]{1,0:T(8,128)(2,1)S(1)}, bf16[48,4096]{1,0:T(8,128)(2,1)S(1)}, u32[]{:S(2)}, u32[]{:S(2)}) %collective-permute-start.5) | collective-permute-done | bytes 393248 | tf_op jit(solution)/shard_map/ppermute | solution.py:120
  35.7 6.8 %collective-permute-done.13 = bf16[48,4096]{1,0:T(8,128)(2,1)S(1)} collective-permute-done((bf16[48,4096]{1,0:T(8,128)(2,1)S(1)}, bf16[48,4096]{1,0:T(8,128)(2,1)S(1)}, u32[]{:S(2)}, u32[]{:S(2)}) %collective-permute-start.13) | collective-permute-done | bytes 393248 | tf_op jit(solution)/shard_map/ppermute | solution.py:120
  42.6 1.6 collective-permute-start.7
  44.2 1.5 collective-permute-start.3
  46.4 6.1 %collective-permute-done.12 = bf16[48,4096]{1,0:T(8,128)(2,1)S(1)} collective-permute-done((bf16[48,4096]{1,0:T(8,128)(2,1)S(1)}, bf16[48,4096]{1,0:T(8,128)(2,1)S(1)}, u32[]{:S(2)}, u32[]{:S(2)}) %collective-permute-start.12) | collective-permute-done | bytes 393248 | tf_op jit(solution)/shard_map/ppermute | solution.py:120
  52.6 3.9 %collective-permute-done.15 = bf16[48,4096]{1,0:T(8,128)(2,1)S(1)} collective-permute-done((bf16[48,4096]{1,0:T(8,128)(2,1)S(1)}, bf16[48,4096]{1,0:T(8,128)(2,1)S(1)}, u32[]{:S(2)}, u32[]{:S(2)}) %collective-permute-start.15) | collective-permute-done | bytes 393248 | tf_op jit(solution)/shard_map/ppermute | solution.py:120
  56.5 6.4 %fusion = f32[192,1280]{1,0:T(8,128)S(1)} fusion(bf16[4096,1280]{1,0:T(8,128)(2,1)} %param.5, bf16[192,4096]{1,0:T(8,128)(2,1)S(1)} %constant_dynamic-update-slice_fusion.12, bf16[192,4096]{1,0:T(8,128)(2,1)S(1)} %constant_dynamic-update-slice_fusion.8, pred[]{:T(512)S(6)} %eq.82), kind=kOutput, calls=%fused_computation | convolution fusion | flops 2014052352 | bytes 14614529 | tf_op jit(solution)/shard_map/dot_general | solution.py:123
  63.0 1.6 collective-permute-start.8
  64.7 2.4 fusion.2.kept_ref
  67.1 3.2 %shard_map.47 = (bf16[32,192,128]{2,1,0:T(8,128)(2,1)S(1)}, f32[192,128]{1,0:T(8,128)S(1)}) custom-call(s32[3,16]{1,0:T(4,128)S(1)} %add_add_fusion.plan_ref, f32[192,1280]{1,0:T(8,128)S(1)} %fusion.2.kept_ref, f32[192,1280]{1,0:T(8,128)S(1)} %collective-permute-done.16.came_ref, bf16[16,128,128]{2,1,0:T(8,128)(2,1)S(1)} %copy-done), custom_call_target="tpu_custom_call" | custom-call | flops 100663296 | bytes 3538944 | tf_op jit(solution)/shard_map/pallas_call | solution.py:44
  70.3 1.2 copy-done.2
  71.5 4.7 %all-to-all-start = ((bf16[16,384,128]{2,1,0:T(8,128)(2,1)}), bf16[16,384,128]{2,1,0:T(8,128)(2,1)S(1)}, u32[]{:S(2)}, u32[]{:S(2)}) async-start(bf16[16,384,128]{2,1,0:T(8,128)(2,1)} %bitcast.62), calls=%async_computation | async-start | bytes 3145728 | tf_op jit(solution)/shard_map/all_to_all | solution.py:134
  77.0 1.9 constant_dynamic-update-slice_fusion
  78.9 1.8 constant_dynamic-update-slice_fusion.4
  80.7 6.9 %fusion.4 = f32[192,1280]{1,0:T(8,128)S(1)} fusion(bf16[4096,1280]{1,0:T(8,128)(2,1)} %param.5, bf16[192,4096]{1,0:T(8,128)(2,1)} %constant_dynamic-update-slice_fusion.4, bf16[192,4096]{1,0:T(8,128)(2,1)} %constant_dynamic-update-slice_fusion, pred[]{:T(512)S(6)} %eq.82), kind=kOutput, calls=%fused_computation.4 | convolution fusion | flops 2014052352 | bytes 14614529 | tf_op jit(solution)/shard_map/dot_general | solution.py:123
  87.6 48.3 %all-gather.3 = s32[16,16,2]{1,2,0:T(2,128)S(1)} all-gather(s32[1,16,2]{1,2,0:T(2,128)S(1)} %bitcast.70), channel_id=2, replica_groups=mesh['vocab'=16,'hid'=2] {'vocab'}, dimensions={0}, use_global_device_ids=true | all-gather | bytes 2176 | tf_op jit(solution)/shard_map/all_gather | solution.py:128
  136.0 2.4 fusion.6.kept_ref
  138.4 3.2 %shard_map.46 = (bf16[32,192,128]{2,1,0:T(8,128)(2,1)S(1)}, f32[192,128]{1,0:T(8,128)S(1)}) custom-call(s32[3,16]{1,0:T(4,128)S(1)} %add_add_fusion.plan_ref, f32[192,1280]{1,0:T(8,128)S(1)} %fusion.6.kept_ref, f32[192,1280]{1,0:T(8,128)S(1)} %collective-permute-done.9.came_ref, bf16[16,128,128]{2,1,0:T(8,128)(2,1)S(1)} %copy-done), custom_call_target="tpu_custom_call" | custom-call | flops 100663296 | bytes 3538944 | tf_op jit(solution)/shard_map/pallas_call | solution.py:44
  141.5 1.1 copy-done.1
  142.7 5.7 %all-to-all-start.1 = ((bf16[16,384,128]{2,1,0:T(8,128)(2,1)}), bf16[16,384,128]{2,1,0:T(8,128)(2,1)S(1)}, u32[]{:S(2)}, u32[]{:S(2)}) async-start(bf16[16,384,128]{2,1,0:T(8,128)(2,1)} %bitcast.61), calls=%async_computation.1 | async-start | bytes 3145728 | tf_op jit(solution)/shard_map/all_to_all | solution.py:134
  149.4 52.5 %all-gather.5 = f32[16,2,192]{2,1,0:T(2,128)S(1)} all-gather(f32[1,2,192]{2,1,0:T(2,128)S(1)} %bitcast.68), channel_id=4, replica_groups=mesh['vocab'=16,'hid'=2] {'vocab'}, dimensions={0}, use_global_device_ids=true | all-gather | bytes 26112 | tf_op jit(solution)/shard_map/all_gather | solution.py:135
  202.1 40.2 %all-gather.4 = f32[16,2,192]{2,1,0:T(2,128)} all-gather(f32[1,2,192]{2,1,0:T(2,128)S(1)} %bitcast.69), channel_id=3, replica_groups=mesh['vocab'=16,'hid'=2] {'vocab'}, dimensions={0}, use_global_device_ids=true | all-gather | bytes 26112 | tf_op jit(solution)/shard_map/all_gather | solution.py:135
  243.8 4.0 %shard_map.48 = f32[384,1536]{1,0:T(8,128)} custom-call(s32[32]{0:T(128)S(1)} %sub.49.label_ref, f32[384,16]{1,0:T(8,128)S(1)} %multiply_bitcast_fusion.factor_ref, bf16[32,192,128]{2,1,0:T(8,128)(2,1)S(1)} %bitcast.59, bf16[32,192,128]{2,1,0:T(8,128)(2,1)S(1)} %bitcast.60), custom_call_target="tpu_custom_call" | custom-call | flops 3145728 | bytes 5505024 | tf_op jit(solution)/shard_map/pallas_call | solution.py:83
  (90 shorter events, 8.2 us)
Async XLA Ops:
  0.0 25.2 %collective-permute-start.4 = (bf16[48,4096]{1,0:T(8,128)(2,1)}, bf16[48,4096]{1,0:T(8,128)(2,1)S(1)}, u32[]{:S(2)}, u32[]{:S(2)}) collective-permute-start(bf16[48,4096]{1,0:T(8,128)(2,1)} %param.4), channel_id=1, source_target_pairs={{0,16},{2,18},{4,20},{6,22},{8,24},{10,26},{12,28},{14,30},{16,0},... | collective-permute-start | bytes 1179656 | tf_op jit(solution)/shard_map/ppermute | solution.py:120
  4.0 18.0 %collective-permute-start = (bf16[48,4096]{1,0:T(8,128)(2,1)}, bf16[48,4096]{1,0:T(8,128)(2,1)S(1)}, u32[]{:S(2)}, u32[]{:S(2)}) collective-permute-start(bf16[48,4096]{1,0:T(8,128)(2,1)} %param.4), channel_id=1, source_target_pairs={{0,8},{2,10},{4,12},{6,14},{8,0},{10,2},{12,4},{14,6},{16,24},{18,... | collective-permute-start | bytes 1179656 | tf_op jit(solution)/shard_map/ppermute | solution.py:120
  5.6 21.1 %collective-permute-start.10 = (bf16[48,4096]{1,0:T(8,128)(2,1)}, bf16[48,4096]{1,0:T(8,128)(2,1)S(1)}, u32[]{:S(2)}, u32[]{:S(2)}) collective-permute-start(bf16[48,4096]{1,0:T(8,128)(2,1)} %param.4), channel_id=1, source_target_pairs={{0,2},{2,0},{4,6},{6,4},{8,10},{10,8},{12,14},{14,12},{16,18},{18,... | collective-permute-start | bytes 1179656 | tf_op jit(solution)/shard_map/ppermute | solution.py:120
  7.1 20.3 %collective-permute-start.11 = (bf16[48,4096]{1,0:T(8,128)(2,1)}, bf16[48,4096]{1,0:T(8,128)(2,1)S(1)}, u32[]{:S(2)}, u32[]{:S(2)}) collective-permute-start(bf16[48,4096]{1,0:T(8,128)(2,1)} %param.4), channel_id=1, source_target_pairs={{0,4},{2,6},{4,0},{6,2},{8,12},{10,14},{12,8},{14,10},{16,20},{18,... | collective-permute-start | bytes 1179656 | tf_op jit(solution)/shard_map/ppermute | solution.py:120
  22.1 12.8 %collective-permute-start.1 = (bf16[48,4096]{1,0:T(8,128)(2,1)S(1)}, bf16[48,4096]{1,0:T(8,128)(2,1)S(1)}, u32[]{:S(2)}, u32[]{:S(2)}) collective-permute-start(bf16[48,4096]{1,0:T(8,128)(2,1)S(1)} %collective-permute-done), channel_id=1, source_target_pairs={{0,2},{2,0},{4,6},{6,4},{8,10},{10,8},{12,14},{14,12},{16,18},{18,... | collective-permute-start | bytes 1179656 | tf_op jit(solution)/shard_map/ppermute | solution.py:120
  23.6 22.0 %collective-permute-start.2 = (bf16[48,4096]{1,0:T(8,128)(2,1)S(1)}, bf16[48,4096]{1,0:T(8,128)(2,1)S(1)}, u32[]{:S(2)}, u32[]{:S(2)}) collective-permute-start(bf16[48,4096]{1,0:T(8,128)(2,1)S(1)} %collective-permute-done), channel_id=1, source_target_pairs={{0,4},{2,6},{4,0},{6,2},{8,12},{10,14},{12,8},{14,10},{16,20},{18,... | collective-permute-start | bytes 1179656 | tf_op jit(solution)/shard_map/ppermute | solution.py:120
  25.2 9.2 %collective-permute-start.5 = (bf16[48,4096]{1,0:T(8,128)(2,1)S(1)}, bf16[48,4096]{1,0:T(8,128)(2,1)S(1)}, u32[]{:S(2)}, u32[]{:S(2)}) collective-permute-start(bf16[48,4096]{1,0:T(8,128)(2,1)S(1)} %collective-permute-done.4), channel_id=1, source_target_pairs={{0,8},{2,10},{4,12},{6,14},{8,0},{10,2},{12,4},{14,6},{16,24},{18,... | collective-permute-start | bytes 1179656 | tf_op jit(solution)/shard_map/ppermute | solution.py:120
  26.7 15.8 %collective-permute-start.13 = (bf16[48,4096]{1,0:T(8,128)(2,1)S(1)}, bf16[48,4096]{1,0:T(8,128)(2,1)S(1)}, u32[]{:S(2)}, u32[]{:S(2)}) collective-permute-start(bf16[48,4096]{1,0:T(8,128)(2,1)S(1)} %collective-permute-done.4), channel_id=1, source_target_pairs={{0,2},{2,0},{4,6},{6,4},{8,10},{10,8},{12,14},{14,12},{16,18},{18,... | collective-permute-start | bytes 1179656 | tf_op jit(solution)/shard_map/ppermute | solution.py:120
  27.4 16.8 %collective-permute-start.14 = (bf16[48,4096]{1,0:T(8,128)(2,1)S(1)}, bf16[48,4096]{1,0:T(8,128)(2,1)S(1)}, u32[]{:S(2)}, u32[]{:S(2)}) collective-permute-start(bf16[48,4096]{1,0:T(8,128)(2,1)S(1)} %collective-permute-done.4), channel_id=1, source_target_pairs={{0,4},{2,6},{4,0},{6,2},{8,12},{10,14},{12,8},{14,10},{16,20},{18,... | collective-permute-start | bytes 1179656 | tf_op jit(solution)/shard_map/ppermute | solution.py:120
  34.4 18.2 %collective-permute-start.12 = (bf16[48,4096]{1,0:T(8,128)(2,1)S(1)}, bf16[48,4096]{1,0:T(8,128)(2,1)S(1)}, u32[]{:S(2)}, u32[]{:S(2)}) collective-permute-start(bf16[48,4096]{1,0:T(8,128)(2,1)S(1)} %collective-permute-done.10), channel_id=1, source_target_pairs={{0,4},{2,6},{4,0},{6,2},{8,12},{10,14},{12,8},{14,10},{16,20},{18,... | collective-permute-start | bytes 1179656 | tf_op jit(solution)/shard_map/ppermute | solution.py:120
  34.9 29.7 %collective-permute-start.6 = (bf16[48,4096]{1,0:T(8,128)(2,1)S(1)}, bf16[48,4096]{1,0:T(8,128)(2,1)S(1)}, u32[]{:S(2)}, u32[]{:S(2)}) collective-permute-start(bf16[48,4096]{1,0:T(8,128)(2,1)S(1)} %collective-permute-done.5), channel_id=1, source_target_pairs={{0,2},{2,0},{4,6},{6,4},{8,10},{10,8},{12,14},{14,12},{16,18},{18,... | collective-permute-start | bytes 1179656 | tf_op jit(solution)/shard_map/ppermute | solution.py:120
  42.6 20.4 %collective-permute-start.7 = (bf16[48,4096]{1,0:T(8,128)(2,1)S(1)}, bf16[48,4096]{1,0:T(8,128)(2,1)S(1)}, u32[]{:S(2)}, u32[]{:S(2)}) collective-permute-start(bf16[48,4096]{1,0:T(8,128)(2,1)S(1)} %collective-permute-done.5), channel_id=1, source_target_pairs={{0,4},{2,6},{4,0},{6,2},{8,12},{10,14},{12,8},{14,10},{16,20},{18,... | collective-permute-start | bytes 1179656 | tf_op jit(solution)/shard_map/ppermute | solution.py:120
  44.2 32.8 %collective-permute-start.3 = (bf16[48,4096]{1,0:T(8,128)(2,1)S(1)}, bf16[48,4096]{1,0:T(8,128)(2,1)}, u32[]{:S(2)}, u32[]{:S(2)}) collective-permute-start(bf16[48,4096]{1,0:T(8,128)(2,1)S(1)} %collective-permute-done.1), channel_id=1, source_target_pairs={{0,4},{2,6},{4,0},{6,2},{8,12},{10,14},{12,8},{14,10},{16,20},{18,... | collective-permute-start | bytes 1179656 | tf_op jit(solution)/shard_map/ppermute | solution.py:120
  45.7 10.8 %collective-permute-start.15 = (bf16[48,4096]{1,0:T(8,128)(2,1)S(1)}, bf16[48,4096]{1,0:T(8,128)(2,1)S(1)}, u32[]{:S(2)}, u32[]{:S(2)}) collective-permute-start(bf16[48,4096]{1,0:T(8,128)(2,1)S(1)} %collective-permute-done.14), channel_id=1, source_target_pairs={{0,2},{2,0},{4,6},{6,4},{8,10},{10,8},{12,14},{14,12},{16,18},{18,... | collective-permute-start | bytes 1179656 | tf_op jit(solution)/shard_map/ppermute | solution.py:120
  46.4 10.1 %copy-start.5 = (bf16[192,4096]{1,0:T(8,128)(2,1)}, bf16[192,4096]{1,0:T(8,128)(2,1)S(1)}, u32[]{:S(2)}) copy-start(bf16[192,4096]{1,0:T(8,128)(2,1)S(1)} %constant_dynamic-update-slice_fusion.1) | copy-start | bytes 4718596
  56.5 8.1 %slice-start = ((s8[10485760]{0:T(1024)(128)(4,1)}), s8[4194304]{0:T(1024)(128)(4,1)S(1)}, s32[]{:S(2)}) async-start(s8[10485760]{0:T(1024)(128)(4,1)} %bitcast.71), calls=%async_computation.2 | async-start | bytes 8388608
  56.5 8.1 %slice-start.1 = ((s8[10485760]{0:T(1024)(128)(4,1)}), s8[4194304]{0:T(1024)(128)(4,1)S(1)}, s32[]{:S(2)}) async-start(s8[10485760]{0:T(1024)(128)(4,1)} %bitcast.71), calls=%async_computation.3 | async-start | bytes 8388608
  56.5 8.1 %slice-start.2 = ((s8[10485760]{0:T(1024)(128)(4,1)}), s8[2097152]{0:T(1024)(128)(4,1)S(1)}, s32[]{:S(2)}) async-start(s8[10485760]{0:T(1024)(128)(4,1)} %bitcast.71), calls=%async_computation.4 | async-start | bytes 4194304
  62.9 4.1 %collective-permute-start.16 = (f32[192,1280]{1,0:T(8,128)S(1)}, f32[192,1280]{1,0:T(8,128)S(1)}, u32[]{:S(2)}, u32[]{:S(2)}) collective-permute-start(f32[192,1280]{1,0:T(8,128)S(1)} %fusion), channel_id=1, source_target_pairs={{0,1},{1,0},{2,3},{3,2},{4,5},{5,4},{6,7},{7,6},{8,9},{9,8},{10,11... | collective-permute-start | bytes 2949128 | tf_op jit(solution)/shard_map/ppermute | solution.py:148
  63.0 15.9 %collective-permute-start.8 = (bf16[48,4096]{1,0:T(8,128)(2,1)S(1)}, bf16[48,4096]{1,0:T(8,128)(2,1)}, u32[]{:S(2)}, u32[]{:S(2)}) collective-permute-start(bf16[48,4096]{1,0:T(8,128)(2,1)S(1)} %collective-permute-done.7), channel_id=1, source_target_pairs={{0,2},{2,0},{4,6},{6,4},{8,10},{10,8},{12,14},{14,12},{16,18},{18,... | collective-permute-start | bytes 1179656 | tf_op jit(solution)/shard_map/ppermute | solution.py:120
  64.6 2.4 copy-start.3
  64.7 2.4 copy-start
  70.3 1.2 copy-start.2
  71.5 71.2 %all-to-all-start = ((bf16[16,384,128]{2,1,0:T(8,128)(2,1)}), bf16[16,384,128]{2,1,0:T(8,128)(2,1)S(1)}, u32[]{:S(2)}, u32[]{:S(2)}) async-start(bf16[16,384,128]{2,1,0:T(8,128)(2,1)} %bitcast.62), calls=%async_computation | async-start | bytes 3145728 | tf_op jit(solution)/shard_map/all_to_all | solution.py:134
  77.0 59.0 %slice-start.3 = ((s8[10485760]{0:T(1024)(128)(4,1)}), s8[4194304]{0:T(1024)(128)(4,1)S(1)}, s32[]{:S(2)}) async-start(s8[10485760]{0:T(1024)(128)(4,1)} %bitcast.73), calls=%async_computation.5 | async-start | bytes 8388608
  80.6 7.0 %copy-start.7 = (s32[16,2]{0,1:T(2,128)S(1)}, s32[16,2]{0,1:T(2,128)}, u32[]{:S(2)}) copy-start(s32[16,2]{0,1:T(2,128)} %param.6) | copy-start | bytes 388
  80.7 55.3 %copy-start.4 = (bf16[192,4096]{1,0:T(8,128)(2,1)S(1)}, bf16[192,4096]{1,0:T(8,128)(2,1)}, u32[]{:S(2)}) copy-start(bf16[192,4096]{1,0:T(8,128)(2,1)} %constant_dynamic-update-slice_fusion.4) | copy-start | bytes 4718596
  80.7 55.3 %copy-start.6 = (bf16[192,4096]{1,0:T(8,128)(2,1)S(1)}, bf16[192,4096]{1,0:T(8,128)(2,1)}, u32[]{:S(2)}) copy-start(bf16[192,4096]{1,0:T(8,128)(2,1)} %constant_dynamic-update-slice_fusion) | copy-start | bytes 4718596
  80.7 55.3 %slice-start.4 = ((s8[10485760]{0:T(1024)(128)(4,1)}), s8[4194304]{0:T(1024)(128)(4,1)S(1)}, s32[]{:S(2)}) async-start(s8[10485760]{0:T(1024)(128)(4,1)} %bitcast.73), calls=%async_computation.6 | async-start | bytes 8388608
  80.7 55.3 %slice-start.5 = ((s8[10485760]{0:T(1024)(128)(4,1)}), s8[2097152]{0:T(1024)(128)(4,1)S(1)}, s32[]{:S(2)}) async-start(s8[10485760]{0:T(1024)(128)(4,1)} %bitcast.73), calls=%async_computation.7 | async-start | bytes 4194304
  87.6 50.8 %collective-permute-start.9 = (f32[192,1280]{1,0:T(8,128)S(1)}, f32[192,1280]{1,0:T(8,128)S(1)}, u32[]{:S(2)}, u32[]{:S(2)}) collective-permute-start(f32[192,1280]{1,0:T(8,128)S(1)} %fusion.4), channel_id=1, source_target_pairs={{0,1},{1,0},{2,3},{3,2},{4,5},{5,4},{6,7},{7,6},{8,9},{9,8},{10,11... | collective-permute-start | bytes 2949128 | tf_op jit(solution)/shard_map/ppermute | solution.py:148
  142.7 101.1 %all-to-all-start.1 = ((bf16[16,384,128]{2,1,0:T(8,128)(2,1)}), bf16[16,384,128]{2,1,0:T(8,128)(2,1)S(1)}, u32[]{:S(2)}, u32[]{:S(2)}) async-start(bf16[16,384,128]{2,1,0:T(8,128)(2,1)} %bitcast.61), calls=%async_computation.1 | async-start | bytes 3145728 | tf_op jit(solution)/shard_map/all_to_all | solution.py:134
  (1 other events, 1.1 us)

commit v2 on v0

v2 whole, which is shorter than its diff:
```python
import functools

import jax
import jax.numpy as jnp
from jax import lax
from jax.experimental import pallas as pl
from jax.experimental.pallas import tpu as pltpu
from jax.sharding import PartitionSpec as P

TILE = 128
STILES_DEV = 12
CAP = 2
STATS = 16
LABEL_ROW = 6
VMEM = pl.BlockSpec(memory_space=pltpu.VMEM)
SMEM = pl.BlockSpec(memory_space=pltpu.SMEM)
ANY = pl.BlockSpec(memory_space=pl.ANY)


def kernel_params(megabytes):
    return pltpu.CompilerParams(vmem_limit_bytes=megabytes << 20)


def stack_kernel(places, *refs):
    out_ref = refs[-1]
    for ref, (row, column) in zip(refs, places):
        out_ref[row : row + ref.shape[0], column : column + ref.shape[1]] = ref[...]


def stack_rows(blocks, earlier=()):
    rows, columns = blocks[0].shape
    places = [(i * rows, 0) for i in range(4)] + [(3 * rows, columns // 2)] * (len(blocks) - 4)
    return pl.pallas_call(
        functools.partial(stack_kernel, places),
        out_shape=jax.ShapeDtypeStruct((4 * rows, columns), blocks[0].dtype),
        in_specs=[VMEM] * len(blocks) + [ANY] * len(earlier),
        out_specs=VMEM,
        compiler_params=kernel_params(16),
        cost_estimate=pl.CostEstimate(
            flops=0, bytes_accessed=16 * rows * columns, transcendentals=0
        ),
    )(*blocks, *earlier)


def softmax_kernel(blocks, choices, where_ref, *refs):
    out_ref, stats_ref = refs[-2:]
    for choice in range(choices):

        @pl.when(where_ref[0] == choice)
        def _(choice=choice):
            kept_ref, came_ref = refs[2 * choice : 2 * choice + 2]
            softmax_block(blocks, where_ref[1], kept_ref, came_ref, out_ref, stats_ref)


def softmax_block(blocks, turn, kept_ref, came_ref, out_ref, stats_ref):
    all_rows = kept_ref.shape[0]
    rows = all_rows // blocks
    lane = lax.broadcasted_iota(jnp.int32, (rows, TILE), 1)
    stats_ref[...] = jnp.zeros_like(stats_ref)
    for i in range(blocks):
        source = pl.ds(pl.multiple_of((turn ^ i) * rows, 8), rows)
        logits = kept_ref[source, :] + came_ref[source, :]
        top = jnp.max(logits, axis=1, keepdims=True)
        values = jnp.exp(logits - top)
        total = jnp.sum(values, axis=1, keepdims=True)
        rest = jnp.where(lane < 3, top, total)
        high = rest.astype(jnp.bfloat16).astype(jnp.float32)
        rest = rest - high
        middle = rest.astype(jnp.bfloat16).astype(jnp.float32)
        place = lane % 3
        pieces = jnp.where(place == 0, high, jnp.where(place == 1, middle, rest - middle))
        stats_ref[pl.ds(i * rows, rows), :] = jnp.where(lane < 6, pieces, 0.0)
        weights = values.astype(jnp.bfloat16)
        for t in range(kept_ref.shape[1] // TILE):
            out_ref[pl.ds(t * all_rows + i * rows, rows), :] = weights[:, t * TILE : (t + 1) * TILE]
    for half in range(2):
        pieces = stats_ref[half * TILE : (half + 1) * TILE, :].T[:8]
        stats_ref[half * 8 : (half + 1) * 8, :] = pieces
    out_ref[out_ref.shape[0] - STATS :, :] = stats_ref[:STATS, :].astype(jnp.bfloat16)


def softmax_tiles(where, choices, blocks, earlier=()):
    rows, columns = choices[0][0].shape
    logits = [x for choice in choices for x in choice]
    return pl.pallas_call(
        functools.partial(softmax_kernel, blocks, len(choices)),
        out_shape=jax.ShapeDtypeStruct((columns // TILE * rows + STATS, TILE), jnp.bfloat16),
        in_specs=[SMEM] + [VMEM] * len(logits) + [ANY] * len(earlier),
        out_specs=VMEM,
        scratch_shapes=[pltpu.VMEM((2 * TILE, TILE), jnp.float32)],
        compiler_params=kernel_params(32),
        cost_estimate=pl.CostEstimate(
            flops=4 * rows * columns, bytes_accessed=10 * rows * columns, transcendentals=rows * columns
        ),
    )(where, *logits, *earlier)


def focus_kernel(rows, me_ref, pair_ref, tiles_ref, focus_ref, out_ref, seen_ref):
    owners, entries = out_ref.shape[0], focus_ref.shape[0]
    first = me_ref[0] * ((tiles_ref.shape[0] - STATS) // rows)
    stats = tiles_ref[tiles_ref.shape[0] - STATS :, :]
    bottom = pl.ds(CAP * rows, STATS)
    for owner in range(owners):
        out_ref[owner, bottom, :] = stats
        seen_ref[owner] = 0
    row = lax.broadcasted_iota(jnp.int32, (STATS, TILE), 0)
    lane = lax.broadcasted_iota(jnp.int32, (STATS, TILE), 1)
    scale = (1 << 19) // STILES_DEV + 1

    @pl.loop(0, entries, unroll=min(entries, 16))
    def _(e):
        student = pair_ref[2 * e + 1]
        owner = student * scale >> 19
        rank = seen_ref[owner]
        seen_ref[owner] = rank + 1
        label = (student - owner * STILES_DEV + 1).astype(jnp.float32)
        mark = jnp.where((row == LABEL_ROW) & (lane == rank), label, 0.0).astype(jnp.bfloat16)
        out_ref[owner, bottom, :] += mark
        source = pl.ds(pl.multiple_of((pair_ref[2 * e] - first) * rows, 16), rows)
        term = jnp.dot(tiles_ref[source, :], focus_ref[e], preferred_element_type=jnp.float32)
        target = pl.ds(pl.multiple_of(rank * rows, 16), rows)
        out_ref[owner, target, :] = term.astype(jnp.bfloat16)


def focus_products(me, pairs, tiles, focus_blocks, rows, owners):
    entries = focus_blocks.shape[0]
    size = CAP * rows + STATS
    return pl.pallas_call(
        functools.partial(focus_kernel, rows),
        out_shape=jax.ShapeDtypeStruct((owners, size, TILE), jnp.bfloat16),
        in_specs=[SMEM, SMEM, VMEM, VMEM],
        out_specs=VMEM,
        scratch_shapes=[pltpu.SMEM((owners,), jnp.int32)],
        compiler_params=kernel_params(32),
        cost_estimate=pl.CostEstimate(
            flops=2 * entries * rows * TILE * TILE,
            bytes_accessed=4 * owners * size * TILE,
            transcendentals=0,
        ),
    )(me, pairs, tiles, focus_blocks)


def sum_kernel(senders, place, *refs):
    out_ref, level_ref, factor_ref, label_ref, sem = refs[-5:]
    chunks = len(refs) - 5
    rows = (refs[0].shape[1] - STATS) // CAP
    for s in range(senders):
        marks = refs[0][s, CAP * rows :, :].astype(jnp.float32)
        level_ref[2, s : s + 1, :TILE] = marks[LABEL_ROW : LABEL_ROW + 1]
    to_scalars = pltpu.make_async_copy(level_ref.at[2, :, :TILE], label_ref, sem)
    to_scalars.start()
    out_ref[...] = jnp.zeros_like(out_ref)
    for group in range(chunks):
        for s in range(senders):
            stats = refs[place(s, group)][s, CAP * rows :, :].astype(jnp.float32)
            for half in range(2):
                columns = pl.ds(half * TILE, TILE)
                for kind in range(2):
                    i = 8 * half + 3 * kind
                    value = stats[i : i + 1] + stats[i + 1 : i + 2] + stats[i + 2 : i + 3]
                    level_ref[kind, s : s + 1, columns] = value
        top, total = level_ref[0, :senders, :], level_ref[1, :senders, :]
        scale = jnp.exp(top - jnp.max(top, axis=0, keepdims=True))
        total = jnp.sum(scale * total, axis=0, keepdims=True)
        level_ref[0, :senders, :] = scale * (STILES_DEV * TILE * senders / total)
        factor_ref[...] = level_ref[0].T
        target = pl.ds(group * rows, rows)
        if group == 0:
            to_scalars.wait()
        for s in range(senders):
            for r in range(CAP):
                label = label_ref[s, r].astype(jnp.int32) - 1

                @pl.when(label >= 0)
                def _(s=s, r=r, label=label, target=target, group=group):
                    factor = factor_ref[:rows, s : s + 1]
                    columns = pl.ds(pl.multiple_of(label * TILE, TILE), TILE)
                    tile = refs[place(s, group)][s, r * rows : (r + 1) * rows, :]
                    out_ref[target, columns] += tile.astype(jnp.float32) * factor


def sum_slots(received, place):
    senders, size, _ = received[0].shape
    rows, chunks = (size - STATS) // CAP, len(received)
    return pl.pallas_call(
        functools.partial(sum_kernel, senders, place),
        out_shape=jax.ShapeDtypeStruct((rows * chunks, STILES_DEV * TILE), jnp.float32),
        in_specs=[VMEM] * chunks,
        out_specs=VMEM,
        scratch_shapes=[
            pltpu.VMEM((3, TILE, 2 * TILE), jnp.float32),
            pltpu.VMEM((2 * TILE, TILE), jnp.float32),
            pltpu.SMEM((TILE, TILE), jnp.float32),
            pltpu.SemaphoreType.DMA,
        ],
        compiler_params=kernel_params(40),
        cost_estimate=pl.CostEstimate(
            flops=2 * senders * chunks * CAP * rows * TILE,
            bytes_accessed=4 * rows * chunks * STILES_DEV * TILE,
            transcendentals=0,
        ),
    )(*received)


def hold_kernel(x_ref, earlier_ref, out_ref):
    out_ref[...] = x_ref[...]


def hold(x, earlier):
    return pl.pallas_call(
        hold_kernel,
        out_shape=jax.ShapeDtypeStruct(x.shape, x.dtype),
        in_specs=[VMEM, ANY],
        out_specs=VMEM,
        compiler_params=kernel_params(16),
    )(x, earlier)


def halves_kernel(left_ref, right_ref, *refs):
    left_out, right_out = refs[-2:]
    half = left_out.shape[1]
    left_out[...] = left_ref[:, :half]
    right_out[...] = right_ref[:, half:]


def halves(left, right, earlier):
    rows, columns = left.shape
    return pl.pallas_call(
        halves_kernel,
        out_shape=[jax.ShapeDtypeStruct((rows, columns // 2), left.dtype)] * 2,
        in_specs=[VMEM] * 2 + [ANY] * len(earlier),
        out_specs=[VMEM] * 2,
        compiler_params=kernel_params(16),
    )(left, right, *earlier)


def per_device(hidden_states, head_weight, focus_tiles, focus_blocks):
    vocab, hid = lax.axis_size("vocab"), lax.axis_size("hid")
    me, core = lax.axis_index("vocab"), lax.axis_index("hid")
    pairs = focus_tiles.reshape(-1)

    def swap(x, k):
        return lax.ppermute(x, "vocab", [(i, i ^ k) for i in range(vocab)])

    def dot(x):
        return jnp.dot(x, head_weight, preferred_element_type=jnp.float32)

    def exchange(weights, rows):
        sent = focus_products(me[None], pairs, weights, focus_blocks, rows, vocab)
        return lax.all_to_all(sent, "vocab", split_axis=0, concat_axis=0, tiled=True)

    if vocab == 16 and hid == 2:
        zero = hidden_states
        two = swap(zero, 8)
        zero_x, zero_y = swap(zero, 1), swap(zero, 2)
        zero_d = swap(zero_x, 2)
        two_x, two_y = swap(two, 1), swap(two, 2)
        to_near = [(2 * v + 1 - (v >> 3), 2 * v + (v >> 3)) for v in range(vocab)]
        to_away = [(b, a) for a, b in to_near]
        mine = (me >> 3) == core
        where = jnp.stack([mine.astype(jnp.int32), me & 3])

        def product(blocks, pairs, earlier=()):
            logits = dot(stack_rows(blocks, earlier))
            return logits, lax.ppermute(logits, ("vocab", "hid"), pairs)

        def chunk(near, away):
            near, away = jnp.concatenate(near), jnp.concatenate(away)
            other = dot(jnp.where(mine, away, near))
            came = lax.ppermute(other, "hid", [(0, 1), (1, 0)])
            kept = dot(jnp.where(mine, near, away))
            return softmax_tiles(where, [(kept, came)] * 2, 4)

        near = product([zero, zero_x, zero_y, zero_d], to_near)
        two_d, two_e = halves(two_x, two_y, (near[0],))
        two_d, two_e = swap(two_d, 2), swap(two_e, 1)
        two_all = [two, two_x, two_y, two_d, two_e]
        one, three = swap(hold(zero, two), 4), swap(two, 4)
        one_x, one_y = swap(one, 1), swap(one, 2)
        three_x, three_y = swap(three, 1), swap(three, 2)
        one_d, three_d = swap(one_x, 2), swap(three_y, 1)
        away = product(two_all, to_away, (one, three))
        first = softmax_tiles(where, [away, near], 4)
        second = chunk([one, one_x, one_y, one_d], [three, three_x, three_y, three_d])
        rows = 4 * zero.shape[0]
        received = [exchange(first, rows), exchange(second, rows)]

        def place(sender, group):
            return (sender >> 2 & 1) ^ group
    else:
        gathered = lax.all_gather(hidden_states, "vocab", axis=0, tiled=True)
        logits = lax.psum_scatter(dot(gathered), "hid", scatter_dimension=0, tiled=True)
        rows = logits.shape[0]
        where = jnp.zeros((2,), jnp.int32)
        weights = softmax_tiles(where, [(logits, jnp.zeros_like(logits))], 1)
        received = [exchange(weights, rows)]

        def place(sender, group):
            return group

    return sum_slots(received, place)


def solution(mesh):
    return jax.shard_map(
        per_device,
        mesh=mesh,
        in_specs=(P("vocab", "hid"), P("hid", "vocab"), P("vocab", None), P("vocab", None, None)),
        out_specs=P("hid", "vocab"),
        check_vma=False,
    )
```

time: 386 us -> 162 us (0.42)
  blocking collectives: 184 us -> 42.1 us
  waiting for transfers between devices: 103 us -> 41.5 us
  local copies, waits for them, and re-layouts: 28.6 us -> 10.3 us
  between operations: 13.5 us -> 0.39 us
  Pallas kernels: 0 us -> 12.6 us
  starting transfers between devices: 20.8 us -> 32.4 us
  matrix products: 29.1 us -> 19.4 us
  other arithmetic: 5.16 us -> 0.08 us
    psum x1 -> x0, blocking collectives: 153 us -> none  [per_device(): denominator = lax.psum(jnp.sum(exp_values, axis=1), 'vocab')]
    all_gather x1 -> x0, waiting for transfers between devices: 97.5 us -> none  [per_device(): gathered = lax.all_gather(hidden_states, 'vocab', axis=0, tiled=True)]
    all_to_all x0 -> x1, blocking collectives: none -> 42.1 us  [exchange(): lax.all_to_all(sent, 'vocab', split_axis=0, concat_axis=0, tiled=True)]
    pmax x1 -> x0, blocking collectives: 30.9 us -> none  [per_device(): row_top = lax.pmax(jnp.max(logits, axis=1), 'vocab')]
    ppermute x0 -> x19, waiting for transfers between devices: none -> 24.7 us  [the longest x16 24.7 us: swap(): return lax.ppermute(x, 'vocab', [(i, i ^ k) for i in range(vocab)])]
    ppermute x0 -> x19, starting transfers between devices: none -> 23.2 us  [the longest x16 20.4 us: swap(): return lax.ppermute(x, 'vocab', [(i, i ^ k) for i in range(vocab)])]
    all_to_all x2 -> x1, waiting for transfers between devices: 0.01 us -> 16.8 us  [exchange(): lax.all_to_all(sent, 'vocab', split_axis=0, concat_axis=0, tiled=True)]
    pallas_call x0 -> x9, Pallas kernels: none -> 12.6 us  [the longest x1 7.26 us: sum_slots(): pl.pallas_call(functools.partial(sum_kernel, senders, place), out_shape=j...]
  transfers between devices with their start and end apart: 4 -> 20, of which waited for: 2 -> 7; matrix products, arithmetic and copies ran while one was open for 7% -> 18% of each run, Pallas kernels for 0% -> 3%
where the time goes in v2:
time: 162 us; the launch traced here: 159 us
  blocking collectives  42.1 us (26%)
  waiting for transfers between devices  41.5 us (26%)
  starting transfers between devices  32.4 us (20%)
  matrix products  19.4 us (12%)
  Pallas kernels  12.6 us (8%)
  local copies, waits for them, and re-layouts  10.3 us (6%)
    all_to_all x1, blocking collectives, exchange(): lax.all_to_all(sent, 'vocab', split_axis=0, concat_axis=0, tiled=True)  42.1 us
    ppermute x16, waiting for transfers between devices, swap(): return lax.ppermute(x, 'vocab', [(i, i ^ k) for i in range(vocab)])  24.7 us
    ppermute x16, starting transfers between devices, swap(): return lax.ppermute(x, 'vocab', [(i, i ^ k) for i in range(vocab)])  20.4 us
    dot_general x4, matrix products, dot(): return jnp.dot(x, head_weight, preferred_element_type=jnp.float32)  19.4 us
    all_to_all x1, waiting for transfers between devices, exchange(): lax.all_to_all(sent, 'vocab', split_axis=0, concat_axis=0, tiled=True)  16.8 us
    all_to_all x1, starting transfers between devices, exchange(): lax.all_to_all(sent, 'vocab', split_axis=0, concat_axis=0, tiled=True)  9.26 us
    pallas_call x1, Pallas kernels, sum_slots(): pl.pallas_call(functools.partial(sum_kernel, senders, place), out_shape=j...  7.26 us
    unnamed x25, local copies, waits for them, and re-layouts  6.55 us
  transfers between devices with their start and end apart: 20, of which 7 were waited for; matrix products, arithmetic and copies ran while one was open for 18% of the time, Pallas kernels for 3%

profile of v2, /device:TPU:10, one launch (start us, length us, event | category | flops | bytes accessed | tf_op | source)
XLA Modules:
  0.0 158.8 jit_solution(2691085760677016808)
XLA Ops:
  0.5 2.6 %collective-permute-start = (bf16[48,4096]{1,0:T(8,128)(2,1)}, bf16[48,4096]{1,0:T(8,128)(2,1)S(1)}, u32[]{:S(2)}, u32[]{:S(2)}) collective-permute-start(bf16[48,4096]{1,0:T(8,128)(2,1)} %x_ref.1), channel_id=1, source_target_pairs={{0,16},{2,18},{4,20},{6,22},{8,24},{10,26},{12,28},{14,30},{16,0},... | collective-permute-start | bytes 1179656 | tf_op jit(solution)/shard_map/ppermute | solution.py:243
  3.1 1.5 collective-permute-start.4
  4.6 6.4 %collective-permute-done.3.refs_1_ = bf16[48,4096]{1,0:T(8,128)(2,1)S(1)} collective-permute-done((bf16[48,4096]{1,0:T(8,128)(2,1)}, bf16[48,4096]{1,0:T(8,128)(2,1)S(1)}, u32[]{:S(2)}, u32[]{:S(2)}) %collective-permute-start.3) | collective-permute-done | bytes 393248 | tf_op jit(solution)/shard_map/ppermute | solution.py:243
  11.1 1.5 collective-permute-start.5
  13.5 6.3 %collective-permute-done.earlier_ref.refs_0_ = bf16[48,4096]{1,0:T(8,128)(2,1)S(1)} collective-permute-done((bf16[48,4096]{1,0:T(8,128)(2,1)}, bf16[48,4096]{1,0:T(8,128)(2,1)S(1)}, u32[]{:S(2)}, u32[]{:S(2)}) %collective-permute-start) | collective-permute-done | bytes 393248 | tf_op jit(solution)/shard_map/ppermute | solution.py:243
  19.8 1.0 copy-done.2
  20.9 1.3 collective-permute-start.8
  23.0 1.5 collective-permute-start.1
  24.5 1.5 collective-permute-start.2
  26.1 6.3 %fusion.6.refs_0_.refs_2_ = f32[192,1280]{1,0:T(8,128)S(1)} fusion(bf16[192,4096]{1,0:T(8,128)(2,1)S(1)} %shard_map.46, bf16[4096,1280]{1,0:T(8,128)(2,1)} %param.5), kind=kOutput, calls=%fused_computation.15 | convolution fusion | flops 2013265920 | bytes 13041664 | tf_op jit(solution)/shard_map/dot_general | solution.py:246
  32.4 1.3 collective-permute-start.11
  34.7 1.6 collective-permute-start.6
  36.8 1.5 collective-permute-start.12
  39.1 1.3 collective-permute-done.9.refs_6_
  40.4 1.5 collective-permute-start.13
  42.7 1.5 collective-permute-start.15
  44.8 2.3 %fusion.7.refs_0_ = f32[192,1280]{1,0:T(8,128)S(1)} fusion(bf16[192,4096]{1,0:T(8,128)(2,1)S(1)} %shard_map.49, bf16[4096,1280]{1,0:T(8,128)(2,1)S(1)} %bitcast.10), kind=kOutput, calls=%fused_computation.16 | convolution fusion | flops 2013265920 | bytes 13041664 | tf_op jit(solution)/shard_map/dot_general | solution.py:246
  47.2 5.4 %collective-permute-done.12 = bf16[48,4096]{1,0:T(8,128)(2,1)S(1)} collective-permute-done((bf16[48,4096]{1,0:T(8,128)(2,1)S(1)}, bf16[48,4096]{1,0:T(8,128)(2,1)S(1)}, u32[]{:S(2)}, u32[]{:S(2)}) %collective-permute-start.12) | collective-permute-done | bytes 393248 | tf_op jit(solution)/shard_map/ppermute | solution.py:243
  52.5 1.3 collective-permute-start.10
  54.7 4.3 %collective-permute-done.15 = bf16[48,4096]{1,0:T(8,128)(2,1)S(1)} collective-permute-done((bf16[48,4096]{1,0:T(8,128)(2,1)S(1)}, bf16[48,4096]{1,0:T(8,128)(2,1)S(1)}, u32[]{:S(2)}, u32[]{:S(2)}) %collective-permute-start.15) | collective-permute-done | bytes 393248 | tf_op jit(solution)/shard_map/ppermute | solution.py:243
  58.9 1.5 collective-permute-start.14
  63.6 2.1 %shard_map.51 = bf16[16,400,128]{2,1,0:T(8,128)(2,1)} custom-call(s32[1]{0:T(128)} %bitcast.me_ref, s32[32]{0:T(128)S(1)} %reshape.3.pair_ref, bf16[1936,128]{1,0:T(8,128)(2,1)S(1)} %shard_map.50.tiles_ref, bf16[16,128,128]{2,1,0:T(8,128)(2,1)S(1)} %copy-done), custom_call_target="tpu_custom_call" | custom-call | flops 100663296 | bytes 3276800 | tf_op jit(solution)/shard_map/pallas_call | solution.py:128
  65.7 9.3 %all-to-all-start = ((bf16[16,400,128]{2,1,0:T(8,128)(2,1)}), bf16[16,400,128]{2,1,0:T(8,128)(2,1)S(1)}, u32[]{:S(2)}, u32[]{:S(2)}) async-start(bf16[16,400,128]{2,1,0:T(8,128)(2,1)} %shard_map.51), calls=%async_computation | async-start | bytes 3276800 | tf_op jit(solution)/shard_map/all_to_all | solution.py:250
  75.8 1.9 %constant_dynamic-update-slice_fusion = bf16[192,4096]{1,0:T(8,128)(2,1)} fusion(bf16[192,4096]{1,0:T(8,128)(2,1)} %constant_dynamic-update-slice_fusion.1, bf16[48,4096]{1,0:T(8,128)(2,1)} %collective-permute-done.14), kind=kLoop, calls=%fused_computation.6 | loop fusion | bytes 786432 | tf_op jit(solution)/shard_map/concatenate | solution.py:268
  77.7 1.8 %constant_dynamic-update-slice_fusion.4 = bf16[192,4096]{1,0:T(8,128)(2,1)} fusion(bf16[192,4096]{1,0:T(8,128)(2,1)} %constant_dynamic-update-slice_fusion.5, bf16[48,4096]{1,0:T(8,128)(2,1)} %collective-permute-done.17), kind=kLoop, calls=%fused_computation.10 | loop fusion | bytes 786432 | tf_op jit(solution)/shard_map/concatenate | solution.py:268
  79.4 6.9 %fusion = f32[192,1280]{1,0:T(8,128)S(1)} fusion(bf16[4096,1280]{1,0:T(8,128)(2,1)} %param.5, bf16[192,4096]{1,0:T(8,128)(2,1)} %constant_dynamic-update-slice_fusion.4, bf16[192,4096]{1,0:T(8,128)(2,1)} %constant_dynamic-update-slice_fusion, pred[]{:T(512)S(6)} %eq.3), kind=kOutput, calls=%fused_computation | convolution fusion | flops 2014052352 | bytes 14614529 | tf_op jit(solution)/shard_map/dot_general | solution.py:246
  86.4 3.9 %fusion.2.refs_0_.refs_2_ = f32[192,1280]{1,0:T(8,128)S(1)} fusion(bf16[4096,1280]{1,0:T(8,128)(2,1)S(1)} %bitcast.12, bf16[192,4096]{1,0:T(8,128)(2,1)} %constant_dynamic-update-slice_fusion, bf16[192,4096]{1,0:T(8,128)(2,1)} %constant_dynamic-update-slice_fusion.4, pred[]{:T(512)S(6)} %eq.3), kind=kOutput, calls=%fused_computation.2 | convolution fusion | flops 2014052352 | bytes 14614529 | tf_op jit(solution)/shard_map/dot_general | solution.py:246
  90.3 1.1 shard_map.52.tiles_ref
  91.4 1.0 shard_map.53
  92.4 16.8 %all-to-all-done.refs_0_ = bf16[16,400,128]{2,1,0:T(8,128)(2,1)S(1)} async-done(((bf16[16,400,128]{2,1,0:T(8,128)(2,1)}), bf16[16,400,128]{2,1,0:T(8,128)(2,1)S(1)}, u32[]{:S(2)}, u32[]{:S(2)}) %all-to-all-start) | async-done | bytes 1638432 | tf_op jit(solution)/shard_map/all_to_all | solution.py:250
  109.2 42.1 %all_to_all.10.refs_1_ = bf16[16,400,128]{2,1,0:T(8,128)(2,1)S(1)} all-to-all(bf16[16,400,128]{2,1,0:T(8,128)(2,1)S(1)} %shard_map.53), channel_id=1, replica_groups=mesh['vocab'=16,'hid'=2] {'vocab'}, dimensions={0} | all-to-all | bytes 3276800 | tf_op jit(solution)/shard_map/all_to_all | solution.py:250
  151.4 7.3 %shard_map.54 = f32[384,1536]{1,0:T(8,128)} custom-call(bf16[16,400,128]{2,1,0:T(8,128)(2,1)S(1)} %all-to-all-done.refs_0_, bf16[16,400,128]{2,1,0:T(8,128)(2,1)S(1)} %all_to_all.10.refs_1_), custom_call_target="tpu_custom_call" | custom-call | flops 3145728 | bytes 2359296 | tf_op jit(solution)/shard_map/pallas_call | solution.py:185
  (53 shorter events, 10.8 us)
Async XLA Ops:
  0.0 11.1 %collective-permute-start.3 = (bf16[48,4096]{1,0:T(8,128)(2,1)}, bf16[48,4096]{1,0:T(8,128)(2,1)S(1)}, u32[]{:S(2)}, u32[]{:S(2)}) collective-permute-start(bf16[48,4096]{1,0:T(8,128)(2,1)} %x_ref.1), channel_id=1, source_target_pairs={{0,2},{2,0},{4,6},{6,4},{8,10},{10,8},{12,14},{14,12},{16,18},{18,... | collective-permute-start | bytes 1179656 | tf_op jit(solution)/shard_map/ppermute | solution.py:243
  0.5 19.3 %collective-permute-start = (bf16[48,4096]{1,0:T(8,128)(2,1)}, bf16[48,4096]{1,0:T(8,128)(2,1)S(1)}, u32[]{:S(2)}, u32[]{:S(2)}) collective-permute-start(bf16[48,4096]{1,0:T(8,128)(2,1)} %x_ref.1), channel_id=1, source_target_pairs={{0,16},{2,18},{4,20},{6,22},{8,24},{10,26},{12,28},{14,30},{16,0},... | collective-permute-start | bytes 1179656 | tf_op jit(solution)/shard_map/ppermute | solution.py:243
  3.1 21.3 %collective-permute-start.4 = (bf16[48,4096]{1,0:T(8,128)(2,1)}, bf16[48,4096]{1,0:T(8,128)(2,1)S(1)}, u32[]{:S(2)}, u32[]{:S(2)}) collective-permute-start(bf16[48,4096]{1,0:T(8,128)(2,1)} %x_ref.1), channel_id=1, source_target_pairs={{0,4},{2,6},{4,0},{6,2},{8,12},{10,14},{12,8},{14,10},{16,20},{18,... | collective-permute-start | bytes 1179656 | tf_op jit(solution)/shard_map/ppermute | solution.py:243
  11.1 14.9 %collective-permute-start.5 = (bf16[48,4096]{1,0:T(8,128)(2,1)S(1)}, bf16[48,4096]{1,0:T(8,128)(2,1)S(1)}, u32[]{:S(2)}, u32[]{:S(2)}) collective-permute-start(bf16[48,4096]{1,0:T(8,128)(2,1)S(1)} %collective-permute-done.3.refs_1_), channel_id=1, source_target_pairs={{0,4},{2,6},{4,0},{6,2},{8,12},{10,14},{12,8},{14,10},{16,20},{18,... | collective-permute-start | bytes 1179656 | tf_op jit(solution)/shard_map/ppermute | solution.py:243
  19.8 1.0 copy-start.2
  20.9 15.9 %collective-permute-start.8 = (bf16[48,4096]{1,0:T(8,128)(2,1)S(1)}, bf16[48,4096]{1,0:T(8,128)(2,1)S(1)}, u32[]{:S(2)}, u32[]{:S(2)}) collective-permute-start(bf16[48,4096]{1,0:T(8,128)(2,1)S(1)} %shard_map.48), channel_id=1, source_target_pairs={{0,8},{2,10},{4,12},{6,14},{8,0},{10,2},{12,4},{14,6},{16,24},{18,... | collective-permute-start | bytes 1179656 | tf_op jit(solution)/shard_map/ppermute | solution.py:243
  22.2 18.2 %collective-permute-start.9 = (bf16[48,4096]{1,0:T(8,128)(2,1)S(1)}, bf16[48,4096]{1,0:T(8,128)(2,1)S(1)}, u32[]{:S(2)}, u32[]{:S(2)}) collective-permute-start(bf16[48,4096]{1,0:T(8,128)(2,1)S(1)} %collective-permute-done.earlier_ref.refs_0_), channel_id=1, source_target_pairs={{0,8},{2,10},{4,12},{6,14},{8,0},{10,2},{12,4},{14,6},{16,24},{18,... | collective-permute-start | bytes 1179656 | tf_op jit(solution)/shard_map/ppermute | solution.py:243
  23.0 10.8 %collective-permute-start.1 = (bf16[48,4096]{1,0:T(8,128)(2,1)S(1)}, bf16[48,4096]{1,0:T(8,128)(2,1)S(1)}, u32[]{:S(2)}, u32[]{:S(2)}) collective-permute-start(bf16[48,4096]{1,0:T(8,128)(2,1)S(1)} %collective-permute-done.earlier_ref.refs_0_), channel_id=1, source_target_pairs={{0,2},{2,0},{4,6},{6,4},{8,10},{10,8},{12,14},{14,12},{16,18},{18,... | collective-permute-start | bytes 1179656 | tf_op jit(solution)/shard_map/ppermute | solution.py:243
  24.5 10.2 %collective-permute-start.2 = (bf16[48,4096]{1,0:T(8,128)(2,1)S(1)}, bf16[48,4096]{1,0:T(8,128)(2,1)S(1)}, u32[]{:S(2)}, u32[]{:S(2)}) collective-permute-start(bf16[48,4096]{1,0:T(8,128)(2,1)S(1)} %collective-permute-done.earlier_ref.refs_0_), channel_id=1, source_target_pairs={{0,4},{2,6},{4,0},{6,2},{8,12},{10,14},{12,8},{14,10},{16,20},{18,... | collective-permute-start | bytes 1179656 | tf_op jit(solution)/shard_map/ppermute | solution.py:243
  26.0 18.8 %slice-start = ((s8[10485760]{0:T(1024)(128)(4,1)}), s8[4194304]{0:T(1024)(128)(4,1)S(1)}, s32[]{:S(2)}) async-start(s8[10485760]{0:T(1024)(128)(4,1)} %bitcast.9), calls=%async_computation.2 | async-start | bytes 8388608
  26.1 18.7 %slice-start.1 = ((s8[10485760]{0:T(1024)(128)(4,1)}), s8[4194304]{0:T(1024)(128)(4,1)S(1)}, s32[]{:S(2)}) async-start(s8[10485760]{0:T(1024)(128)(4,1)} %bitcast.9), calls=%async_computation.3 | async-start | bytes 8388608
  26.1 18.7 %slice-start.2 = ((s8[10485760]{0:T(1024)(128)(4,1)}), s8[2097152]{0:T(1024)(128)(4,1)S(1)}, s32[]{:S(2)}) async-start(s8[10485760]{0:T(1024)(128)(4,1)} %bitcast.9), calls=%async_computation.4 | async-start | bytes 4194304
  32.4 30.1 %collective-permute-start.11 = (f32[192,1280]{1,0:T(8,128)S(1)}, f32[192,1280]{1,0:T(8,128)S(1)}, u32[]{:S(2)}, u32[]{:S(2)}) collective-permute-start(f32[192,1280]{1,0:T(8,128)S(1)} %fusion.6.refs_0_.refs_2_), channel_id=1, source_target_pairs={{1,0},{3,2},{5,4},{7,6},{9,8},{11,10},{13,12},{15,14},{16,17},{18,... | collective-permute-start | bytes 2949128 | tf_op jit(solution)/shard_map/ppermute | solution.py:265
  34.7 8.0 %collective-permute-start.6 = (bf16[48,2048]{1,0:T(8,128)(2,1)S(1)}, bf16[48,2048]{1,0:T(8,128)(2,1)S(1)}, u32[]{:S(2)}, u32[]{:S(2)}) collective-permute-start(bf16[48,2048]{1,0:T(8,128)(2,1)S(1)} %get-tuple-element.7), channel_id=1, source_target_pairs={{0,4},{2,6},{4,0},{6,2},{8,12},{10,14},{12,8},{14,10},{16,20},{18,... | collective-permute-start | bytes 589832 | tf_op jit(solution)/shard_map/ppermute | solution.py:243
  36.3 7.9 %collective-permute-start.7 = (bf16[48,2048]{1,0:T(8,128)(2,1)S(1)}, bf16[48,2048]{1,0:T(8,128)(2,1)S(1)}, u32[]{:S(2)}, u32[]{:S(2)}) collective-permute-start(bf16[48,2048]{1,0:T(8,128)(2,1)S(1)} %get-tuple-element.8), channel_id=1, source_target_pairs={{0,2},{2,0},{4,6},{6,4},{8,10},{10,8},{12,14},{14,12},{16,18},{18,... | collective-permute-start | bytes 589832 | tf_op jit(solution)/shard_map/ppermute | solution.py:243
  36.8 15.7 %collective-permute-start.12 = (bf16[48,4096]{1,0:T(8,128)(2,1)S(1)}, bf16[48,4096]{1,0:T(8,128)(2,1)S(1)}, u32[]{:S(2)}, u32[]{:S(2)}) collective-permute-start(bf16[48,4096]{1,0:T(8,128)(2,1)S(1)} %collective-permute-done.8.refs_5_), channel_id=1, source_target_pairs={{0,2},{2,0},{4,6},{6,4},{8,10},{10,8},{12,14},{14,12},{16,18},{18,... | collective-permute-start | bytes 1179656 | tf_op jit(solution)/shard_map/ppermute | solution.py:243
  40.4 34.5 %collective-permute-start.13 = (bf16[48,4096]{1,0:T(8,128)(2,1)S(1)}, bf16[48,4096]{1,0:T(8,128)(2,1)S(1)}, u32[]{:S(2)}, u32[]{:S(2)}) collective-permute-start(bf16[48,4096]{1,0:T(8,128)(2,1)S(1)} %collective-permute-done.8.refs_5_), channel_id=1, source_target_pairs={{0,4},{2,6},{4,0},{6,2},{8,12},{10,14},{12,8},{14,10},{16,20},{18,... | collective-permute-start | bytes 1179656 | tf_op jit(solution)/shard_map/ppermute | solution.py:243
  42.7 16.2 %collective-permute-start.15 = (bf16[48,4096]{1,0:T(8,128)(2,1)S(1)}, bf16[48,4096]{1,0:T(8,128)(2,1)S(1)}, u32[]{:S(2)}, u32[]{:S(2)}) collective-permute-start(bf16[48,4096]{1,0:T(8,128)(2,1)S(1)} %collective-permute-done.9.refs_6_), channel_id=1, source_target_pairs={{0,2},{2,0},{4,6},{6,4},{8,10},{10,8},{12,14},{14,12},{16,18},{18,... | collective-permute-start | bytes 1179656 | tf_op jit(solution)/shard_map/ppermute | solution.py:243
  44.2 16.3 %collective-permute-start.16 = (bf16[48,4096]{1,0:T(8,128)(2,1)S(1)}, bf16[48,4096]{1,0:T(8,128)(2,1)S(1)}, u32[]{:S(2)}, u32[]{:S(2)}) collective-permute-start(bf16[48,4096]{1,0:T(8,128)(2,1)S(1)} %collective-permute-done.9.refs_6_), channel_id=1, source_target_pairs={{0,4},{2,6},{4,0},{6,2},{8,12},{10,14},{12,8},{14,10},{16,20},{18,... | collective-permute-start | bytes 1179656 | tf_op jit(solution)/shard_map/ppermute | solution.py:243
  52.5 10.0 %collective-permute-start.10 = (f32[192,1280]{1,0:T(8,128)S(1)}, f32[192,1280]{1,0:T(8,128)S(1)}, u32[]{:S(2)}, u32[]{:S(2)}) collective-permute-start(f32[192,1280]{1,0:T(8,128)S(1)} %fusion.7.refs_0_), channel_id=1, source_target_pairs={{0,1},{2,3},{4,5},{6,7},{8,9},{10,11},{12,13},{14,15},{17,16},{19,... | collective-permute-start | bytes 2949128 | tf_op jit(solution)/shard_map/ppermute | solution.py:265
  58.9 16.8 %collective-permute-start.14 = (bf16[48,4096]{1,0:T(8,128)(2,1)S(1)}, bf16[48,4096]{1,0:T(8,128)(2,1)}, u32[]{:S(2)}, u32[]{:S(2)}) collective-permute-start(bf16[48,4096]{1,0:T(8,128)(2,1)S(1)} %collective-permute-done.12), channel_id=1, source_target_pairs={{0,4},{2,6},{4,0},{6,2},{8,12},{10,14},{12,8},{14,10},{16,20},{18,... | collective-permute-start | bytes 1179656 | tf_op jit(solution)/shard_map/ppermute | solution.py:243
  60.5 17.2 %collective-permute-start.17 = (bf16[48,4096]{1,0:T(8,128)(2,1)S(1)}, bf16[48,4096]{1,0:T(8,128)(2,1)}, u32[]{:S(2)}, u32[]{:S(2)}) collective-permute-start(bf16[48,4096]{1,0:T(8,128)(2,1)S(1)} %collective-permute-done.16), channel_id=1, source_target_pairs={{0,2},{2,0},{4,6},{6,4},{8,10},{10,8},{12,14},{14,12},{16,18},{18,... | collective-permute-start | bytes 1179656 | tf_op jit(solution)/shard_map/ppermute | solution.py:243
  62.6 1.0 copy-start
  65.7 43.5 %all-to-all-start = ((bf16[16,400,128]{2,1,0:T(8,128)(2,1)}), bf16[16,400,128]{2,1,0:T(8,128)(2,1)S(1)}, u32[]{:S(2)}, u32[]{:S(2)}) async-start(bf16[16,400,128]{2,1,0:T(8,128)(2,1)} %shard_map.51), calls=%async_computation | async-start | bytes 3276800 | tf_op jit(solution)/shard_map/all_to_all | solution.py:250
  75.8 10.6 %slice-start.3 = ((s8[10485760]{0:T(1024)(128)(4,1)}), s8[4194304]{0:T(1024)(128)(4,1)S(1)}, s32[]{:S(2)}) async-start(s8[10485760]{0:T(1024)(128)(4,1)} %bitcast.11), calls=%async_computation.5 | async-start | bytes 8388608
  79.4 7.0 %slice-start.4 = ((s8[10485760]{0:T(1024)(128)(4,1)}), s8[4194304]{0:T(1024)(128)(4,1)S(1)}, s32[]{:S(2)}) async-start(s8[10485760]{0:T(1024)(128)(4,1)} %bitcast.11), calls=%async_computation.6 | async-start | bytes 8388608
  79.4 7.0 %slice-start.5 = ((s8[10485760]{0:T(1024)(128)(4,1)}), s8[2097152]{0:T(1024)(128)(4,1)S(1)}, s32[]{:S(2)}) async-start(s8[10485760]{0:T(1024)(128)(4,1)} %bitcast.11), calls=%async_computation.7 | async-start | bytes 4194304
  86.3 4.0 %collective-permute-start.18 = (f32[192,1280]{1,0:T(8,128)S(1)}, f32[192,1280]{1,0:T(8,128)S(1)}, u32[]{:S(2)}, u32[]{:S(2)}) collective-permute-start(f32[192,1280]{1,0:T(8,128)S(1)} %fusion), channel_id=1, source_target_pairs={{0,1},{1,0},{2,3},{3,2},{4,5},{5,4},{6,7},{7,6},{8,9},{9,8},{10,11... | collective-permute-start | bytes 2949128 | tf_op jit(solution)/shard_map/ppermute | solution.py:270
  90.3 1.1 copy-start.1

commit v3 on v2

--- a/solution.py
+++ b/solution.py
@@ -140,19 +140,73 @@
     )(me, pairs, tiles, focus_blocks)
 
 
-def sum_kernel(senders, place, *refs):
-    out_ref, level_ref, factor_ref, label_ref, sem = refs[-5:]
-    chunks = len(refs) - 5
-    rows = (refs[0].shape[1] - STATS) // CAP
+def focus_each_kernel(rows, me_ref, pair_ref, tiles_ref, focus_ref, *refs):
+    outs, seen_ref = refs[:-1], refs[-1]
+    first = me_ref[0] * ((tiles_ref.shape[0] - STATS) // rows)
+    stats = tiles_ref[tiles_ref.shape[0] - STATS :, :]
+    bottom = pl.ds(CAP * rows, STATS)
+    for o, out_ref in enumerate(outs):
+        out_ref[bottom, :] = stats
+        seen_ref[o] = 0
+    row = lax.broadcasted_iota(jnp.int32, (STATS, TILE), 0)
+    lane = lax.broadcasted_iota(jnp.int32, (STATS, TILE), 1)
+    scale = (1 << 19) // STILES_DEV + 1
+
+    @pl.loop(0, focus_ref.shape[0])
+    def _(e):
+        student = pair_ref[2 * e + 1]
+        owner = student * scale >> 19
+        here = owner ^ me_ref[0]
+        rank = seen_ref[here]
+        seen_ref[here] = rank + 1
+        label = (student - owner * STILES_DEV + 1).astype(jnp.float32)
+        mark = jnp.where((row == LABEL_ROW) & (lane == rank), label, 0.0).astype(jnp.bfloat16)
+        source = pl.ds(pl.multiple_of((pair_ref[2 * e] - first) * rows, 16), rows)
+        term = jnp.dot(tiles_ref[source, :], focus_ref[e], preferred_element_type=jnp.float32)
+        term = term.astype(jnp.bfloat16)
+        target = pl.ds(pl.multiple_of(rank * rows, 16), rows)
+        for o, out_ref in enumerate(outs):
+
+            @pl.when(here == o)
+            def _(out_ref=out_ref):
+                out_ref[bottom, :] += mark
+                out_ref[target, :] = term
+
+
+def focus_each(me, pairs, tiles, focus_blocks, rows, owners):
+    size = CAP * rows + STATS
+    return pl.pallas_call(
+        functools.partial(focus_each_kernel, rows),
+        out_shape=[jax.ShapeDtypeStruct((size, TILE), jnp.bfloat16)] * owners,
+        in_specs=[SMEM, SMEM, VMEM, VMEM],
+        out_specs=[VMEM] * owners,
+        scratch_shapes=[pltpu.SMEM((owners,), jnp.int32)],
+        compiler_params=kernel_params(32),
+    )(me, pairs, tiles, focus_blocks)
+
+
+def sum_kernel(senders, place, me_ref, *refs):
+    *whole_refs, out_ref, level_ref, factor_ref, label_ref, sem = refs
+    me = me_ref[0]
+    chunks = []
+    while whole_refs:
+        if len(whole_refs[0].shape) == 3:
+            whole = whole_refs.pop(0)
+            chunks.append([whole.at[s ^ me] for s in range(senders)])
+        else:
+            chunks.append(whole_refs[:senders])
+            del whole_refs[:senders]
+    rows = (chunks[0][0].shape[0] - STATS) // CAP
     for s in range(senders):
-        marks = refs[0][s, CAP * rows :, :].astype(jnp.float32)
+        marks = chunks[0][s][CAP * rows :, :].astype(jnp.float32)
         level_ref[2, s : s + 1, :TILE] = marks[LABEL_ROW : LABEL_ROW + 1]
     to_scalars = pltpu.make_async_copy(level_ref.at[2, :, :TILE], label_ref, sem)
     to_scalars.start()
     out_ref[...] = jnp.zeros_like(out_ref)
-    for group in range(chunks):
+    for group in range(len(chunks)):
+        came = [chunks[place(s, group)][s] for s in range(senders)]
         for s in range(senders):
-            stats = refs[place(s, group)][s, CAP * rows :, :].astype(jnp.float32)
+            stats = came[s][CAP * rows :, :].astype(jnp.float32)
             for half in range(2):
                 columns = pl.ds(half * TILE, TILE)
                 for kind in range(2):
@@ -164,7 +218,7 @@
         total = jnp.sum(scale * total, axis=0, keepdims=True)
         level_ref[0, :senders, :] = scale * (STILES_DEV * TILE * senders / total)
         factor_ref[...] = level_ref[0].T
-        target = pl.ds(group * rows, rows)
+        target = pl.ds(pl.multiple_of((group ^ me_ref[1]) * rows, 8), rows)
         if group == 0:
             to_scalars.wait()
         for s in range(senders):
@@ -172,20 +226,23 @@
                 label = label_ref[s, r].astype(jnp.int32) - 1
 
                 @pl.when(label >= 0)
-                def _(s=s, r=r, label=label, target=target, group=group):
+                def _(s=s, r=r, label=label, target=target, tile_ref=came[s]):
                     factor = factor_ref[:rows, s : s + 1]
                     columns = pl.ds(pl.multiple_of(label * TILE, TILE), TILE)
-                    tile = refs[place(s, group)][s, r * rows : (r + 1) * rows, :]
+                    tile = tile_ref[r * rows : (r + 1) * rows, :]
                     out_ref[target, columns] += tile.astype(jnp.float32) * factor
 
 
-def sum_slots(received, place):
-    senders, size, _ = received[0].shape
-    rows, chunks = (size - STATS) // CAP, len(received)
+def sum_slots(me, senders, received, place):
+    chunks = len(received)
+    rows = ((received[0][0] if isinstance(received[0], list) else received[0]).shape[-2] - STATS) // CAP
+    arrays = []
+    for one in received:
+        arrays += one if isinstance(one, list) else [one]
     return pl.pallas_call(
         functools.partial(sum_kernel, senders, place),
         out_shape=jax.ShapeDtypeStruct((rows * chunks, STILES_DEV * TILE), jnp.float32),
-        in_specs=[VMEM] * chunks,
+        in_specs=[SMEM] + [VMEM] * len(arrays),
         out_specs=VMEM,
         scratch_shapes=[
             pltpu.VMEM((3, TILE, 2 * TILE), jnp.float32),
@@ -199,7 +256,7 @@
             bytes_accessed=4 * rows * chunks * STILES_DEV * TILE,
             transcendentals=0,
         ),
-    )(*received)
+    )(me, *arrays)
 
 
 def hold_kernel(x_ref, earlier_ref, out_ref):
@@ -278,12 +335,16 @@
         one, three = swap(hold(zero, two), 4), swap(two, 4)
         one_x, one_y = swap(one, 1), swap(one, 2)
         three_x, three_y = swap(three, 1), swap(three, 2)
-        one_d, three_d = swap(one_x, 2), swap(three_y, 1)
+        one_d = swap(zero_d, 4)
+        three_d = swap(jnp.concatenate([two_d, two_e], axis=1), 4)
         away = product(two_all, to_away, (one, three))
         first = softmax_tiles(where, [away, near], 4)
         second = chunk([one, one_x, one_y, one_d], [three, three_x, three_y, three_d])
         rows = 4 * zero.shape[0]
-        received = [exchange(first, rows), exchange(second, rows)]
+        sent = focus_each(me[None], pairs, second, focus_blocks, rows, vocab)
+        came = [sent[0]] + [swap(sent[j], j) for j in range(1, vocab)]
+        received = [exchange(first, rows), came]
+        turn = jnp.stack([me, me >> 2 & 1])
 
         def place(sender, group):
             return (sender >> 2 & 1) ^ group
@@ -294,11 +355,12 @@
         where = jnp.zeros((2,), jnp.int32)
         weights = softmax_tiles(where, [(logits, jnp.zeros_like(logits))], 1)
         received = [exchange(weights, rows)]
+        turn = jnp.zeros((2,), jnp.int32)
 
         def place(sender, group):
             return group
 
-    return sum_slots(received, place)
+    return sum_slots(turn, vocab, received, place)
 
 
 def solution(mesh):

time: 162 us -> 154 us (0.951); the launches traced: 159 us -> 153 us
  blocking collectives: 42.1 us -> 0 us
  starting transfers between devices: 32.4 us -> 59.7 us
  waiting for transfers between devices: 41.5 us -> 50.7 us
  Pallas kernels: 12.6 us -> 15.6 us
  local copies, waits for them, and re-layouts: 10.3 us -> 8.37 us
    all_to_all x1 -> x0, blocking collectives: 42.1 us -> none  [exchange(): lax.all_to_all(sent, 'vocab', split_axis=0, concat_axis=0, tiled=True)]
    ppermute x16 -> x31, starting transfers between devices: 20.4 us -> 49.8 us  [swap(): return lax.ppermute(x, 'vocab', [(i, i ^ k) for i in range(vocab)])]
    ppermute x16 -> x31, waiting for transfers between devices: 24.7 us -> 50.7 us  [swap(): return lax.ppermute(x, 'vocab', [(i, i ^ k) for i in range(vocab)])]
    all_to_all x1, waiting for transfers between devices: 16.8 us -> 0.01 us  [exchange(): lax.all_to_all(sent, 'vocab', split_axis=0, concat_axis=0, tiled=True)]
    pallas_call x0 -> x1, Pallas kernels: none -> 4.41 us  [focus_each(): pl.pallas_call(functools.partial(focus_each_kernel, rows), out_shape=[jax...]
    all_to_all x1, starting transfers between devices: 9.26 us -> 7.16 us  [exchange(): lax.all_to_all(sent, 'vocab', split_axis=0, concat_axis=0, tiled=True)]
    concatenate x2, local copies, waits for them, and re-layouts: 3.68 us -> 1.8 us  [chunk(): near, away = (jnp.concatenate(near), jnp.concatenate(away))]
    unnamed x25 -> x29, local copies, waits for them, and re-layouts: 6.55 us -> 6.48 us
  transfers between devices with their start and end apart: 20 -> 35, of which waited for: 7 -> 14; matrix products, arithmetic and copies ran while one was open for 18% -> 16% of each run, Pallas kernels for 3% -> 6%
where the time goes in v3:
time: 154 us; the launch traced here: 153 us
  starting transfers between devices  59.7 us (39%)
  waiting for transfers between devices  50.7 us (33%)
  matrix products  18 us (12%)
  Pallas kernels  15.6 us (10%)
  local copies, waits for them, and re-layouts  8.37 us (5%)
    ppermute x31, waiting for transfers between devices, swap(): return lax.ppermute(x, 'vocab', [(i, i ^ k) for i in range(vocab)])  50.7 us
    ppermute x31, starting transfers between devices, swap(): return lax.ppermute(x, 'vocab', [(i, i ^ k) for i in range(vocab)])  49.8 us
    dot_general x4, matrix products, dot(): return jnp.dot(x, head_weight, preferred_element_type=jnp.float32)  18 us
    all_to_all x1, starting transfers between devices, exchange(): lax.all_to_all(sent, 'vocab', split_axis=0, concat_axis=0, tiled=True)  7.16 us
    pallas_call x1, Pallas kernels, sum_slots(): pl.pallas_call(functools.partial(sum_kernel, senders, place), out_shape=j...  6.8 us
    unnamed x29, local copies, waits for them, and re-layouts  6.48 us
    pallas_call x1, Pallas kernels, focus_each(): pl.pallas_call(functools.partial(focus_each_kernel, rows), out_shape=[jax...  4.41 us
  transfers between devices with their start and end apart: 35, of which 14 were waited for; matrix products, arithmetic and copies ran while one was open for 16% of the time, Pallas kernels for 6%

profile of v3, /device:TPU:10, one launch (start us, length us, event | category | flops | bytes accessed | tf_op | source)
XLA Modules:
  0.0 153.0 jit_solution(4032637527370278407)
XLA Ops:
  0.5 2.6 %collective-permute-start = (bf16[48,4096]{1,0:T(8,128)(2,1)}, bf16[48,4096]{1,0:T(8,128)(2,1)S(1)}, u32[]{:S(2)}, u32[]{:S(2)}) collective-permute-start(bf16[48,4096]{1,0:T(8,128)(2,1)} %x_ref.1), channel_id=1, source_target_pairs={{0,16},{2,18},{4,20},{6,22},{8,24},{10,26},{12,28},{14,30},{16,0},... | collective-permute-start | bytes 1179656 | tf_op jit(solution)/shard_map/ppermute | solution.py:300
  4.6 6.4 %collective-permute-done.3.refs_1_ = bf16[48,4096]{1,0:T(8,128)(2,1)S(1)} collective-permute-done((bf16[48,4096]{1,0:T(8,128)(2,1)}, bf16[48,4096]{1,0:T(8,128)(2,1)S(1)}, u32[]{:S(2)}, u32[]{:S(2)}) %collective-permute-start.3) | collective-permute-done | bytes 393248 | tf_op jit(solution)/shard_map/ppermute | solution.py:300
  13.5 6.3 %collective-permute-done.earlier_ref.refs_0_ = bf16[48,4096]{1,0:T(8,128)(2,1)S(1)} collective-permute-done((bf16[48,4096]{1,0:T(8,128)(2,1)}, bf16[48,4096]{1,0:T(8,128)(2,1)S(1)}, u32[]{:S(2)}, u32[]{:S(2)}) %collective-permute-start) | collective-permute-done | bytes 393248 | tf_op jit(solution)/shard_map/ppermute | solution.py:300
  22.2 1.5 collective-permute-start.1
  26.1 6.3 %fusion.6.refs_0_.refs_2_ = f32[192,1280]{1,0:T(8,128)S(1)} fusion(bf16[192,4096]{1,0:T(8,128)(2,1)S(1)} %shard_map.46, bf16[4096,1280]{1,0:T(8,128)(2,1)} %param.5), kind=kOutput, calls=%fused_computation.17 | convolution fusion | flops 2013265920 | bytes 13041664 | tf_op jit(solution)/shard_map/dot_general | solution.py:303
  35.4 1.5 collective-permute-start.12
  37.0 3.4 %collective-permute-done.9.refs_6_ = bf16[48,4096]{1,0:T(8,128)(2,1)S(1)} collective-permute-done((bf16[48,4096]{1,0:T(8,128)(2,1)S(1)}, bf16[48,4096]{1,0:T(8,128)(2,1)S(1)}, u32[]{:S(2)}, u32[]{:S(2)}) %collective-permute-start.9) | collective-permute-done | bytes 393248 | tf_op jit(solution)/shard_map/ppermute | solution.py:300
  44.6 2.3 %fusion.7.refs_0_ = f32[192,1280]{1,0:T(8,128)S(1)} fusion(bf16[192,4096]{1,0:T(8,128)(2,1)S(1)} %shard_map.49, bf16[4096,1280]{1,0:T(8,128)(2,1)S(1)} %bitcast.11), kind=kOutput, calls=%fused_computation.18 | convolution fusion | flops 2013265920 | bytes 13041664 | tf_op jit(solution)/shard_map/dot_general | solution.py:303
  47.0 4.1 %collective-permute-done.12 = bf16[48,4096]{1,0:T(8,128)(2,1)S(1)} collective-permute-done((bf16[48,4096]{1,0:T(8,128)(2,1)S(1)}, bf16[48,4096]{1,0:T(8,128)(2,1)S(1)}, u32[]{:S(2)}, u32[]{:S(2)}) %collective-permute-start.12) | collective-permute-done | bytes 393248 | tf_op jit(solution)/shard_map/ppermute | solution.py:300
  52.5 1.7 %collective-permute-start.16 = (bf16[48,4096]{1,0:T(8,128)(2,1)S(1)}, bf16[48,4096]{1,0:T(8,128)(2,1)}, u32[]{:S(2)}, u32[]{:S(2)}) collective-permute-start(bf16[48,4096]{1,0:T(8,128)(2,1)S(1)} %collective-permute-done.9.refs_6_), channel_id=1, source_target_pairs={{0,4},{2,6},{4,0},{6,2},{8,12},{10,14},{12,8},{14,10},{16,20},{18,... | collective-permute-start | bytes 1179656 | tf_op jit(solution)/shard_map/ppermute | solution.py:300
  57.7 2.1 %shard_map.51 = bf16[16,400,128]{2,1,0:T(8,128)(2,1)} custom-call(s32[1]{0:T(128)} %bitcast.me_ref, s32[32]{0:T(128)S(1)} %reshape.3.pair_ref, bf16[1936,128]{1,0:T(8,128)(2,1)S(1)} %shard_map.50.tiles_ref, bf16[16,128,128]{2,1,0:T(8,128)(2,1)S(1)} %copy-done), custom_call_target="tpu_custom_call" | custom-call | flops 100663296 | bytes 3276800 | tf_op jit(solution)/shard_map/pallas_call | solution.py:128
  59.7 7.2 %all-to-all-start = ((bf16[16,400,128]{2,1,0:T(8,128)(2,1)}), bf16[16,400,128]{2,1,0:T(8,128)(2,1)S(1)}, u32[]{:S(2)}, u32[]{:S(2)}) async-start(bf16[16,400,128]{2,1,0:T(8,128)(2,1)} %shard_map.51), calls=%async_computation | async-start | bytes 3276800 | tf_op jit(solution)/shard_map/all_to_all | solution.py:307
  67.7 1.9 %constant_dynamic-update-slice_fusion.5 = bf16[192,4096]{1,0:T(8,128)(2,1)} fusion(bf16[192,4096]{1,0:T(8,128)(2,1)} %constant_dynamic-update-slice_fusion.6, bf16[48,4096]{1,0:T(8,128)(2,1)} %collective-permute-done.16), kind=kLoop, calls=%fused_computation.12 | loop fusion | bytes 786432
  69.6 1.8 %constant_dynamic-update-slice_fusion.4 = bf16[192,4096]{1,0:T(8,128)(2,1)} fusion(bf16[192,4096]{1,0:T(8,128)(2,1)} %constant_dynamic-update-slice_fusion.5, bf16[48,4096]{1,0:T(8,128)(2,1)} %collective-permute-done.17), kind=kLoop, calls=%fused_computation.11 | loop fusion | bytes 786432 | tf_op jit(solution)/shard_map/concatenate | solution.py:325
  71.4 6.9 %fusion = f32[192,1280]{1,0:T(8,128)S(1)} fusion(bf16[4096,1280]{1,0:T(8,128)(2,1)} %param.5, bf16[192,4096]{1,0:T(8,128)(2,1)} %constant_dynamic-update-slice_fusion.4, bf16[192,4096]{1,0:T(8,128)(2,1)S(1)} %copy-done.4, pred[]{:T(512)S(6)} %eq.3), kind=kOutput, calls=%fused_computation | convolution fusion | flops 2014052352 | bytes 14614529 | tf_op jit(solution)/shard_map/dot_general | solution.py:303
  78.4 2.5 %fusion.2.refs_0_.refs_2_ = f32[192,1280]{1,0:T(8,128)S(1)} fusion(bf16[4096,1280]{1,0:T(8,128)(2,1)S(1)} %bitcast.13, bf16[192,4096]{1,0:T(8,128)(2,1)S(1)} %copy-done.4, bf16[192,4096]{1,0:T(8,128)(2,1)S(1)} %copy-done.2, pred[]{:T(512)S(6)} %eq.3), kind=kOutput, calls=%fused_computation.2 | convolution fusion | flops 2014052352 | bytes 14614529 | tf_op jit(solution)/shard_map/dot_general | solution.py:303
  82.1 4.4 %shard_map.53 = (bf16[400,128]{1,0:T(8,128)(2,1)S(1)}, bf16[400,128]{1,0:T(8,128)(2,1)S(1)}, bf16[400,128]{1,0:T(8,128)(2,1)S(1)}, bf16[400,128]{1,0:T(8,128)(2,...) custom-call(s32[1]{0:T(128)} %bitcast.me_ref, ...), custom_call_target="tpu_custom_call" | custom-call | tf_op jit(solution)/shard_map/pallas_call | solution.py:178
  88.4 1.6 %collective-permute-start.21 = (bf16[400,128]{1,0:T(8,128)(2,1)S(1)}, bf16[400,128]{1,0:T(8,128)(2,1)S(1)}, u32[]{:S(2)}, u32[]{:S(2)}) collective-permute-start(bf16[400,128]{1,0:T(8,128)(2,1)S(1)} %get-tuple-element.28), channel_id=1, source_target_pairs={{0,6},{2,4},{4,2},{6,0},{8,14},{10,12},{12,10},{14,8},{16,22},{18,... | collective-permute-start | bytes 307208 | tf_op jit(solution)/shard_map/ppermute | solution.py:300
  90.3 1.5 %collective-permute-start.23 = (bf16[400,128]{1,0:T(8,128)(2,1)S(1)}, bf16[400,128]{1,0:T(8,128)(2,1)S(1)}, u32[]{:S(2)}, u32[]{:S(2)}) collective-permute-start(bf16[400,128]{1,0:T(8,128)(2,1)S(1)} %get-tuple-element.30), channel_id=1, source_target_pairs={{0,10},{2,8},{4,14},{6,12},{8,2},{10,0},{12,6},{14,4},{16,26},{18,... | collective-permute-start | bytes 307208 | tf_op jit(solution)/shard_map/ppermute | solution.py:300
  91.8 2.9 %collective-permute-done.19.refs_2_ = bf16[400,128]{1,0:T(8,128)(2,1)S(1)} collective-permute-done((bf16[400,128]{1,0:T(8,128)(2,1)S(1)}, bf16[400,128]{1,0:T(8,128)(2,1)S(1)}, u32[]{:S(2)}, u32[]{:S(2)}) %collective-permute-start.19) | collective-permute-done | bytes 102432 | tf_op jit(solution)/shard_map/ppermute | solution.py:300
  94.8 2.7 %collective-permute-done.20.refs_3_ = bf16[400,128]{1,0:T(8,128)(2,1)S(1)} collective-permute-done((bf16[400,128]{1,0:T(8,128)(2,1)S(1)}, bf16[400,128]{1,0:T(8,128)(2,1)S(1)}, u32[]{:S(2)}, u32[]{:S(2)}) %collective-permute-start.20) | collective-permute-done | bytes 102432 | tf_op jit(solution)/shard_map/ppermute | solution.py:300
  98.7 9.0 %collective-permute-start.26 = (bf16[400,128]{1,0:T(8,128)(2,1)S(1)}, bf16[400,128]{1,0:T(8,128)(2,1)S(1)}, u32[]{:S(2)}, u32[]{:S(2)}) collective-permute-start(bf16[400,128]{1,0:T(8,128)(2,1)S(1)} %get-tuple-element.33), channel_id=1, source_target_pairs={{0,16},{2,18},{4,20},{6,22},{8,24},{10,26},{12,28},{14,30},{16,0},... | collective-permute-start | bytes 307208 | tf_op jit(solution)/shard_map/ppermute | solution.py:300
  108.1 3.7 %collective-permute-start.28 = (bf16[400,128]{1,0:T(8,128)(2,1)S(1)}, bf16[400,128]{1,0:T(8,128)(2,1)S(1)}, u32[]{:S(2)}, u32[]{:S(2)}) collective-permute-start(bf16[400,128]{1,0:T(8,128)(2,1)S(1)} %get-tuple-element.35), channel_id=1, source_target_pairs={{0,20},{2,22},{4,16},{6,18},{8,28},{10,30},{12,24},{14,26},{16,4},... | collective-permute-start | bytes 307208 | tf_op jit(solution)/shard_map/ppermute | solution.py:300
  112.4 4.3 %collective-permute-start.30 = (bf16[400,128]{1,0:T(8,128)(2,1)}, bf16[400,128]{1,0:T(8,128)(2,1)S(1)}, u32[]{:S(2)}, u32[]{:S(2)}) collective-permute-start(bf16[400,128]{1,0:T(8,128)(2,1)} %get-tuple-element.37), channel_id=1, source_target_pairs={{0,24},{2,26},{4,28},{6,30},{8,16},{10,18},{12,20},{14,22},{16,8},... | collective-permute-start | bytes 307208 | tf_op jit(solution)/shard_map/ppermute | solution.py:300
  116.7 6.4 %collective-permute-done.26.refs_9_ = bf16[400,128]{1,0:T(8,128)(2,1)S(1)} collective-permute-done((bf16[400,128]{1,0:T(8,128)(2,1)S(1)}, bf16[400,128]{1,0:T(8,128)(2,1)S(1)}, u32[]{:S(2)}, u32[]{:S(2)}) %collective-permute-start.26) | collective-permute-done | bytes 102432 | tf_op jit(solution)/shard_map/ppermute | solution.py:300
  127.5 2.1 %collective-permute-start.33 = (bf16[400,128]{1,0:T(8,128)(2,1)S(1)}, bf16[400,128]{1,0:T(8,128)(2,1)S(1)}, u32[]{:S(2)}, u32[]{:S(2)}) collective-permute-start(bf16[400,128]{1,0:T(8,128)(2,1)S(1)} %get-tuple-element.40), channel_id=1, source_target_pairs={{0,30},{2,28},{4,26},{6,24},{8,22},{10,20},{12,18},{14,16},{16,14}... | collective-permute-start | bytes 307208 | tf_op jit(solution)/shard_map/ppermute | solution.py:300
  129.7 4.4 %collective-permute-done.29.refs_12_ = bf16[400,128]{1,0:T(8,128)(2,1)S(1)} collective-permute-done((bf16[400,128]{1,0:T(8,128)(2,1)}, bf16[400,128]{1,0:T(8,128)(2,1)S(1)}, u32[]{:S(2)}, u32[]{:S(2)}) %collective-permute-start.29) | collective-permute-done | bytes 102432 | tf_op jit(solution)/shard_map/ppermute | solution.py:300
  134.1 3.9 %collective-permute-done.30.refs_13_ = bf16[400,128]{1,0:T(8,128)(2,1)S(1)} collective-permute-done((bf16[400,128]{1,0:T(8,128)(2,1)}, bf16[400,128]{1,0:T(8,128)(2,1)S(1)}, u32[]{:S(2)}, u32[]{:S(2)}) %collective-permute-start.30) | collective-permute-done | bytes 102432 | tf_op jit(solution)/shard_map/ppermute | solution.py:300
  138.0 2.9 %collective-permute-done.31.refs_14_ = bf16[400,128]{1,0:T(8,128)(2,1)S(1)} collective-permute-done((bf16[400,128]{1,0:T(8,128)(2,1)}, bf16[400,128]{1,0:T(8,128)(2,1)S(1)}, u32[]{:S(2)}, u32[]{:S(2)}) %collective-permute-start.31) | collective-permute-done | bytes 102432 | tf_op jit(solution)/shard_map/ppermute | solution.py:300
  140.9 2.9 %collective-permute-done.32.refs_15_ = bf16[400,128]{1,0:T(8,128)(2,1)S(1)} collective-permute-done((bf16[400,128]{1,0:T(8,128)(2,1)S(1)}, bf16[400,128]{1,0:T(8,128)(2,1)S(1)}, u32[]{:S(2)}, u32[]{:S(2)}) %collective-permute-start.32) | collective-permute-done | bytes 102432 | tf_op jit(solution)/shard_map/ppermute | solution.py:300
  143.8 2.2 %collective-permute-done.33.refs_16_ = bf16[400,128]{1,0:T(8,128)(2,1)S(1)} collective-permute-done((bf16[400,128]{1,0:T(8,128)(2,1)S(1)}, bf16[400,128]{1,0:T(8,128)(2,1)S(1)}, u32[]{:S(2)}, u32[]{:S(2)}) %collective-permute-start.33) | collective-permute-done | bytes 102432 | tf_op jit(solution)/shard_map/ppermute | solution.py:300
  146.0 6.8 %shard_map.54 = f32[384,1536]{1,0:T(8,128)} custom-call(s32[2]{0:T(128)S(1)} %pad_add_fusion.me_ref, bf16[16,400,128]{2,1,0:T(8,128)(2,1)S(1)} %all-to-all-done.refs_0_, bf16[400,128]{1,0:T(8,128)(2,1)S(1)} %get-tuple-element.25.refs_1_, bf16[400,128]{1,0:T(8,128)(2,1)S(1)} %collective-permute-done.19.refs_2_, ...), custom_call_target="tpu_custom_call" | custom-call | flops 3145728 | bytes 2359296 | tf_op jit(solution)/shard_map/pallas_call | solution.py:242
  (88 shorter events, 32.2 us)
Async XLA Ops:
  0.0 11.1 %collective-permute-start.3 = (bf16[48,4096]{1,0:T(8,128)(2,1)}, bf16[48,4096]{1,0:T(8,128)(2,1)S(1)}, u32[]{:S(2)}, u32[]{:S(2)}) collective-permute-start(bf16[48,4096]{1,0:T(8,128)(2,1)} %x_ref.1), channel_id=1, source_target_pairs={{0,2},{2,0},{4,6},{6,4},{8,10},{10,8},{12,14},{14,12},{16,18},{18,... | collective-permute-start | bytes 1179656 | tf_op jit(solution)/shard_map/ppermute | solution.py:300
  0.5 19.3 %collective-permute-start = (bf16[48,4096]{1,0:T(8,128)(2,1)}, bf16[48,4096]{1,0:T(8,128)(2,1)S(1)}, u32[]{:S(2)}, u32[]{:S(2)}) collective-permute-start(bf16[48,4096]{1,0:T(8,128)(2,1)} %x_ref.1), channel_id=1, source_target_pairs={{0,16},{2,18},{4,20},{6,22},{8,24},{10,26},{12,28},{14,30},{16,0},... | collective-permute-start | bytes 1179656 | tf_op jit(solution)/shard_map/ppermute | solution.py:300
  3.1 22.1 %collective-permute-start.4 = (bf16[48,4096]{1,0:T(8,128)(2,1)}, bf16[48,4096]{1,0:T(8,128)(2,1)S(1)}, u32[]{:S(2)}, u32[]{:S(2)}) collective-permute-start(bf16[48,4096]{1,0:T(8,128)(2,1)} %x_ref.1), channel_id=1, source_target_pairs={{0,4},{2,6},{4,0},{6,2},{8,12},{10,14},{12,8},{14,10},{16,20},{18,... | collective-permute-start | bytes 1179656 | tf_op jit(solution)/shard_map/ppermute | solution.py:300
  11.1 14.9 %collective-permute-start.5 = (bf16[48,4096]{1,0:T(8,128)(2,1)S(1)}, bf16[48,4096]{1,0:T(8,128)(2,1)S(1)}, u32[]{:S(2)}, u32[]{:S(2)}) collective-permute-start(bf16[48,4096]{1,0:T(8,128)(2,1)S(1)} %collective-permute-done.3.refs_1_), channel_id=1, source_target_pairs={{0,4},{2,6},{4,0},{6,2},{8,12},{10,14},{12,8},{14,10},{16,20},{18,... | collective-permute-start | bytes 1179656 | tf_op jit(solution)/shard_map/ppermute | solution.py:300
  20.9 14.5 %collective-permute-start.8 = (bf16[48,4096]{1,0:T(8,128)(2,1)S(1)}, bf16[48,4096]{1,0:T(8,128)(2,1)S(1)}, u32[]{:S(2)}, u32[]{:S(2)}) collective-permute-start(bf16[48,4096]{1,0:T(8,128)(2,1)S(1)} %shard_map.48), channel_id=1, source_target_pairs={{0,8},{2,10},{4,12},{6,14},{8,0},{10,2},{12,4},{14,6},{16,24},{18,... | collective-permute-start | bytes 1179656 | tf_op jit(solution)/shard_map/ppermute | solution.py:300
  22.2 11.6 %collective-permute-start.1 = (bf16[48,4096]{1,0:T(8,128)(2,1)S(1)}, bf16[48,4096]{1,0:T(8,128)(2,1)S(1)}, u32[]{:S(2)}, u32[]{:S(2)}) collective-permute-start(bf16[48,4096]{1,0:T(8,128)(2,1)S(1)} %collective-permute-done.earlier_ref.refs_0_), channel_id=1, source_target_pairs={{0,2},{2,0},{4,6},{6,4},{8,10},{10,8},{12,14},{14,12},{16,18},{18,... | collective-permute-start | bytes 1179656 | tf_op jit(solution)/shard_map/ppermute | solution.py:300
  23.7 10.1 %collective-permute-start.2 = (bf16[48,4096]{1,0:T(8,128)(2,1)S(1)}, bf16[48,4096]{1,0:T(8,128)(2,1)S(1)}, u32[]{:S(2)}, u32[]{:S(2)}) collective-permute-start(bf16[48,4096]{1,0:T(8,128)(2,1)S(1)} %collective-permute-done.earlier_ref.refs_0_), channel_id=1, source_target_pairs={{0,4},{2,6},{4,0},{6,2},{8,12},{10,14},{12,8},{14,10},{16,20},{18,... | collective-permute-start | bytes 1179656 | tf_op jit(solution)/shard_map/ppermute | solution.py:300
  25.2 15.2 %collective-permute-start.9 = (bf16[48,4096]{1,0:T(8,128)(2,1)S(1)}, bf16[48,4096]{1,0:T(8,128)(2,1)S(1)}, u32[]{:S(2)}, u32[]{:S(2)}) collective-permute-start(bf16[48,4096]{1,0:T(8,128)(2,1)S(1)} %collective-permute-done.earlier_ref.refs_0_), channel_id=1, source_target_pairs={{0,8},{2,10},{4,12},{6,14},{8,0},{10,2},{12,4},{14,6},{16,24},{18,... | collective-permute-start | bytes 1179656 | tf_op jit(solution)/shard_map/ppermute | solution.py:300
  32.4 23.1 %collective-permute-start.11 = (f32[192,1280]{1,0:T(8,128)S(1)}, f32[192,1280]{1,0:T(8,128)S(1)}, u32[]{:S(2)}, u32[]{:S(2)}) collective-permute-start(f32[192,1280]{1,0:T(8,128)S(1)} %fusion.6.refs_0_.refs_2_), channel_id=1, source_target_pairs={{1,0},{3,2},{5,4},{7,6},{9,8},{11,10},{13,12},{15,14},{16,17},{18,... | collective-permute-start | bytes 2949128 | tf_op jit(solution)/shard_map/ppermute | solution.py:322
  33.8 8.9 %collective-permute-start.6 = (bf16[48,2048]{1,0:T(8,128)(2,1)S(1)}, bf16[48,2048]{1,0:T(8,128)(2,1)S(1)}, u32[]{:S(2)}, u32[]{:S(2)}) collective-permute-start(bf16[48,2048]{1,0:T(8,128)(2,1)S(1)} %get-tuple-element.23), channel_id=1, source_target_pairs={{0,4},{2,6},{4,0},{6,2},{8,12},{10,14},{12,8},{14,10},{16,20},{18,... | collective-permute-start | bytes 589832 | tf_op jit(solution)/shard_map/ppermute | solution.py:300
  35.4 15.6 %collective-permute-start.12 = (bf16[48,4096]{1,0:T(8,128)(2,1)S(1)}, bf16[48,4096]{1,0:T(8,128)(2,1)S(1)}, u32[]{:S(2)}, u32[]{:S(2)}) collective-permute-start(bf16[48,4096]{1,0:T(8,128)(2,1)S(1)} %collective-permute-done.8.refs_5_), channel_id=1, source_target_pairs={{0,2},{2,0},{4,6},{6,4},{8,10},{10,8},{12,14},{14,12},{16,18},{18,... | collective-permute-start | bytes 1179656 | tf_op jit(solution)/shard_map/ppermute | solution.py:300
  40.4 12.0 %collective-permute-start.13 = (bf16[48,4096]{1,0:T(8,128)(2,1)S(1)}, bf16[48,4096]{1,0:T(8,128)(2,1)S(1)}, u32[]{:S(2)}, u32[]{:S(2)}) collective-permute-start(bf16[48,4096]{1,0:T(8,128)(2,1)S(1)} %collective-permute-done.8.refs_5_), channel_id=1, source_target_pairs={{0,4},{2,6},{4,0},{6,2},{8,12},{10,14},{12,8},{14,10},{16,20},{18,... | collective-permute-start | bytes 1179656 | tf_op jit(solution)/shard_map/ppermute | solution.py:300
  42.7 11.5 %collective-permute-start.14 = (bf16[48,4096]{1,0:T(8,128)(2,1)S(1)}, bf16[48,4096]{1,0:T(8,128)(2,1)S(1)}, u32[]{:S(2)}, u32[]{:S(2)}) collective-permute-start(bf16[48,4096]{1,0:T(8,128)(2,1)S(1)} %collective-permute-done.5.refs_3_), channel_id=1, source_target_pairs={{0,8},{2,10},{4,12},{6,14},{8,0},{10,2},{12,4},{14,6},{16,24},{18,... | collective-permute-start | bytes 1179656 | tf_op jit(solution)/shard_map/ppermute | solution.py:300
  43.0 23.9 %collective-permute-start.15 = (bf16[48,4096]{1,0:T(8,128)(2,1)S(1)}, bf16[48,4096]{1,0:T(8,128)(2,1)S(1)}, u32[]{:S(2)}, u32[]{:S(2)}) collective-permute-start(bf16[48,4096]{1,0:T(8,128)(2,1)S(1)} %collective-permute-done.9.refs_6_), channel_id=1, source_target_pairs={{0,2},{2,0},{4,6},{6,4},{8,10},{10,8},{12,14},{14,12},{16,18},{18,... | collective-permute-start | bytes 1179656 | tf_op jit(solution)/shard_map/ppermute | solution.py:300
  52.5 15.3 %collective-permute-start.16 = (bf16[48,4096]{1,0:T(8,128)(2,1)S(1)}, bf16[48,4096]{1,0:T(8,128)(2,1)}, u32[]{:S(2)}, u32[]{:S(2)}) collective-permute-start(bf16[48,4096]{1,0:T(8,128)(2,1)S(1)} %collective-permute-done.9.refs_6_), channel_id=1, source_target_pairs={{0,4},{2,6},{4,0},{6,2},{8,12},{10,14},{12,8},{14,10},{16,20},{18,... | collective-permute-start | bytes 1179656 | tf_op jit(solution)/shard_map/ppermute | solution.py:300
  54.2 15.4 %collective-permute-start.17 = (bf16[48,4096]{1,0:T(8,128)(2,1)S(1)}, bf16[48,4096]{1,0:T(8,128)(2,1)}, u32[]{:S(2)}, u32[]{:S(2)}) collective-permute-start(bf16[48,4096]{1,0:T(8,128)(2,1)S(1)} %pad_maximum_fusion), channel_id=1, source_target_pairs={{0,8},{2,10},{4,12},{6,14},{8,0},{10,2},{12,4},{14,6},{16,24},{18,... | collective-permute-start | bytes 1179656 | tf_op jit(solution)/shard_map/ppermute | solution.py:300
  59.7 86.3 %all-to-all-start = ((bf16[16,400,128]{2,1,0:T(8,128)(2,1)}), bf16[16,400,128]{2,1,0:T(8,128)(2,1)S(1)}, u32[]{:S(2)}, u32[]{:S(2)}) async-start(bf16[16,400,128]{2,1,0:T(8,128)(2,1)} %shard_map.51), calls=%async_computation | async-start | bytes 3276800 | tf_op jit(solution)/shard_map/all_to_all | solution.py:307
  86.5 8.3 %collective-permute-start.19 = (bf16[400,128]{1,0:T(8,128)(2,1)S(1)}, bf16[400,128]{1,0:T(8,128)(2,1)S(1)}, u32[]{:S(2)}, u32[]{:S(2)}) collective-permute-start(bf16[400,128]{1,0:T(8,128)(2,1)S(1)} %get-tuple-element.26), channel_id=1, source_target_pairs={{0,2},{2,0},{4,6},{6,4},{8,10},{10,8},{12,14},{14,12},{16,18},{18,... | collective-permute-start | bytes 307208 | tf_op jit(solution)/shard_map/ppermute | solution.py:300
  86.9 10.6 %collective-permute-start.20 = (bf16[400,128]{1,0:T(8,128)(2,1)S(1)}, bf16[400,128]{1,0:T(8,128)(2,1)S(1)}, u32[]{:S(2)}, u32[]{:S(2)}) collective-permute-start(bf16[400,128]{1,0:T(8,128)(2,1)S(1)} %get-tuple-element.27), channel_id=1, source_target_pairs={{0,4},{2,6},{4,0},{6,2},{8,12},{10,14},{12,8},{14,10},{16,20},{18,... | collective-permute-start | bytes 307208 | tf_op jit(solution)/shard_map/ppermute | solution.py:300
  88.4 10.3 %collective-permute-start.21 = (bf16[400,128]{1,0:T(8,128)(2,1)S(1)}, bf16[400,128]{1,0:T(8,128)(2,1)S(1)}, u32[]{:S(2)}, u32[]{:S(2)}) collective-permute-start(bf16[400,128]{1,0:T(8,128)(2,1)S(1)} %get-tuple-element.28), channel_id=1, source_target_pairs={{0,6},{2,4},{4,2},{6,0},{8,14},{10,12},{12,10},{14,8},{16,22},{18,... | collective-permute-start | bytes 307208 | tf_op jit(solution)/shard_map/ppermute | solution.py:300
  90.0 17.7 %collective-permute-start.22 = (bf16[400,128]{1,0:T(8,128)(2,1)S(1)}, bf16[400,128]{1,0:T(8,128)(2,1)S(1)}, u32[]{:S(2)}, u32[]{:S(2)}) collective-permute-start(bf16[400,128]{1,0:T(8,128)(2,1)S(1)} %get-tuple-element.29), channel_id=1, source_target_pairs={{0,8},{2,10},{4,12},{6,14},{8,0},{10,2},{12,4},{14,6},{16,24},{18,... | collective-permute-start | bytes 307208 | tf_op jit(solution)/shard_map/ppermute | solution.py:300
  90.3 17.8 %collective-permute-start.23 = (bf16[400,128]{1,0:T(8,128)(2,1)S(1)}, bf16[400,128]{1,0:T(8,128)(2,1)S(1)}, u32[]{:S(2)}, u32[]{:S(2)}) collective-permute-start(bf16[400,128]{1,0:T(8,128)(2,1)S(1)} %get-tuple-element.30), channel_id=1, source_target_pairs={{0,10},{2,8},{4,14},{6,12},{8,2},{10,0},{12,6},{14,4},{16,26},{18,... | collective-permute-start | bytes 307208 | tf_op jit(solution)/shard_map/ppermute | solution.py:300
  94.8 17.0 %collective-permute-start.24 = (bf16[400,128]{1,0:T(8,128)(2,1)S(1)}, bf16[400,128]{1,0:T(8,128)(2,1)S(1)}, u32[]{:S(2)}, u32[]{:S(2)}) collective-permute-start(bf16[400,128]{1,0:T(8,128)(2,1)S(1)} %get-tuple-element.31), channel_id=1, source_target_pairs={{0,12},{2,14},{4,8},{6,10},{8,4},{10,6},{12,0},{14,2},{16,28},{18,... | collective-permute-start | bytes 307208 | tf_op jit(solution)/shard_map/ppermute | solution.py:300
  97.5 15.0 %collective-permute-start.25 = (bf16[400,128]{1,0:T(8,128)(2,1)S(1)}, bf16[400,128]{1,0:T(8,128)(2,1)S(1)}, u32[]{:S(2)}, u32[]{:S(2)}) collective-permute-start(bf16[400,128]{1,0:T(8,128)(2,1)S(1)} %get-tuple-element.32), channel_id=1, source_target_pairs={{0,14},{2,12},{4,10},{6,8},{8,6},{10,4},{12,2},{14,0},{16,30},{18,... | collective-permute-start | bytes 307208 | tf_op jit(solution)/shard_map/ppermute | solution.py:300
  98.7 24.5 %collective-permute-start.26 = (bf16[400,128]{1,0:T(8,128)(2,1)S(1)}, bf16[400,128]{1,0:T(8,128)(2,1)S(1)}, u32[]{:S(2)}, u32[]{:S(2)}) collective-permute-start(bf16[400,128]{1,0:T(8,128)(2,1)S(1)} %get-tuple-element.33), channel_id=1, source_target_pairs={{0,16},{2,18},{4,20},{6,22},{8,24},{10,26},{12,28},{14,30},{16,0},... | collective-permute-start | bytes 307208 | tf_op jit(solution)/shard_map/ppermute | solution.py:300
  107.7 17.6 %collective-permute-start.27 = (bf16[400,128]{1,0:T(8,128)(2,1)S(1)}, bf16[400,128]{1,0:T(8,128)(2,1)S(1)}, u32[]{:S(2)}, u32[]{:S(2)}) collective-permute-start(bf16[400,128]{1,0:T(8,128)(2,1)S(1)} %get-tuple-element.34), channel_id=1, source_target_pairs={{0,18},{2,16},{4,22},{6,20},{8,26},{10,24},{12,30},{14,28},{16,2},... | collective-permute-start | bytes 307208 | tf_op jit(solution)/shard_map/ppermute | solution.py:300
  108.1 19.4 %collective-permute-start.28 = (bf16[400,128]{1,0:T(8,128)(2,1)S(1)}, bf16[400,128]{1,0:T(8,128)(2,1)S(1)}, u32[]{:S(2)}, u32[]{:S(2)}) collective-permute-start(bf16[400,128]{1,0:T(8,128)(2,1)S(1)} %get-tuple-element.35), channel_id=1, source_target_pairs={{0,20},{2,22},{4,16},{6,18},{8,28},{10,30},{12,24},{14,26},{16,4},... | collective-permute-start | bytes 307208 | tf_op jit(solution)/shard_map/ppermute | solution.py:300
  111.8 22.2 %collective-permute-start.29 = (bf16[400,128]{1,0:T(8,128)(2,1)}, bf16[400,128]{1,0:T(8,128)(2,1)S(1)}, u32[]{:S(2)}, u32[]{:S(2)}) collective-permute-start(bf16[400,128]{1,0:T(8,128)(2,1)} %get-tuple-element.36), channel_id=1, source_target_pairs={{0,22},{2,20},{4,18},{6,16},{8,30},{10,28},{12,26},{14,24},{16,6},... | collective-permute-start | bytes 307208 | tf_op jit(solution)/shard_map/ppermute | solution.py:300
  112.4 25.6 %collective-permute-start.30 = (bf16[400,128]{1,0:T(8,128)(2,1)}, bf16[400,128]{1,0:T(8,128)(2,1)S(1)}, u32[]{:S(2)}, u32[]{:S(2)}) collective-permute-start(bf16[400,128]{1,0:T(8,128)(2,1)} %get-tuple-element.37), channel_id=1, source_target_pairs={{0,24},{2,26},{4,28},{6,30},{8,16},{10,18},{12,20},{14,22},{16,8},... | collective-permute-start | bytes 307208 | tf_op jit(solution)/shard_map/ppermute | solution.py:300
  123.1 17.8 %collective-permute-start.31 = (bf16[400,128]{1,0:T(8,128)(2,1)}, bf16[400,128]{1,0:T(8,128)(2,1)S(1)}, u32[]{:S(2)}, u32[]{:S(2)}) collective-permute-start(bf16[400,128]{1,0:T(8,128)(2,1)} %get-tuple-element.38), channel_id=1, source_target_pairs={{0,26},{2,24},{4,30},{6,28},{8,18},{10,16},{12,22},{14,20},{16,10}... | collective-permute-start | bytes 307208 | tf_op jit(solution)/shard_map/ppermute | solution.py:300
  125.3 18.4 %collective-permute-start.32 = (bf16[400,128]{1,0:T(8,128)(2,1)S(1)}, bf16[400,128]{1,0:T(8,128)(2,1)S(1)}, u32[]{:S(2)}, u32[]{:S(2)}) collective-permute-start(bf16[400,128]{1,0:T(8,128)(2,1)S(1)} %get-tuple-element.39), channel_id=1, source_target_pairs={{0,28},{2,30},{4,24},{6,26},{8,20},{10,22},{12,16},{14,18},{16,12}... | collective-permute-start | bytes 307208 | tf_op jit(solution)/shard_map/ppermute | solution.py:300
  127.5 18.5 %collective-permute-start.33 = (bf16[400,128]{1,0:T(8,128)(2,1)S(1)}, bf16[400,128]{1,0:T(8,128)(2,1)S(1)}, u32[]{:S(2)}, u32[]{:S(2)}) collective-permute-start(bf16[400,128]{1,0:T(8,128)(2,1)S(1)} %get-tuple-element.40), channel_id=1, source_target_pairs={{0,30},{2,28},{4,26},{6,24},{8,22},{10,20},{12,18},{14,16},{16,14}... | collective-permute-start | bytes 307208 | tf_op jit(solution)/shard_map/ppermute | solution.py:300
  (14 other events, 112.4 us)

commit v4 on v3

--- a/solution.py
+++ b/solution.py
@@ -186,7 +186,7 @@
 
 
 def sum_kernel(senders, place, me_ref, *refs):
-    *whole_refs, out_ref, level_ref, factor_ref, label_ref, sem = refs
+    *whole_refs, out_ref, piece_ref, mark_ref, factor_ref, label_ref, sem = refs
     me = me_ref[0]
     chunks = []
     while whole_refs:
@@ -197,40 +197,50 @@
             chunks.append(whole_refs[:senders])
             del whole_refs[:senders]
     rows = (chunks[0][0].shape[0] - STATS) // CAP
-    for s in range(senders):
-        marks = chunks[0][s][CAP * rows :, :].astype(jnp.float32)
-        level_ref[2, s : s + 1, :TILE] = marks[LABEL_ROW : LABEL_ROW + 1]
-    to_scalars = pltpu.make_async_copy(level_ref.at[2, :, :TILE], label_ref, sem)
-    to_scalars.start()
-    out_ref[...] = jnp.zeros_like(out_ref)
+    to_scalars = pltpu.make_async_copy(mark_ref, label_ref, sem)
+
+    def take(came):
+        for s in range(senders):
+            stats = came[s][CAP * rows :, :].astype(jnp.float32)
+            piece_ref[s, :, :TILE] = stats[:8]
+            piece_ref[s, :, TILE:] = stats[8:]
+
+    def three(first):
+        return piece_ref[:, first, :] + piece_ref[:, first + 1, :] + piece_ref[:, first + 2, :]
+
     for group in range(len(chunks)):
         came = [chunks[place(s, group)][s] for s in range(senders)]
-        for s in range(senders):
-            stats = came[s][CAP * rows :, :].astype(jnp.float32)
-            for half in range(2):
-                columns = pl.ds(half * TILE, TILE)
-                for kind in range(2):
-                    i = 8 * half + 3 * kind
-                    value = stats[i : i + 1] + stats[i + 1 : i + 2] + stats[i + 2 : i + 3]
-                    level_ref[kind, s : s + 1, columns] = value
-        top, total = level_ref[0, :senders, :], level_ref[1, :senders, :]
-        scale = jnp.exp(top - jnp.max(top, axis=0, keepdims=True))
-        total = jnp.sum(scale * total, axis=0, keepdims=True)
-        level_ref[0, :senders, :] = scale * (STILES_DEV * TILE * senders / total)
-        factor_ref[...] = level_ref[0].T
-        target = pl.ds(pl.multiple_of((group ^ me_ref[1]) * rows, 8), rows)
-        if group == 0:
-            to_scalars.wait()
-        for s in range(senders):
-            for r in range(CAP):
-                label = label_ref[s, r].astype(jnp.int32) - 1
-
-                @pl.when(label >= 0)
-                def _(s=s, r=r, label=label, target=target, tile_ref=came[s]):
-                    factor = factor_ref[:rows, s : s + 1]
-                    columns = pl.ds(pl.multiple_of(label * TILE, TILE), TILE)
-                    tile = tile_ref[r * rows : (r + 1) * rows, :]
-                    out_ref[target, columns] += tile.astype(jnp.float32) * factor
+
+        @pl.when(pl.program_id(0) == group)
+        def _(group=group, came=came):
+            take(came)
+            if group == 0:
+                mark_ref[...] = piece_ref[:, LABEL_ROW, :TILE]
+                to_scalars.start()
+            out_ref[...] = jnp.zeros_like(out_ref)
+            top, total = three(0), three(3)
+            scale = jnp.exp(top - jnp.max(top, axis=0, keepdims=True))
+            total = jnp.sum(scale * total, axis=0, keepdims=True)
+            scale *= STILES_DEV * TILE * senders / total
+            rest = jnp.zeros((TILE - senders, scale.shape[1]), jnp.float32)
+            factor_ref[...] = jnp.concatenate([scale, rest]).T
+            if group == 0:
+                to_scalars.wait()
+            for s in range(senders):
+                add_slots(label_ref, s, 0, came[s], rows, lambda s=s: factor_ref[:rows, s : s + 1], out_ref)
+
+
+def add_slots(label_ref, s, r, tile_ref, rows, factor, out_ref):
+    label = label_ref[s, r].astype(jnp.int32) - 1
+
+    @pl.when(label >= 0)
+    def _():
+        scale = jnp.broadcast_to(factor(), (rows, TILE))
+        columns = pl.ds(pl.multiple_of(label * TILE, TILE), TILE)
+        tile = tile_ref[r * rows : (r + 1) * rows, :].astype(jnp.float32)
+        out_ref[:, columns] += tile * scale
+        if r + 1 < CAP:
+            add_slots(label_ref, s, r + 1, tile_ref, rows, lambda: scale, out_ref)
 
 
 def sum_slots(me, senders, received, place):
@@ -239,17 +249,23 @@
     arrays = []
     for one in received:
         arrays += one if isinstance(one, list) else [one]
+    whole = pl.BlockSpec(memory_space=pltpu.VMEM)
     return pl.pallas_call(
         functools.partial(sum_kernel, senders, place),
         out_shape=jax.ShapeDtypeStruct((rows * chunks, STILES_DEV * TILE), jnp.float32),
-        in_specs=[SMEM] + [VMEM] * len(arrays),
-        out_specs=VMEM,
-        scratch_shapes=[
-            pltpu.VMEM((3, TILE, 2 * TILE), jnp.float32),
-            pltpu.VMEM((2 * TILE, TILE), jnp.float32),
-            pltpu.SMEM((TILE, TILE), jnp.float32),
-            pltpu.SemaphoreType.DMA,
-        ],
+        grid_spec=pltpu.PrefetchScalarGridSpec(
+            num_scalar_prefetch=1,
+            grid=(chunks,),
+            in_specs=[whole] * len(arrays),
+            out_specs=pl.BlockSpec((rows, STILES_DEV * TILE), lambda group, me: (group ^ me[1], 0)),
+            scratch_shapes=[
+                pltpu.VMEM((senders, 8, 2 * TILE), jnp.float32),
+                pltpu.VMEM((senders, TILE), jnp.float32),
+                pltpu.VMEM((2 * TILE, TILE), jnp.float32),
+                pltpu.SMEM((senders, TILE), jnp.float32),
+                pltpu.SemaphoreType.DMA,
+            ],
+        ),
         compiler_params=kernel_params(40),
         cost_estimate=pl.CostEstimate(
             flops=2 * senders * chunks * CAP * rows * TILE,
@@ -310,7 +326,7 @@
         zero = hidden_states
         two = swap(zero, 8)
         zero_x, zero_y = swap(zero, 1), swap(zero, 2)
-        zero_d = swap(zero_x, 2)
+        zero_d = swap(zero_y, 1)
         two_x, two_y = swap(two, 1), swap(two, 2)
         to_near = [(2 * v + 1 - (v >> 3), 2 * v + (v >> 3)) for v in range(vocab)]
         to_away = [(b, a) for a, b in to_near]

time: 154 us -> 151 us (0.981)
  starting transfers between devices: 59.7 us -> 55.6 us
  waiting for transfers between devices: 50.7 us -> 54.2 us
  Pallas kernels: 15.6 us -> 13.1 us
    ppermute x31, starting transfers between devices: 49.8 us -> 45.3 us  [swap(): return lax.ppermute(x, 'vocab', [(i, i ^ k) for i in range(vocab)])]
    ppermute x31, waiting for transfers between devices: 50.7 us -> 54.2 us  [swap(): return lax.ppermute(x, 'vocab', [(i, i ^ k) for i in range(vocab)])]
    pallas_call x1, Pallas kernels: 6.8 us -> 4.55 us  [sum_slots(): pl.pallas_call(functools.partial(sum_kernel, senders, place), out_shape=j...]
  transfers between devices with their start and end apart: 35 -> 35, of which waited for: 14 -> 16; matrix products, arithmetic and copies ran while one was open for 16% -> 16% of each run, Pallas kernels for 6% -> 6%
where the time goes in v4:
time: 151 us; the launch traced here: 150 us
  starting transfers between devices  55.6 us (37%)
  waiting for transfers between devices  54.2 us (36%)
  matrix products  18 us (12%)
  Pallas kernels  13.1 us (9%)
  local copies, waits for them, and re-layouts  8.37 us (6%)
    ppermute x31, waiting for transfers between devices, swap(): return lax.ppermute(x, 'vocab', [(i, i ^ k) for i in range(vocab)])  54.2 us
    ppermute x31, starting transfers between devices, swap(): return lax.ppermute(x, 'vocab', [(i, i ^ k) for i in range(vocab)])  45.3 us
    dot_general x4, matrix products, dot(): return jnp.dot(x, head_weight, preferred_element_type=jnp.float32)  18 us
    all_to_all x1, starting transfers between devices, exchange(): lax.all_to_all(sent, 'vocab', split_axis=0, concat_axis=0, tiled=True)  6.96 us
    unnamed x29, local copies, waits for them, and re-layouts  6.48 us
    pallas_call x1, Pallas kernels, sum_slots(): pl.pallas_call(functools.partial(sum_kernel, senders, place), out_shape=j...  4.55 us
    pallas_call x1, Pallas kernels, focus_each(): pl.pallas_call(functools.partial(focus_each_kernel, rows), out_shape=[jax...  4.13 us
    ppermute x2, starting transfers between devices, product(): return (logits, lax.ppermute(logits, ('vocab', 'hid'), pairs))  3.24 us
  transfers between devices with their start and end apart: 35, of which 16 were waited for; matrix products, arithmetic and copies ran while one was open for 16% of the time, Pallas kernels for 6%

profile of v4, /device:TPU:10, one launch (start us, length us, event | category | flops | bytes accessed | tf_op | source)
XLA Modules:
  0.0 149.8 jit_solution(15056599869655745288)
XLA Ops:
  0.0 1.5 %collective-permute-start.4 = (bf16[48,4096]{1,0:T(8,128)(2,1)}, bf16[48,4096]{1,0:T(8,128)(2,1)S(1)}, u32[]{:S(2)}, u32[]{:S(2)}) collective-permute-start(bf16[48,4096]{1,0:T(8,128)(2,1)} %x_ref.1), channel_id=1, source_target_pairs={{0,4},{2,6},{4,0},{6,2},{8,12},{10,14},{12,8},{14,10},{16,20},{18,... | collective-permute-start | bytes 1179656 | tf_op jit(solution)/shard_map/ppermute | solution.py:316
  1.5 2.6 %collective-permute-start = (bf16[48,4096]{1,0:T(8,128)(2,1)}, bf16[48,4096]{1,0:T(8,128)(2,1)S(1)}, u32[]{:S(2)}, u32[]{:S(2)}) collective-permute-start(bf16[48,4096]{1,0:T(8,128)(2,1)} %x_ref.1), channel_id=1, source_target_pairs={{0,16},{2,18},{4,20},{6,22},{8,24},{10,26},{12,28},{14,30},{16,0},... | collective-permute-start | bytes 1179656 | tf_op jit(solution)/shard_map/ppermute | solution.py:316
  4.6 6.4 %collective-permute-done.4.refs_2_ = bf16[48,4096]{1,0:T(8,128)(2,1)S(1)} collective-permute-done((bf16[48,4096]{1,0:T(8,128)(2,1)}, bf16[48,4096]{1,0:T(8,128)(2,1)S(1)}, u32[]{:S(2)}, u32[]{:S(2)}) %collective-permute-start.4) | collective-permute-done | bytes 393248 | tf_op jit(solution)/shard_map/ppermute | solution.py:316
  12.5 8.3 %collective-permute-done.earlier_ref.refs_0_ = bf16[48,4096]{1,0:T(8,128)(2,1)S(1)} collective-permute-done((bf16[48,4096]{1,0:T(8,128)(2,1)}, bf16[48,4096]{1,0:T(8,128)(2,1)S(1)}, u32[]{:S(2)}, u32[]{:S(2)}) %collective-permute-start) | collective-permute-done | bytes 393248 | tf_op jit(solution)/shard_map/ppermute | solution.py:316
  25.1 6.3 %fusion.6.refs_0_.refs_2_ = f32[192,1280]{1,0:T(8,128)S(1)} fusion(bf16[192,4096]{1,0:T(8,128)(2,1)S(1)} %shard_map.46, bf16[4096,1280]{1,0:T(8,128)(2,1)} %param.5), kind=kOutput, calls=%fused_computation.17 | convolution fusion | flops 2013265920 | bytes 13041664 | tf_op jit(solution)/shard_map/dot_general | solution.py:319
  36.5 4.9 %collective-permute-done.9.refs_6_ = bf16[48,4096]{1,0:T(8,128)(2,1)S(1)} collective-permute-done((bf16[48,4096]{1,0:T(8,128)(2,1)S(1)}, bf16[48,4096]{1,0:T(8,128)(2,1)S(1)}, u32[]{:S(2)}, u32[]{:S(2)}) %collective-permute-start.9) | collective-permute-done | bytes 393248 | tf_op jit(solution)/shard_map/ppermute | solution.py:316
  44.1 2.3 %fusion.7.refs_0_ = f32[192,1280]{1,0:T(8,128)S(1)} fusion(bf16[192,4096]{1,0:T(8,128)(2,1)S(1)} %shard_map.49, bf16[4096,1280]{1,0:T(8,128)(2,1)S(1)} %bitcast.11), kind=kOutput, calls=%fused_computation.18 | convolution fusion | flops 2013265920 | bytes 13041664 | tf_op jit(solution)/shard_map/dot_general | solution.py:319
  46.5 4.1 %collective-permute-done.12 = bf16[48,4096]{1,0:T(8,128)(2,1)S(1)} collective-permute-done((bf16[48,4096]{1,0:T(8,128)(2,1)S(1)}, bf16[48,4096]{1,0:T(8,128)(2,1)S(1)}, u32[]{:S(2)}, u32[]{:S(2)}) %collective-permute-start.12) | collective-permute-done | bytes 393248 | tf_op jit(solution)/shard_map/ppermute | solution.py:316
  50.6 1.9 %collective-permute-start.10 = (f32[192,1280]{1,0:T(8,128)S(1)}, f32[192,1280]{1,0:T(8,128)S(1)}, u32[]{:S(2)}, u32[]{:S(2)}) collective-permute-start(f32[192,1280]{1,0:T(8,128)S(1)} %fusion.7.refs_0_), channel_id=1, source_target_pairs={{0,1},{2,3},{4,5},{6,7},{8,9},{10,11},{12,13},{14,15},{17,16},{19,... | collective-permute-start | bytes 2949128 | tf_op jit(solution)/shard_map/ppermute | solution.py:338
  53.1 1.8 %collective-permute-start.17 = (bf16[48,4096]{1,0:T(8,128)(2,1)S(1)}, bf16[48,4096]{1,0:T(8,128)(2,1)}, u32[]{:S(2)}, u32[]{:S(2)}) collective-permute-start(bf16[48,4096]{1,0:T(8,128)(2,1)S(1)} %pad_maximum_fusion), channel_id=1, source_target_pairs={{0,8},{2,10},{4,12},{6,14},{8,0},{10,2},{12,4},{14,6},{16,24},{18,... | collective-permute-start | bytes 1179656 | tf_op jit(solution)/shard_map/ppermute | solution.py:316
  57.0 2.1 %shard_map.51 = bf16[16,400,128]{2,1,0:T(8,128)(2,1)} custom-call(s32[1]{0:T(128)} %bitcast.me_ref, s32[32]{0:T(128)S(1)} %reshape.3.pair_ref, bf16[1936,128]{1,0:T(8,128)(2,1)S(1)} %shard_map.50.tiles_ref, bf16[16,128,128]{2,1,0:T(8,128)(2,1)S(1)} %copy-done), custom_call_target="tpu_custom_call" | custom-call | flops 100663296 | bytes 3276800 | tf_op jit(solution)/shard_map/pallas_call | solution.py:128
  59.1 7.0 %all-to-all-start = ((bf16[16,400,128]{2,1,0:T(8,128)(2,1)}), bf16[16,400,128]{2,1,0:T(8,128)(2,1)S(1)}, u32[]{:S(2)}, u32[]{:S(2)}) async-start(bf16[16,400,128]{2,1,0:T(8,128)(2,1)} %shard_map.51), calls=%async_computation | async-start | bytes 3276800 | tf_op jit(solution)/shard_map/all_to_all | solution.py:323
  66.8 1.9 %constant_dynamic-update-slice_fusion.5 = bf16[192,4096]{1,0:T(8,128)(2,1)} fusion(bf16[192,4096]{1,0:T(8,128)(2,1)} %constant_dynamic-update-slice_fusion.6, bf16[48,4096]{1,0:T(8,128)(2,1)} %collective-permute-done.16), kind=kLoop, calls=%fused_computation.12 | loop fusion | bytes 786432
  68.8 1.8 %constant_dynamic-update-slice_fusion.4 = bf16[192,4096]{1,0:T(8,128)(2,1)} fusion(bf16[192,4096]{1,0:T(8,128)(2,1)} %constant_dynamic-update-slice_fusion.5, bf16[48,4096]{1,0:T(8,128)(2,1)} %collective-permute-done.17), kind=kLoop, calls=%fused_computation.11 | loop fusion | bytes 786432 | tf_op jit(solution)/shard_map/concatenate | solution.py:341
  70.5 6.9 %fusion = f32[192,1280]{1,0:T(8,128)S(1)} fusion(bf16[4096,1280]{1,0:T(8,128)(2,1)} %param.5, bf16[192,4096]{1,0:T(8,128)(2,1)} %constant_dynamic-update-slice_fusion.4, bf16[192,4096]{1,0:T(8,128)(2,1)S(1)} %copy-done.4, pred[]{:T(512)S(6)} %eq.3), kind=kOutput, calls=%fused_computation | convolution fusion | flops 2014052352 | bytes 14614529 | tf_op jit(solution)/shard_map/dot_general | solution.py:319
  77.6 2.5 %fusion.2.refs_0_.refs_2_ = f32[192,1280]{1,0:T(8,128)S(1)} fusion(bf16[4096,1280]{1,0:T(8,128)(2,1)S(1)} %bitcast.13, bf16[192,4096]{1,0:T(8,128)(2,1)S(1)} %copy-done.4, bf16[192,4096]{1,0:T(8,128)(2,1)S(1)} %copy-done.2, pred[]{:T(512)S(6)} %eq.3), kind=kOutput, calls=%fused_computation.2 | convolution fusion | flops 2014052352 | bytes 14614529 | tf_op jit(solution)/shard_map/dot_general | solution.py:319
  81.2 4.1 %shard_map.53 = (bf16[400,128]{1,0:T(8,128)(2,1)S(1)}, bf16[400,128]{1,0:T(8,128)(2,1)S(1)}, bf16[400,128]{1,0:T(8,128)(2,1)S(1)}, bf16[400,128]{1,0:T(8,128)(2,...) custom-call(s32[1]{0:T(128)} %bitcast.me_ref, ...), custom_call_target="tpu_custom_call" | custom-call | tf_op jit(solution)/shard_map/pallas_call | solution.py:178
  91.1 2.8 %collective-permute-done.19.refs_2_ = bf16[400,128]{1,0:T(8,128)(2,1)S(1)} collective-permute-done((bf16[400,128]{1,0:T(8,128)(2,1)S(1)}, bf16[400,128]{1,0:T(8,128)(2,1)S(1)}, u32[]{:S(2)}, u32[]{:S(2)}) %collective-permute-start.19) | collective-permute-done | bytes 102432 | tf_op jit(solution)/shard_map/ppermute | solution.py:316
  93.9 2.7 %collective-permute-done.20.refs_3_ = bf16[400,128]{1,0:T(8,128)(2,1)S(1)} collective-permute-done((bf16[400,128]{1,0:T(8,128)(2,1)S(1)}, bf16[400,128]{1,0:T(8,128)(2,1)S(1)}, u32[]{:S(2)}, u32[]{:S(2)}) %collective-permute-start.20) | collective-permute-done | bytes 102432 | tf_op jit(solution)/shard_map/ppermute | solution.py:316
  97.8 8.9 %collective-permute-start.26 = (bf16[400,128]{1,0:T(8,128)(2,1)S(1)}, bf16[400,128]{1,0:T(8,128)(2,1)S(1)}, u32[]{:S(2)}, u32[]{:S(2)}) collective-permute-start(bf16[400,128]{1,0:T(8,128)(2,1)S(1)} %get-tuple-element.33), channel_id=1, source_target_pairs={{0,16},{2,18},{4,20},{6,22},{8,24},{10,26},{12,28},{14,30},{16,0},... | collective-permute-start | bytes 307208 | tf_op jit(solution)/shard_map/ppermute | solution.py:316
  107.1 3.8 %collective-permute-start.28 = (bf16[400,128]{1,0:T(8,128)(2,1)S(1)}, bf16[400,128]{1,0:T(8,128)(2,1)S(1)}, u32[]{:S(2)}, u32[]{:S(2)}) collective-permute-start(bf16[400,128]{1,0:T(8,128)(2,1)S(1)} %get-tuple-element.35), channel_id=1, source_target_pairs={{0,20},{2,22},{4,16},{6,18},{8,28},{10,30},{12,24},{14,26},{16,4},... | collective-permute-start | bytes 307208 | tf_op jit(solution)/shard_map/ppermute | solution.py:316
  110.9 2.6 %collective-permute-start.29 = (bf16[400,128]{1,0:T(8,128)(2,1)}, bf16[400,128]{1,0:T(8,128)(2,1)S(1)}, u32[]{:S(2)}, u32[]{:S(2)}) collective-permute-start(bf16[400,128]{1,0:T(8,128)(2,1)} %get-tuple-element.36), channel_id=1, source_target_pairs={{0,22},{2,20},{4,18},{6,16},{8,30},{10,28},{12,26},{14,24},{16,6},... | collective-permute-start | bytes 307208 | tf_op jit(solution)/shard_map/ppermute | solution.py:316
  113.5 2.3 %collective-permute-start.30 = (bf16[400,128]{1,0:T(8,128)(2,1)}, bf16[400,128]{1,0:T(8,128)(2,1)S(1)}, u32[]{:S(2)}, u32[]{:S(2)}) collective-permute-start(bf16[400,128]{1,0:T(8,128)(2,1)} %get-tuple-element.37), channel_id=1, source_target_pairs={{0,24},{2,26},{4,28},{6,30},{8,16},{10,18},{12,20},{14,22},{16,8},... | collective-permute-start | bytes 307208 | tf_op jit(solution)/shard_map/ppermute | solution.py:316
  115.9 6.3 %collective-permute-done.26.refs_9_ = bf16[400,128]{1,0:T(8,128)(2,1)S(1)} collective-permute-done((bf16[400,128]{1,0:T(8,128)(2,1)S(1)}, bf16[400,128]{1,0:T(8,128)(2,1)S(1)}, u32[]{:S(2)}, u32[]{:S(2)}) %collective-permute-start.26) | collective-permute-done | bytes 102432 | tf_op jit(solution)/shard_map/ppermute | solution.py:316
  124.3 1.6 %collective-permute-start.32 = (bf16[400,128]{1,0:T(8,128)(2,1)S(1)}, bf16[400,128]{1,0:T(8,128)(2,1)S(1)}, u32[]{:S(2)}, u32[]{:S(2)}) collective-permute-start(bf16[400,128]{1,0:T(8,128)(2,1)S(1)} %get-tuple-element.39), channel_id=1, source_target_pairs={{0,28},{2,30},{4,24},{6,26},{8,20},{10,22},{12,16},{14,18},{16,12}... | collective-permute-start | bytes 307208 | tf_op jit(solution)/shard_map/ppermute | solution.py:316
  126.5 2.2 %collective-permute-start.33 = (bf16[400,128]{1,0:T(8,128)(2,1)S(1)}, bf16[400,128]{1,0:T(8,128)(2,1)S(1)}, u32[]{:S(2)}, u32[]{:S(2)}) collective-permute-start(bf16[400,128]{1,0:T(8,128)(2,1)S(1)} %get-tuple-element.40), channel_id=1, source_target_pairs={{0,30},{2,28},{4,26},{6,24},{8,22},{10,20},{12,18},{14,16},{16,14}... | collective-permute-start | bytes 307208 | tf_op jit(solution)/shard_map/ppermute | solution.py:316
  128.8 4.3 %collective-permute-done.29.refs_12_ = bf16[400,128]{1,0:T(8,128)(2,1)S(1)} collective-permute-done((bf16[400,128]{1,0:T(8,128)(2,1)}, bf16[400,128]{1,0:T(8,128)(2,1)S(1)}, u32[]{:S(2)}, u32[]{:S(2)}) %collective-permute-start.29) | collective-permute-done | bytes 102432 | tf_op jit(solution)/shard_map/ppermute | solution.py:316
  133.1 4.0 %collective-permute-done.30.refs_13_ = bf16[400,128]{1,0:T(8,128)(2,1)S(1)} collective-permute-done((bf16[400,128]{1,0:T(8,128)(2,1)}, bf16[400,128]{1,0:T(8,128)(2,1)S(1)}, u32[]{:S(2)}, u32[]{:S(2)}) %collective-permute-start.30) | collective-permute-done | bytes 102432 | tf_op jit(solution)/shard_map/ppermute | solution.py:316
  137.1 3.0 %collective-permute-done.31.refs_14_ = bf16[400,128]{1,0:T(8,128)(2,1)S(1)} collective-permute-done((bf16[400,128]{1,0:T(8,128)(2,1)}, bf16[400,128]{1,0:T(8,128)(2,1)S(1)}, u32[]{:S(2)}, u32[]{:S(2)}) %collective-permute-start.31) | collective-permute-done | bytes 102432 | tf_op jit(solution)/shard_map/ppermute | solution.py:316
  140.1 2.8 %collective-permute-done.32.refs_15_ = bf16[400,128]{1,0:T(8,128)(2,1)S(1)} collective-permute-done((bf16[400,128]{1,0:T(8,128)(2,1)S(1)}, bf16[400,128]{1,0:T(8,128)(2,1)S(1)}, u32[]{:S(2)}, u32[]{:S(2)}) %collective-permute-start.32) | collective-permute-done | bytes 102432 | tf_op jit(solution)/shard_map/ppermute | solution.py:316
  142.8 2.3 %collective-permute-done.33.refs_16_ = bf16[400,128]{1,0:T(8,128)(2,1)S(1)} collective-permute-done((bf16[400,128]{1,0:T(8,128)(2,1)S(1)}, bf16[400,128]{1,0:T(8,128)(2,1)S(1)}, u32[]{:S(2)}, u32[]{:S(2)}) %collective-permute-start.33) | collective-permute-done | bytes 102432 | tf_op jit(solution)/shard_map/ppermute | solution.py:316
  145.1 4.6 %shard_map.54 = f32[384,1536]{1,0:T(8,128)} custom-call(s32[2]{0:T(128)S(1)} %pad_add_fusion.me_ref, bf16[16,400,128]{2,1,0:T(8,128)(2,1)S(1)} %all-to-all-done.refs_0_, bf16[400,128]{1,0:T(8,128)(2,1)S(1)} %get-tuple-element.25.refs_1_, bf16[400,128]{1,0:T(8,128)(2,1)S(1)} %collective-permute-done.19.refs_2_, ...), custom_call_target="tpu_custom_call" | custom-call | flops 3145728 | bytes 2359296 | tf_op jit(solution)/shard_map/pallas_call | solution.py:253
  (88 shorter events, 28.9 us)
Async XLA Ops:
  0.0 11.1 %collective-permute-start.4 = (bf16[48,4096]{1,0:T(8,128)(2,1)}, bf16[48,4096]{1,0:T(8,128)(2,1)S(1)}, u32[]{:S(2)}, u32[]{:S(2)}) collective-permute-start(bf16[48,4096]{1,0:T(8,128)(2,1)} %x_ref.1), channel_id=1, source_target_pairs={{0,4},{2,6},{4,0},{6,2},{8,12},{10,14},{12,8},{14,10},{16,20},{18,... | collective-permute-start | bytes 1179656 | tf_op jit(solution)/shard_map/ppermute | solution.py:316
  1.5 19.3 %collective-permute-start = (bf16[48,4096]{1,0:T(8,128)(2,1)}, bf16[48,4096]{1,0:T(8,128)(2,1)S(1)}, u32[]{:S(2)}, u32[]{:S(2)}) collective-permute-start(bf16[48,4096]{1,0:T(8,128)(2,1)} %x_ref.1), channel_id=1, source_target_pairs={{0,16},{2,18},{4,20},{6,22},{8,24},{10,26},{12,28},{14,30},{16,0},... | collective-permute-start | bytes 1179656 | tf_op jit(solution)/shard_map/ppermute | solution.py:316
  4.1 20.1 %collective-permute-start.3 = (bf16[48,4096]{1,0:T(8,128)(2,1)}, bf16[48,4096]{1,0:T(8,128)(2,1)S(1)}, u32[]{:S(2)}, u32[]{:S(2)}) collective-permute-start(bf16[48,4096]{1,0:T(8,128)(2,1)} %x_ref.1), channel_id=1, source_target_pairs={{0,2},{2,0},{4,6},{6,4},{8,10},{10,8},{12,14},{14,12},{16,18},{18,... | collective-permute-start | bytes 1179656 | tf_op jit(solution)/shard_map/ppermute | solution.py:316
  11.1 13.9 %collective-permute-start.5 = (bf16[48,4096]{1,0:T(8,128)(2,1)S(1)}, bf16[48,4096]{1,0:T(8,128)(2,1)S(1)}, u32[]{:S(2)}, u32[]{:S(2)}) collective-permute-start(bf16[48,4096]{1,0:T(8,128)(2,1)S(1)} %collective-permute-done.4.refs_2_), channel_id=1, source_target_pairs={{0,2},{2,0},{4,6},{6,4},{8,10},{10,8},{12,14},{14,12},{16,18},{18,... | collective-permute-start | bytes 1179656 | tf_op jit(solution)/shard_map/ppermute | solution.py:316
  21.9 14.0 %collective-permute-start.8 = (bf16[48,4096]{1,0:T(8,128)(2,1)S(1)}, bf16[48,4096]{1,0:T(8,128)(2,1)S(1)}, u32[]{:S(2)}, u32[]{:S(2)}) collective-permute-start(bf16[48,4096]{1,0:T(8,128)(2,1)S(1)} %shard_map.48), channel_id=1, source_target_pairs={{0,8},{2,10},{4,12},{6,14},{8,0},{10,2},{12,4},{14,6},{16,24},{18,... | collective-permute-start | bytes 1179656 | tf_op jit(solution)/shard_map/ppermute | solution.py:316
  23.2 9.8 %collective-permute-start.1 = (bf16[48,4096]{1,0:T(8,128)(2,1)S(1)}, bf16[48,4096]{1,0:T(8,128)(2,1)S(1)}, u32[]{:S(2)}, u32[]{:S(2)}) collective-permute-start(bf16[48,4096]{1,0:T(8,128)(2,1)S(1)} %collective-permute-done.earlier_ref.refs_0_), channel_id=1, source_target_pairs={{0,2},{2,0},{4,6},{6,4},{8,10},{10,8},{12,14},{14,12},{16,18},{18,... | collective-permute-start | bytes 1179656 | tf_op jit(solution)/shard_map/ppermute | solution.py:316
  23.7 9.6 %collective-permute-start.2 = (bf16[48,4096]{1,0:T(8,128)(2,1)S(1)}, bf16[48,4096]{1,0:T(8,128)(2,1)S(1)}, u32[]{:S(2)}, u32[]{:S(2)}) collective-permute-start(bf16[48,4096]{1,0:T(8,128)(2,1)S(1)} %collective-permute-done.earlier_ref.refs_0_), channel_id=1, source_target_pairs={{0,4},{2,6},{4,0},{6,2},{8,12},{10,14},{12,8},{14,10},{16,20},{18,... | collective-permute-start | bytes 1179656 | tf_op jit(solution)/shard_map/ppermute | solution.py:316
  24.2 17.2 %collective-permute-start.9 = (bf16[48,4096]{1,0:T(8,128)(2,1)S(1)}, bf16[48,4096]{1,0:T(8,128)(2,1)S(1)}, u32[]{:S(2)}, u32[]{:S(2)}) collective-permute-start(bf16[48,4096]{1,0:T(8,128)(2,1)S(1)} %collective-permute-done.earlier_ref.refs_0_), channel_id=1, source_target_pairs={{0,8},{2,10},{4,12},{6,14},{8,0},{10,2},{12,4},{14,6},{16,24},{18,... | collective-permute-start | bytes 1179656 | tf_op jit(solution)/shard_map/ppermute | solution.py:316
  31.5 23.4 %collective-permute-start.11 = (f32[192,1280]{1,0:T(8,128)S(1)}, f32[192,1280]{1,0:T(8,128)S(1)}, u32[]{:S(2)}, u32[]{:S(2)}) collective-permute-start(f32[192,1280]{1,0:T(8,128)S(1)} %fusion.6.refs_0_.refs_2_), channel_id=1, source_target_pairs={{1,0},{3,2},{5,4},{7,6},{9,8},{11,10},{13,12},{15,14},{16,17},{18,... | collective-permute-start | bytes 2949128 | tf_op jit(solution)/shard_map/ppermute | solution.py:338
  33.3 9.3 %collective-permute-start.6 = (bf16[48,2048]{1,0:T(8,128)(2,1)S(1)}, bf16[48,2048]{1,0:T(8,128)(2,1)S(1)}, u32[]{:S(2)}, u32[]{:S(2)}) collective-permute-start(bf16[48,2048]{1,0:T(8,128)(2,1)S(1)} %get-tuple-element.23), channel_id=1, source_target_pairs={{0,4},{2,6},{4,0},{6,2},{8,12},{10,14},{12,8},{14,10},{16,20},{18,... | collective-permute-start | bytes 589832 | tf_op jit(solution)/shard_map/ppermute | solution.py:316
  35.9 14.7 %collective-permute-start.12 = (bf16[48,4096]{1,0:T(8,128)(2,1)S(1)}, bf16[48,4096]{1,0:T(8,128)(2,1)S(1)}, u32[]{:S(2)}, u32[]{:S(2)}) collective-permute-start(bf16[48,4096]{1,0:T(8,128)(2,1)S(1)} %collective-permute-done.8.refs_5_), channel_id=1, source_target_pairs={{0,2},{2,0},{4,6},{6,4},{8,10},{10,8},{12,14},{14,12},{16,18},{18,... | collective-permute-start | bytes 1179656 | tf_op jit(solution)/shard_map/ppermute | solution.py:316
  41.4 11.2 %collective-permute-start.13 = (bf16[48,4096]{1,0:T(8,128)(2,1)S(1)}, bf16[48,4096]{1,0:T(8,128)(2,1)S(1)}, u32[]{:S(2)}, u32[]{:S(2)}) collective-permute-start(bf16[48,4096]{1,0:T(8,128)(2,1)S(1)} %collective-permute-done.8.refs_5_), channel_id=1, source_target_pairs={{0,4},{2,6},{4,0},{6,2},{8,12},{10,14},{12,8},{14,10},{16,20},{18,... | collective-permute-start | bytes 1179656 | tf_op jit(solution)/shard_map/ppermute | solution.py:316
  42.7 10.4 %collective-permute-start.14 = (bf16[48,4096]{1,0:T(8,128)(2,1)S(1)}, bf16[48,4096]{1,0:T(8,128)(2,1)S(1)}, u32[]{:S(2)}, u32[]{:S(2)}) collective-permute-start(bf16[48,4096]{1,0:T(8,128)(2,1)S(1)} %collective-permute-done.5.refs_3_), channel_id=1, source_target_pairs={{0,8},{2,10},{4,12},{6,14},{8,0},{10,2},{12,4},{14,6},{16,24},{18,... | collective-permute-start | bytes 1179656 | tf_op jit(solution)/shard_map/ppermute | solution.py:316
  43.0 23.1 %collective-permute-start.15 = (bf16[48,4096]{1,0:T(8,128)(2,1)S(1)}, bf16[48,4096]{1,0:T(8,128)(2,1)S(1)}, u32[]{:S(2)}, u32[]{:S(2)}) collective-permute-start(bf16[48,4096]{1,0:T(8,128)(2,1)S(1)} %collective-permute-done.9.refs_6_), channel_id=1, source_target_pairs={{0,2},{2,0},{4,6},{6,4},{8,10},{10,8},{12,14},{14,12},{16,18},{18,... | collective-permute-start | bytes 1179656 | tf_op jit(solution)/shard_map/ppermute | solution.py:316
  52.6 14.2 %collective-permute-start.16 = (bf16[48,4096]{1,0:T(8,128)(2,1)S(1)}, bf16[48,4096]{1,0:T(8,128)(2,1)}, u32[]{:S(2)}, u32[]{:S(2)}) collective-permute-start(bf16[48,4096]{1,0:T(8,128)(2,1)S(1)} %collective-permute-done.9.refs_6_), channel_id=1, source_target_pairs={{0,4},{2,6},{4,0},{6,2},{8,12},{10,14},{12,8},{14,10},{16,20},{18,... | collective-permute-start | bytes 1179656 | tf_op jit(solution)/shard_map/ppermute | solution.py:316
  53.1 15.7 %collective-permute-start.17 = (bf16[48,4096]{1,0:T(8,128)(2,1)S(1)}, bf16[48,4096]{1,0:T(8,128)(2,1)}, u32[]{:S(2)}, u32[]{:S(2)}) collective-permute-start(bf16[48,4096]{1,0:T(8,128)(2,1)S(1)} %pad_maximum_fusion), channel_id=1, source_target_pairs={{0,8},{2,10},{4,12},{6,14},{8,0},{10,2},{12,4},{14,6},{16,24},{18,... | collective-permute-start | bytes 1179656 | tf_op jit(solution)/shard_map/ppermute | solution.py:316
  59.1 86.0 %all-to-all-start = ((bf16[16,400,128]{2,1,0:T(8,128)(2,1)}), bf16[16,400,128]{2,1,0:T(8,128)(2,1)S(1)}, u32[]{:S(2)}, u32[]{:S(2)}) async-start(bf16[16,400,128]{2,1,0:T(8,128)(2,1)} %shard_map.51), calls=%async_computation | async-start | bytes 3276800 | tf_op jit(solution)/shard_map/all_to_all | solution.py:323
  85.3 8.6 %collective-permute-start.19 = (bf16[400,128]{1,0:T(8,128)(2,1)S(1)}, bf16[400,128]{1,0:T(8,128)(2,1)S(1)}, u32[]{:S(2)}, u32[]{:S(2)}) collective-permute-start(bf16[400,128]{1,0:T(8,128)(2,1)S(1)} %get-tuple-element.26), channel_id=1, source_target_pairs={{0,2},{2,0},{4,6},{6,4},{8,10},{10,8},{12,14},{14,12},{16,18},{18,... | collective-permute-start | bytes 307208 | tf_op jit(solution)/shard_map/ppermute | solution.py:316
  86.1 10.4 %collective-permute-start.20 = (bf16[400,128]{1,0:T(8,128)(2,1)S(1)}, bf16[400,128]{1,0:T(8,128)(2,1)S(1)}, u32[]{:S(2)}, u32[]{:S(2)}) collective-permute-start(bf16[400,128]{1,0:T(8,128)(2,1)S(1)} %get-tuple-element.27), channel_id=1, source_target_pairs={{0,4},{2,6},{4,0},{6,2},{8,12},{10,14},{12,8},{14,10},{16,20},{18,... | collective-permute-start | bytes 307208 | tf_op jit(solution)/shard_map/ppermute | solution.py:316
  87.5 10.3 %collective-permute-start.21 = (bf16[400,128]{1,0:T(8,128)(2,1)S(1)}, bf16[400,128]{1,0:T(8,128)(2,1)S(1)}, u32[]{:S(2)}, u32[]{:S(2)}) collective-permute-start(bf16[400,128]{1,0:T(8,128)(2,1)S(1)} %get-tuple-element.28), channel_id=1, source_target_pairs={{0,6},{2,4},{4,2},{6,0},{8,14},{10,12},{12,10},{14,8},{16,22},{18,... | collective-permute-start | bytes 307208 | tf_op jit(solution)/shard_map/ppermute | solution.py:316
  88.8 17.9 %collective-permute-start.22 = (bf16[400,128]{1,0:T(8,128)(2,1)S(1)}, bf16[400,128]{1,0:T(8,128)(2,1)S(1)}, u32[]{:S(2)}, u32[]{:S(2)}) collective-permute-start(bf16[400,128]{1,0:T(8,128)(2,1)S(1)} %get-tuple-element.29), channel_id=1, source_target_pairs={{0,8},{2,10},{4,12},{6,14},{8,0},{10,2},{12,4},{14,6},{16,24},{18,... | collective-permute-start | bytes 307208 | tf_op jit(solution)/shard_map/ppermute | solution.py:316
  89.6 17.5 %collective-permute-start.23 = (bf16[400,128]{1,0:T(8,128)(2,1)S(1)}, bf16[400,128]{1,0:T(8,128)(2,1)S(1)}, u32[]{:S(2)}, u32[]{:S(2)}) collective-permute-start(bf16[400,128]{1,0:T(8,128)(2,1)S(1)} %get-tuple-element.30), channel_id=1, source_target_pairs={{0,10},{2,8},{4,14},{6,12},{8,2},{10,0},{12,6},{14,4},{16,26},{18,... | collective-permute-start | bytes 307208 | tf_op jit(solution)/shard_map/ppermute | solution.py:316
  93.9 17.0 %collective-permute-start.24 = (bf16[400,128]{1,0:T(8,128)(2,1)S(1)}, bf16[400,128]{1,0:T(8,128)(2,1)S(1)}, u32[]{:S(2)}, u32[]{:S(2)}) collective-permute-start(bf16[400,128]{1,0:T(8,128)(2,1)S(1)} %get-tuple-element.31), channel_id=1, source_target_pairs={{0,12},{2,14},{4,8},{6,10},{8,4},{10,6},{12,0},{14,2},{16,28},{18,... | collective-permute-start | bytes 307208 | tf_op jit(solution)/shard_map/ppermute | solution.py:316
  96.6 17.0 %collective-permute-start.25 = (bf16[400,128]{1,0:T(8,128)(2,1)S(1)}, bf16[400,128]{1,0:T(8,128)(2,1)S(1)}, u32[]{:S(2)}, u32[]{:S(2)}) collective-permute-start(bf16[400,128]{1,0:T(8,128)(2,1)S(1)} %get-tuple-element.32), channel_id=1, source_target_pairs={{0,14},{2,12},{4,10},{6,8},{8,6},{10,4},{12,2},{14,0},{16,30},{18,... | collective-permute-start | bytes 307208 | tf_op jit(solution)/shard_map/ppermute | solution.py:316
  97.8 24.4 %collective-permute-start.26 = (bf16[400,128]{1,0:T(8,128)(2,1)S(1)}, bf16[400,128]{1,0:T(8,128)(2,1)S(1)}, u32[]{:S(2)}, u32[]{:S(2)}) collective-permute-start(bf16[400,128]{1,0:T(8,128)(2,1)S(1)} %get-tuple-element.33), channel_id=1, source_target_pairs={{0,16},{2,18},{4,20},{6,22},{8,24},{10,26},{12,28},{14,30},{16,0},... | collective-permute-start | bytes 307208 | tf_op jit(solution)/shard_map/ppermute | solution.py:316
  106.7 17.6 %collective-permute-start.27 = (bf16[400,128]{1,0:T(8,128)(2,1)S(1)}, bf16[400,128]{1,0:T(8,128)(2,1)S(1)}, u32[]{:S(2)}, u32[]{:S(2)}) collective-permute-start(bf16[400,128]{1,0:T(8,128)(2,1)S(1)} %get-tuple-element.34), channel_id=1, source_target_pairs={{0,18},{2,16},{4,22},{6,20},{8,26},{10,24},{12,30},{14,28},{16,2},... | collective-permute-start | bytes 307208 | tf_op jit(solution)/shard_map/ppermute | solution.py:316
  107.1 19.4 %collective-permute-start.28 = (bf16[400,128]{1,0:T(8,128)(2,1)S(1)}, bf16[400,128]{1,0:T(8,128)(2,1)S(1)}, u32[]{:S(2)}, u32[]{:S(2)}) collective-permute-start(bf16[400,128]{1,0:T(8,128)(2,1)S(1)} %get-tuple-element.35), channel_id=1, source_target_pairs={{0,20},{2,22},{4,16},{6,18},{8,28},{10,30},{12,24},{14,26},{16,4},... | collective-permute-start | bytes 307208 | tf_op jit(solution)/shard_map/ppermute | solution.py:316
  110.9 22.1 %collective-permute-start.29 = (bf16[400,128]{1,0:T(8,128)(2,1)}, bf16[400,128]{1,0:T(8,128)(2,1)S(1)}, u32[]{:S(2)}, u32[]{:S(2)}) collective-permute-start(bf16[400,128]{1,0:T(8,128)(2,1)} %get-tuple-element.36), channel_id=1, source_target_pairs={{0,22},{2,20},{4,18},{6,16},{8,30},{10,28},{12,26},{14,24},{16,6},... | collective-permute-start | bytes 307208 | tf_op jit(solution)/shard_map/ppermute | solution.py:316
  113.5 23.5 %collective-permute-start.30 = (bf16[400,128]{1,0:T(8,128)(2,1)}, bf16[400,128]{1,0:T(8,128)(2,1)S(1)}, u32[]{:S(2)}, u32[]{:S(2)}) collective-permute-start(bf16[400,128]{1,0:T(8,128)(2,1)} %get-tuple-element.37), channel_id=1, source_target_pairs={{0,24},{2,26},{4,28},{6,30},{8,16},{10,18},{12,20},{14,22},{16,8},... | collective-permute-start | bytes 307208 | tf_op jit(solution)/shard_map/ppermute | solution.py:316
  122.1 17.9 %collective-permute-start.31 = (bf16[400,128]{1,0:T(8,128)(2,1)}, bf16[400,128]{1,0:T(8,128)(2,1)S(1)}, u32[]{:S(2)}, u32[]{:S(2)}) collective-permute-start(bf16[400,128]{1,0:T(8,128)(2,1)} %get-tuple-element.38), channel_id=1, source_target_pairs={{0,26},{2,24},{4,30},{6,28},{8,18},{10,16},{12,22},{14,20},{16,10}... | collective-permute-start | bytes 307208 | tf_op jit(solution)/shard_map/ppermute | solution.py:316
  124.3 18.5 %collective-permute-start.32 = (bf16[400,128]{1,0:T(8,128)(2,1)S(1)}, bf16[400,128]{1,0:T(8,128)(2,1)S(1)}, u32[]{:S(2)}, u32[]{:S(2)}) collective-permute-start(bf16[400,128]{1,0:T(8,128)(2,1)S(1)} %get-tuple-element.39), channel_id=1, source_target_pairs={{0,28},{2,30},{4,24},{6,26},{8,20},{10,22},{12,16},{14,18},{16,12}... | collective-permute-start | bytes 307208 | tf_op jit(solution)/shard_map/ppermute | solution.py:316
  126.5 18.6 %collective-permute-start.33 = (bf16[400,128]{1,0:T(8,128)(2,1)S(1)}, bf16[400,128]{1,0:T(8,128)(2,1)S(1)}, u32[]{:S(2)}, u32[]{:S(2)}) collective-permute-start(bf16[400,128]{1,0:T(8,128)(2,1)S(1)} %get-tuple-element.40), channel_id=1, source_target_pairs={{0,30},{2,28},{4,26},{6,24},{8,22},{10,20},{12,18},{14,16},{16,14}... | collective-permute-start | bytes 307208 | tf_op jit(solution)/shard_map/ppermute | solution.py:316
  (14 other events, 114.1 us)

commit v5 on v4

--- a/solution.py
+++ b/solution.py
@@ -12,6 +12,7 @@
 CAP = 2
 STATS = 16
 LABEL_ROW = 6
+SENT = (0, 4, 5, 6, 7, 1, 2, 3, 8, 12, 9, 13, 10, 14, 11, 15)
 VMEM = pl.BlockSpec(memory_space=pltpu.VMEM)
 SMEM = pl.BlockSpec(memory_space=pltpu.SMEM)
 ANY = pl.BlockSpec(memory_space=pl.ANY)
@@ -194,7 +195,7 @@
             whole = whole_refs.pop(0)
             chunks.append([whole.at[s ^ me] for s in range(senders)])
         else:
-            chunks.append(whole_refs[:senders])
+            chunks.append([whole_refs[SENT.index(s)] for s in range(senders)])
             del whole_refs[:senders]
     rows = (chunks[0][0].shape[0] - STATS) // CAP
     to_scalars = pltpu.make_async_copy(mark_ref, label_ref, sem)
@@ -325,7 +326,8 @@
     if vocab == 16 and hid == 2:
         zero = hidden_states
         two = swap(zero, 8)
-        zero_x, zero_y = swap(zero, 1), swap(zero, 2)
+        held = hold(zero, focus_blocks)
+        zero_x, zero_y = swap(held, 1), swap(zero, 2)
         zero_d = swap(zero_y, 1)
         two_x, two_y = swap(two, 1), swap(two, 2)
         to_near = [(2 * v + 1 - (v >> 3), 2 * v + (v >> 3)) for v in range(vocab)]
@@ -358,7 +360,7 @@
         second = chunk([one, one_x, one_y, one_d], [three, three_x, three_y, three_d])
         rows = 4 * zero.shape[0]
         sent = focus_each(me[None], pairs, second, focus_blocks, rows, vocab)
-        came = [sent[0]] + [swap(sent[j], j) for j in range(1, vocab)]
+        came = [swap(sent[j], j) if j else sent[j] for j in SENT]
         received = [exchange(first, rows), came]
         turn = jnp.stack([me, me >> 2 & 1])
 

time: 151 us -> 149 us (0.987)
  starting transfers between devices: 55.6 us -> 50.5 us
  Pallas kernels: 13.1 us -> 15 us
    ppermute x31, starting transfers between devices: 45.3 us -> 41 us  [swap(): return lax.ppermute(x, 'vocab', [(i, i ^ k) for i in range(vocab)])]
    pallas_call x1, Pallas kernels: 4.55 us -> 6.16 us  [sum_slots(): pl.pallas_call(functools.partial(sum_kernel, senders, place), out_shape=j...]
    unnamed x29 -> x33, local copies, waits for them, and re-layouts: 6.48 us -> 7.54 us
  transfers between devices with their start and end apart: 35 -> 35, of which waited for: 16 -> 17; matrix products, arithmetic and copies ran while one was open for 16% -> 16% of each run, Pallas kernels for 6% -> 6%
where the time goes in v5:
time: 149 us; the launch traced here: 148 us
  waiting for transfers between devices  54.8 us (37%)
  starting transfers between devices  50.5 us (34%)
  matrix products  18 us (12%)
  Pallas kernels  15 us (10%)
  local copies, waits for them, and re-layouts  9.42 us (6%)
    ppermute x31, waiting for transfers between devices, swap(): return lax.ppermute(x, 'vocab', [(i, i ^ k) for i in range(vocab)])  54.8 us
    ppermute x31, starting transfers between devices, swap(): return lax.ppermute(x, 'vocab', [(i, i ^ k) for i in range(vocab)])  41 us
    dot_general x4, matrix products, dot(): return jnp.dot(x, head_weight, preferred_element_type=jnp.float32)  18 us
    unnamed x33, local copies, waits for them, and re-layouts  7.54 us
    all_to_all x1, starting transfers between devices, exchange(): lax.all_to_all(sent, 'vocab', split_axis=0, concat_axis=0, tiled=True)  6.27 us
    pallas_call x1, Pallas kernels, sum_slots(): pl.pallas_call(functools.partial(sum_kernel, senders, place), out_shape=j...  6.16 us
    pallas_call x1, Pallas kernels, focus_each(): pl.pallas_call(functools.partial(focus_each_kernel, rows), out_shape=[jax...  4.42 us
    ppermute x2, starting transfers between devices, product(): return (logits, lax.ppermute(logits, ('vocab', 'hid'), pairs))  3.24 us
  transfers between devices with their start and end apart: 35, of which 17 were waited for; matrix products, arithmetic and copies ran while one was open for 16% of the time, Pallas kernels for 6%

profile of v5, /device:TPU:10, one launch (start us, length us, event | category | flops | bytes accessed | tf_op | source)
XLA Modules:
  0.0 148.4 jit_solution(50710214758566987)
XLA Ops:
  1.5 2.6 %collective-permute-start = (bf16[48,4096]{1,0:T(8,128)(2,1)}, bf16[48,4096]{1,0:T(8,128)(2,1)S(1)}, u32[]{:S(2)}, u32[]{:S(2)}) collective-permute-start(bf16[48,4096]{1,0:T(8,128)(2,1)} %x_ref.3), channel_id=1, source_target_pairs={{0,16},{2,18},{4,20},{6,22},{8,24},{10,26},{12,28},{14,30},{16,0},... | collective-permute-start | bytes 1179656 | tf_op jit(solution)/shard_map/ppermute | solution.py:317
  6.8 4.3 %collective-permute-done.4.refs_2_ = bf16[48,4096]{1,0:T(8,128)(2,1)S(1)} collective-permute-done((bf16[48,4096]{1,0:T(8,128)(2,1)}, bf16[48,4096]{1,0:T(8,128)(2,1)S(1)}, u32[]{:S(2)}, u32[]{:S(2)}) %collective-permute-start.4) | collective-permute-done | bytes 393248 | tf_op jit(solution)/shard_map/ppermute | solution.py:317
  12.5 8.3 %collective-permute-done.earlier_ref.refs_0_ = bf16[48,4096]{1,0:T(8,128)(2,1)S(1)} collective-permute-done((bf16[48,4096]{1,0:T(8,128)(2,1)}, bf16[48,4096]{1,0:T(8,128)(2,1)S(1)}, u32[]{:S(2)}, u32[]{:S(2)}) %collective-permute-start) | collective-permute-done | bytes 393248 | tf_op jit(solution)/shard_map/ppermute | solution.py:317
  24.0 2.2 %collective-permute-done.5.refs_3_ = bf16[48,4096]{1,0:T(8,128)(2,1)S(1)} collective-permute-done((bf16[48,4096]{1,0:T(8,128)(2,1)S(1)}, bf16[48,4096]{1,0:T(8,128)(2,1)S(1)}, u32[]{:S(2)}, u32[]{:S(2)}) %collective-permute-start.5) | collective-permute-done | bytes 393248 | tf_op jit(solution)/shard_map/ppermute | solution.py:317
  26.4 6.3 %fusion.6.refs_0_.refs_2_ = f32[192,1280]{1,0:T(8,128)S(1)} fusion(bf16[192,4096]{1,0:T(8,128)(2,1)S(1)} %shard_map.47, bf16[4096,1280]{1,0:T(8,128)(2,1)} %param.5), kind=kOutput, calls=%fused_computation.17 | convolution fusion | flops 2013265920 | bytes 13041664 | tf_op jit(solution)/shard_map/dot_general | solution.py:320
  36.7 3.7 %collective-permute-done.9.refs_6_ = bf16[48,4096]{1,0:T(8,128)(2,1)S(1)} collective-permute-done((bf16[48,4096]{1,0:T(8,128)(2,1)S(1)}, bf16[48,4096]{1,0:T(8,128)(2,1)S(1)}, u32[]{:S(2)}, u32[]{:S(2)}) %collective-permute-start.9) | collective-permute-done | bytes 393248 | tf_op jit(solution)/shard_map/ppermute | solution.py:317
  43.1 2.3 %fusion.7.refs_0_ = f32[192,1280]{1,0:T(8,128)S(1)} fusion(bf16[192,4096]{1,0:T(8,128)(2,1)S(1)} %shard_map.50, bf16[4096,1280]{1,0:T(8,128)(2,1)S(1)} %bitcast.11), kind=kOutput, calls=%fused_computation.18 | convolution fusion | flops 2013265920 | bytes 13041664 | tf_op jit(solution)/shard_map/dot_general | solution.py:320
  45.5 5.4 %collective-permute-done.12 = bf16[48,4096]{1,0:T(8,128)(2,1)S(1)} collective-permute-done((bf16[48,4096]{1,0:T(8,128)(2,1)S(1)}, bf16[48,4096]{1,0:T(8,128)(2,1)S(1)}, u32[]{:S(2)}, u32[]{:S(2)}) %collective-permute-start.12) | collective-permute-done | bytes 393248 | tf_op jit(solution)/shard_map/ppermute | solution.py:317
  50.8 1.9 %collective-permute-start.10 = (f32[192,1280]{1,0:T(8,128)S(1)}, f32[192,1280]{1,0:T(8,128)S(1)}, u32[]{:S(2)}, u32[]{:S(2)}) collective-permute-start(f32[192,1280]{1,0:T(8,128)S(1)} %fusion.7.refs_0_), channel_id=1, source_target_pairs={{0,1},{2,3},{4,5},{6,7},{8,9},{10,11},{12,13},{14,15},{17,16},{19,... | collective-permute-start | bytes 2949128 | tf_op jit(solution)/shard_map/ppermute | solution.py:340
  56.7 2.1 %shard_map.52 = bf16[16,400,128]{2,1,0:T(8,128)(2,1)} custom-call(s32[1]{0:T(128)} %bitcast.me_ref, s32[32]{0:T(128)S(1)} %reshape.3.pair_ref, bf16[1936,128]{1,0:T(8,128)(2,1)S(1)} %shard_map.51.tiles_ref, bf16[16,128,128]{2,1,0:T(8,128)(2,1)S(1)} %copy-done.1), custom_call_target="tpu_custom_call" | custom-call | flops 100663296 | bytes 3276800 | tf_op jit(solution)/shard_map/pallas_call | solution.py:129
  58.8 6.3 %all-to-all-start = ((bf16[16,400,128]{2,1,0:T(8,128)(2,1)}), bf16[16,400,128]{2,1,0:T(8,128)(2,1)S(1)}, u32[]{:S(2)}, u32[]{:S(2)}) async-start(bf16[16,400,128]{2,1,0:T(8,128)(2,1)} %shard_map.52), calls=%async_computation | async-start | bytes 3276800 | tf_op jit(solution)/shard_map/all_to_all | solution.py:324
  65.9 1.9 %constant_dynamic-update-slice_fusion.5 = bf16[192,4096]{1,0:T(8,128)(2,1)} fusion(bf16[192,4096]{1,0:T(8,128)(2,1)} %constant_dynamic-update-slice_fusion.6, bf16[48,4096]{1,0:T(8,128)(2,1)} %collective-permute-done.16), kind=kLoop, calls=%fused_computation.12 | loop fusion | bytes 786432
  67.8 1.8 %constant_dynamic-update-slice_fusion.4 = bf16[192,4096]{1,0:T(8,128)(2,1)} fusion(bf16[192,4096]{1,0:T(8,128)(2,1)} %constant_dynamic-update-slice_fusion.5, bf16[48,4096]{1,0:T(8,128)(2,1)} %collective-permute-done.17), kind=kLoop, calls=%fused_computation.11 | loop fusion | bytes 786432 | tf_op jit(solution)/shard_map/concatenate | solution.py:343
  69.5 6.9 %fusion = f32[192,1280]{1,0:T(8,128)S(1)} fusion(bf16[4096,1280]{1,0:T(8,128)(2,1)} %param.5, bf16[192,4096]{1,0:T(8,128)(2,1)} %constant_dynamic-update-slice_fusion.4, bf16[192,4096]{1,0:T(8,128)(2,1)S(1)} %copy-done.6, pred[]{:T(512)S(6)} %eq.3), kind=kOutput, calls=%fused_computation | convolution fusion | flops 2014052352 | bytes 14614529 | tf_op jit(solution)/shard_map/dot_general | solution.py:320
  76.6 2.5 %fusion.2.refs_0_.refs_2_ = f32[192,1280]{1,0:T(8,128)S(1)} fusion(bf16[4096,1280]{1,0:T(8,128)(2,1)S(1)} %bitcast.13, bf16[192,4096]{1,0:T(8,128)(2,1)S(1)} %copy-done.6, bf16[192,4096]{1,0:T(8,128)(2,1)S(1)} %copy-done.4, pred[]{:T(512)S(6)} %eq.3), kind=kOutput, calls=%fused_computation.2 | convolution fusion | flops 2014052352 | bytes 14614529 | tf_op jit(solution)/shard_map/dot_general | solution.py:320
  80.2 4.4 %shard_map.54 = (bf16[400,128]{1,0:T(8,128)(2,1)S(1)}, bf16[400,128]{1,0:T(8,128)(2,1)S(1)}, bf16[400,128]{1,0:T(8,128)(2,1)S(1)}, bf16[400,128]{1,0:T(8,128)(2,...) custom-call(s32[1]{0:T(128)} %bitcast.me_ref, ...), custom_call_target="tpu_custom_call" | custom-call | tf_op jit(solution)/shard_map/pallas_call | solution.py:179
  88.1 2.3 %collective-permute-start.22 = (bf16[400,128]{1,0:T(8,128)(2,1)S(1)}, bf16[400,128]{1,0:T(8,128)(2,1)S(1)}, u32[]{:S(2)}, u32[]{:S(2)}) collective-permute-start(bf16[400,128]{1,0:T(8,128)(2,1)S(1)} %get-tuple-element.29), channel_id=1, source_target_pairs={{0,14},{2,12},{4,10},{6,8},{8,6},{10,4},{12,2},{14,0},{16,30},{18,... | collective-permute-start | bytes 307208 | tf_op jit(solution)/shard_map/ppermute | solution.py:317
  91.0 5.2 %collective-permute-done.19.refs_2_ = bf16[400,128]{1,0:T(8,128)(2,1)S(1)} collective-permute-done((bf16[400,128]{1,0:T(8,128)(2,1)S(1)}, bf16[400,128]{1,0:T(8,128)(2,1)S(1)}, u32[]{:S(2)}, u32[]{:S(2)}) %collective-permute-start.19) | collective-permute-done | bytes 102432 | tf_op jit(solution)/shard_map/ppermute | solution.py:317
  96.2 1.8 %collective-permute-start.24 = (bf16[400,128]{1,0:T(8,128)(2,1)S(1)}, bf16[400,128]{1,0:T(8,128)(2,1)S(1)}, u32[]{:S(2)}, u32[]{:S(2)}) collective-permute-start(bf16[400,128]{1,0:T(8,128)(2,1)S(1)} %get-tuple-element.31), channel_id=1, source_target_pairs={{0,4},{2,6},{4,0},{6,2},{8,12},{10,14},{12,8},{14,10},{16,20},{18,... | collective-permute-start | bytes 307208 | tf_op jit(solution)/shard_map/ppermute | solution.py:317
  98.5 2.6 %collective-permute-start.25 = (bf16[400,128]{1,0:T(8,128)(2,1)}, bf16[400,128]{1,0:T(8,128)(2,1)S(1)}, u32[]{:S(2)}, u32[]{:S(2)}) collective-permute-start(bf16[400,128]{1,0:T(8,128)(2,1)} %get-tuple-element.32), channel_id=1, source_target_pairs={{0,6},{2,4},{4,2},{6,0},{8,14},{10,12},{12,10},{14,8},{16,22},{18,... | collective-permute-start | bytes 307208 | tf_op jit(solution)/shard_map/ppermute | solution.py:317
  102.6 4.7 %collective-permute-start.26 = (bf16[400,128]{1,0:T(8,128)(2,1)S(1)}, bf16[400,128]{1,0:T(8,128)(2,1)S(1)}, u32[]{:S(2)}, u32[]{:S(2)}) collective-permute-start(bf16[400,128]{1,0:T(8,128)(2,1)S(1)} %get-tuple-element.33), channel_id=1, source_target_pairs={{0,16},{2,18},{4,20},{6,22},{8,24},{10,26},{12,28},{14,30},{16,0},... | collective-permute-start | bytes 307208 | tf_op jit(solution)/shard_map/ppermute | solution.py:317
  108.1 2.0 %collective-permute-start.28 = (bf16[400,128]{1,0:T(8,128)(2,1)S(1)}, bf16[400,128]{1,0:T(8,128)(2,1)S(1)}, u32[]{:S(2)}, u32[]{:S(2)}) collective-permute-start(bf16[400,128]{1,0:T(8,128)(2,1)S(1)} %get-tuple-element.35), channel_id=1, source_target_pairs={{0,18},{2,16},{4,22},{6,20},{8,26},{10,24},{12,30},{14,28},{16,2},... | collective-permute-start | bytes 307208 | tf_op jit(solution)/shard_map/ppermute | solution.py:317
  110.1 2.6 %collective-permute-start.29 = (bf16[400,128]{1,0:T(8,128)(2,1)}, bf16[400,128]{1,0:T(8,128)(2,1)S(1)}, u32[]{:S(2)}, u32[]{:S(2)}) collective-permute-start(bf16[400,128]{1,0:T(8,128)(2,1)} %get-tuple-element.36), channel_id=1, source_target_pairs={{0,26},{2,24},{4,30},{6,28},{8,18},{10,16},{12,22},{14,20},{16,10}... | collective-permute-start | bytes 307208 | tf_op jit(solution)/shard_map/ppermute | solution.py:317
  114.3 6.2 %collective-permute-done.26.refs_9_ = bf16[400,128]{1,0:T(8,128)(2,1)S(1)} collective-permute-done((bf16[400,128]{1,0:T(8,128)(2,1)S(1)}, bf16[400,128]{1,0:T(8,128)(2,1)S(1)}, u32[]{:S(2)}, u32[]{:S(2)}) %collective-permute-start.26) | collective-permute-done | bytes 102432 | tf_op jit(solution)/shard_map/ppermute | solution.py:317
  120.5 2.2 %collective-permute-done.27.refs_10_ = bf16[400,128]{1,0:T(8,128)(2,1)S(1)} collective-permute-done((bf16[400,128]{1,0:T(8,128)(2,1)S(1)}, bf16[400,128]{1,0:T(8,128)(2,1)S(1)}, u32[]{:S(2)}, u32[]{:S(2)}) %collective-permute-start.27) | collective-permute-done | bytes 102432 | tf_op jit(solution)/shard_map/ppermute | solution.py:317
  126.0 2.8 %collective-permute-start.33 = (bf16[400,128]{1,0:T(8,128)(2,1)S(1)}, bf16[400,128]{1,0:T(8,128)(2,1)S(1)}, u32[]{:S(2)}, u32[]{:S(2)}) collective-permute-start(bf16[400,128]{1,0:T(8,128)(2,1)S(1)} %get-tuple-element.40), channel_id=1, source_target_pairs={{0,30},{2,28},{4,26},{6,24},{8,22},{10,20},{12,18},{14,16},{16,14}... | collective-permute-start | bytes 307208 | tf_op jit(solution)/shard_map/ppermute | solution.py:317
  128.9 2.9 %collective-permute-done.29.refs_12_ = bf16[400,128]{1,0:T(8,128)(2,1)S(1)} collective-permute-done((bf16[400,128]{1,0:T(8,128)(2,1)}, bf16[400,128]{1,0:T(8,128)(2,1)S(1)}, u32[]{:S(2)}, u32[]{:S(2)}) %collective-permute-start.29) | collective-permute-done | bytes 102432 | tf_op jit(solution)/shard_map/ppermute | solution.py:317
  131.7 3.1 %collective-permute-done.30.refs_13_ = bf16[400,128]{1,0:T(8,128)(2,1)S(1)} collective-permute-done((bf16[400,128]{1,0:T(8,128)(2,1)}, bf16[400,128]{1,0:T(8,128)(2,1)S(1)}, u32[]{:S(2)}, u32[]{:S(2)}) %collective-permute-start.30) | collective-permute-done | bytes 102432 | tf_op jit(solution)/shard_map/ppermute | solution.py:317
  134.8 2.2 %collective-permute-done.31.refs_14_ = bf16[400,128]{1,0:T(8,128)(2,1)S(1)} collective-permute-done((bf16[400,128]{1,0:T(8,128)(2,1)}, bf16[400,128]{1,0:T(8,128)(2,1)S(1)}, u32[]{:S(2)}, u32[]{:S(2)}) %collective-permute-start.31) | collective-permute-done | bytes 102432 | tf_op jit(solution)/shard_map/ppermute | solution.py:317
  137.0 2.1 %collective-permute-done.32.refs_15_ = bf16[400,128]{1,0:T(8,128)(2,1)S(1)} collective-permute-done((bf16[400,128]{1,0:T(8,128)(2,1)S(1)}, bf16[400,128]{1,0:T(8,128)(2,1)S(1)}, u32[]{:S(2)}, u32[]{:S(2)}) %collective-permute-start.32) | collective-permute-done | bytes 102432 | tf_op jit(solution)/shard_map/ppermute | solution.py:317
  139.1 3.0 %collective-permute-done.33.refs_16_ = bf16[400,128]{1,0:T(8,128)(2,1)S(1)} collective-permute-done((bf16[400,128]{1,0:T(8,128)(2,1)S(1)}, bf16[400,128]{1,0:T(8,128)(2,1)S(1)}, u32[]{:S(2)}, u32[]{:S(2)}) %collective-permute-start.33) | collective-permute-done | bytes 102432 | tf_op jit(solution)/shard_map/ppermute | solution.py:317
  142.1 6.2 %shard_map.55 = f32[384,1536]{1,0:T(8,128)} custom-call(s32[2]{0:T(128)S(1)} %pad_add_fusion.me_ref, bf16[16,400,128]{2,1,0:T(8,128)(2,1)S(1)} %all-to-all-done.refs_0_, bf16[400,128]{1,0:T(8,128)(2,1)S(1)} %get-tuple-element.25.refs_1_, bf16[400,128]{1,0:T(8,128)(2,1)S(1)} %collective-permute-done.19.refs_2_, ...), custom_call_target="tpu_custom_call" | custom-call | flops 3145728 | bytes 2359296 | tf_op jit(solution)/shard_map/pallas_call | solution.py:254
  (93 shorter events, 33.4 us)
Async XLA Ops:
  0.0 11.1 %collective-permute-start.4 = (bf16[48,4096]{1,0:T(8,128)(2,1)}, bf16[48,4096]{1,0:T(8,128)(2,1)S(1)}, u32[]{:S(2)}, u32[]{:S(2)}) collective-permute-start(bf16[48,4096]{1,0:T(8,128)(2,1)} %x_ref.3), channel_id=1, source_target_pairs={{0,4},{2,6},{4,0},{6,2},{8,12},{10,14},{12,8},{14,10},{16,20},{18,... | collective-permute-start | bytes 1179656 | tf_op jit(solution)/shard_map/ppermute | solution.py:317
  1.5 19.3 %collective-permute-start = (bf16[48,4096]{1,0:T(8,128)(2,1)}, bf16[48,4096]{1,0:T(8,128)(2,1)S(1)}, u32[]{:S(2)}, u32[]{:S(2)}) collective-permute-start(bf16[48,4096]{1,0:T(8,128)(2,1)} %x_ref.3), channel_id=1, source_target_pairs={{0,16},{2,18},{4,20},{6,22},{8,24},{10,26},{12,28},{14,30},{16,0},... | collective-permute-start | bytes 1179656 | tf_op jit(solution)/shard_map/ppermute | solution.py:317
  6.2 17.0 %collective-permute-start.3 = (bf16[48,4096]{1,0:T(8,128)(2,1)S(1)}, bf16[48,4096]{1,0:T(8,128)(2,1)S(1)}, u32[]{:S(2)}, u32[]{:S(2)}) collective-permute-start(bf16[48,4096]{1,0:T(8,128)(2,1)S(1)} %shard_map.46), channel_id=1, source_target_pairs={{0,2},{2,0},{4,6},{6,4},{8,10},{10,8},{12,14},{14,12},{16,18},{18,... | collective-permute-start | bytes 1179656 | tf_op jit(solution)/shard_map/ppermute | solution.py:317
  11.1 15.2 %collective-permute-start.5 = (bf16[48,4096]{1,0:T(8,128)(2,1)S(1)}, bf16[48,4096]{1,0:T(8,128)(2,1)S(1)}, u32[]{:S(2)}, u32[]{:S(2)}) collective-permute-start(bf16[48,4096]{1,0:T(8,128)(2,1)S(1)} %collective-permute-done.4.refs_2_), channel_id=1, source_target_pairs={{0,2},{2,0},{4,6},{6,4},{8,10},{10,8},{12,14},{14,12},{16,18},{18,... | collective-permute-start | bytes 1179656 | tf_op jit(solution)/shard_map/ppermute | solution.py:317
  20.9 14.3 %collective-permute-start.8 = (bf16[48,4096]{1,0:T(8,128)(2,1)S(1)}, bf16[48,4096]{1,0:T(8,128)(2,1)S(1)}, u32[]{:S(2)}, u32[]{:S(2)}) collective-permute-start(bf16[48,4096]{1,0:T(8,128)(2,1)S(1)} %shard_map.49), channel_id=1, source_target_pairs={{0,8},{2,10},{4,12},{6,14},{8,0},{10,2},{12,4},{14,6},{16,24},{18,... | collective-permute-start | bytes 1179656 | tf_op jit(solution)/shard_map/ppermute | solution.py:317
  22.2 11.8 %collective-permute-start.1 = (bf16[48,4096]{1,0:T(8,128)(2,1)S(1)}, bf16[48,4096]{1,0:T(8,128)(2,1)S(1)}, u32[]{:S(2)}, u32[]{:S(2)}) collective-permute-start(bf16[48,4096]{1,0:T(8,128)(2,1)S(1)} %collective-permute-done.earlier_ref.refs_0_), channel_id=1, source_target_pairs={{0,2},{2,0},{4,6},{6,4},{8,10},{10,8},{12,14},{14,12},{16,18},{18,... | collective-permute-start | bytes 1179656 | tf_op jit(solution)/shard_map/ppermute | solution.py:317
  22.7 11.3 %collective-permute-start.2 = (bf16[48,4096]{1,0:T(8,128)(2,1)S(1)}, bf16[48,4096]{1,0:T(8,128)(2,1)S(1)}, u32[]{:S(2)}, u32[]{:S(2)}) collective-permute-start(bf16[48,4096]{1,0:T(8,128)(2,1)S(1)} %collective-permute-done.earlier_ref.refs_0_), channel_id=1, source_target_pairs={{0,4},{2,6},{4,0},{6,2},{8,12},{10,14},{12,8},{14,10},{16,20},{18,... | collective-permute-start | bytes 1179656 | tf_op jit(solution)/shard_map/ppermute | solution.py:317
  23.2 17.2 %collective-permute-start.9 = (bf16[48,4096]{1,0:T(8,128)(2,1)S(1)}, bf16[48,4096]{1,0:T(8,128)(2,1)S(1)}, u32[]{:S(2)}, u32[]{:S(2)}) collective-permute-start(bf16[48,4096]{1,0:T(8,128)(2,1)S(1)} %collective-permute-done.earlier_ref.refs_0_), channel_id=1, source_target_pairs={{0,8},{2,10},{4,12},{6,14},{8,0},{10,2},{12,4},{14,6},{16,24},{18,... | collective-permute-start | bytes 1179656 | tf_op jit(solution)/shard_map/ppermute | solution.py:317
  32.7 21.9 %collective-permute-start.11 = (f32[192,1280]{1,0:T(8,128)S(1)}, f32[192,1280]{1,0:T(8,128)S(1)}, u32[]{:S(2)}, u32[]{:S(2)}) collective-permute-start(f32[192,1280]{1,0:T(8,128)S(1)} %fusion.6.refs_0_.refs_2_), channel_id=1, source_target_pairs={{1,0},{3,2},{5,4},{7,6},{9,8},{11,10},{13,12},{15,14},{16,17},{18,... | collective-permute-start | bytes 2949128 | tf_op jit(solution)/shard_map/ppermute | solution.py:340
  34.6 7.8 %collective-permute-start.7 = (bf16[48,2048]{1,0:T(8,128)(2,1)S(1)}, bf16[48,2048]{1,0:T(8,128)(2,1)S(1)}, u32[]{:S(2)}, u32[]{:S(2)}) collective-permute-start(bf16[48,2048]{1,0:T(8,128)(2,1)S(1)} %get-tuple-element.24), channel_id=1, source_target_pairs={{0,2},{2,0},{4,6},{6,4},{8,10},{10,8},{12,14},{14,12},{16,18},{18,... | collective-permute-start | bytes 589832 | tf_op jit(solution)/shard_map/ppermute | solution.py:317
  35.2 15.7 %collective-permute-start.12 = (bf16[48,4096]{1,0:T(8,128)(2,1)S(1)}, bf16[48,4096]{1,0:T(8,128)(2,1)S(1)}, u32[]{:S(2)}, u32[]{:S(2)}) collective-permute-start(bf16[48,4096]{1,0:T(8,128)(2,1)S(1)} %collective-permute-done.8.refs_5_), channel_id=1, source_target_pairs={{0,2},{2,0},{4,6},{6,4},{8,10},{10,8},{12,14},{14,12},{16,18},{18,... | collective-permute-start | bytes 1179656 | tf_op jit(solution)/shard_map/ppermute | solution.py:317
  40.4 12.4 %collective-permute-start.13 = (bf16[48,4096]{1,0:T(8,128)(2,1)S(1)}, bf16[48,4096]{1,0:T(8,128)(2,1)S(1)}, u32[]{:S(2)}, u32[]{:S(2)}) collective-permute-start(bf16[48,4096]{1,0:T(8,128)(2,1)S(1)} %collective-permute-done.8.refs_5_), channel_id=1, source_target_pairs={{0,4},{2,6},{4,0},{6,2},{8,12},{10,14},{12,8},{14,10},{16,20},{18,... | collective-permute-start | bytes 1179656 | tf_op jit(solution)/shard_map/ppermute | solution.py:317
  41.7 12.8 %collective-permute-start.14 = (bf16[48,4096]{1,0:T(8,128)(2,1)S(1)}, bf16[48,4096]{1,0:T(8,128)(2,1)S(1)}, u32[]{:S(2)}, u32[]{:S(2)}) collective-permute-start(bf16[48,4096]{1,0:T(8,128)(2,1)S(1)} %collective-permute-done.5.refs_3_), channel_id=1, source_target_pairs={{0,8},{2,10},{4,12},{6,14},{8,0},{10,2},{12,4},{14,6},{16,24},{18,... | collective-permute-start | bytes 1179656 | tf_op jit(solution)/shard_map/ppermute | solution.py:317
  42.4 22.7 %collective-permute-start.15 = (bf16[48,4096]{1,0:T(8,128)(2,1)S(1)}, bf16[48,4096]{1,0:T(8,128)(2,1)S(1)}, u32[]{:S(2)}, u32[]{:S(2)}) collective-permute-start(bf16[48,4096]{1,0:T(8,128)(2,1)S(1)} %collective-permute-done.9.refs_6_), channel_id=1, source_target_pairs={{0,2},{2,0},{4,6},{6,4},{8,10},{10,8},{12,14},{14,12},{16,18},{18,... | collective-permute-start | bytes 1179656 | tf_op jit(solution)/shard_map/ppermute | solution.py:317
  52.8 13.0 %collective-permute-start.16 = (bf16[48,4096]{1,0:T(8,128)(2,1)S(1)}, bf16[48,4096]{1,0:T(8,128)(2,1)}, u32[]{:S(2)}, u32[]{:S(2)}) collective-permute-start(bf16[48,4096]{1,0:T(8,128)(2,1)S(1)} %collective-permute-done.9.refs_6_), channel_id=1, source_target_pairs={{0,4},{2,6},{4,0},{6,2},{8,12},{10,14},{12,8},{14,10},{16,20},{18,... | collective-permute-start | bytes 1179656 | tf_op jit(solution)/shard_map/ppermute | solution.py:317
  54.5 13.3 %collective-permute-start.17 = (bf16[48,4096]{1,0:T(8,128)(2,1)S(1)}, bf16[48,4096]{1,0:T(8,128)(2,1)}, u32[]{:S(2)}, u32[]{:S(2)}) collective-permute-start(bf16[48,4096]{1,0:T(8,128)(2,1)S(1)} %pad_maximum_fusion), channel_id=1, source_target_pairs={{0,8},{2,10},{4,12},{6,14},{8,0},{10,2},{12,4},{14,6},{16,24},{18,... | collective-permute-start | bytes 1179656 | tf_op jit(solution)/shard_map/ppermute | solution.py:317
  58.8 83.3 %all-to-all-start = ((bf16[16,400,128]{2,1,0:T(8,128)(2,1)}), bf16[16,400,128]{2,1,0:T(8,128)(2,1)S(1)}, u32[]{:S(2)}, u32[]{:S(2)}) async-start(bf16[16,400,128]{2,1,0:T(8,128)(2,1)} %shard_map.52), calls=%async_computation | async-start | bytes 3276800 | tf_op jit(solution)/shard_map/all_to_all | solution.py:324
  84.6 11.6 %collective-permute-start.19 = (bf16[400,128]{1,0:T(8,128)(2,1)S(1)}, bf16[400,128]{1,0:T(8,128)(2,1)S(1)}, u32[]{:S(2)}, u32[]{:S(2)}) collective-permute-start(bf16[400,128]{1,0:T(8,128)(2,1)S(1)} %get-tuple-element.26), channel_id=1, source_target_pairs={{0,8},{2,10},{4,12},{6,14},{8,0},{10,2},{12,4},{14,6},{16,24},{18,... | collective-permute-start | bytes 307208 | tf_op jit(solution)/shard_map/ppermute | solution.py:317
  85.3 13.2 %collective-permute-start.20 = (bf16[400,128]{1,0:T(8,128)(2,1)S(1)}, bf16[400,128]{1,0:T(8,128)(2,1)S(1)}, u32[]{:S(2)}, u32[]{:S(2)}) collective-permute-start(bf16[400,128]{1,0:T(8,128)(2,1)S(1)} %get-tuple-element.27), channel_id=1, source_target_pairs={{0,10},{2,8},{4,14},{6,12},{8,2},{10,0},{12,6},{14,4},{16,26},{18,... | collective-permute-start | bytes 307208 | tf_op jit(solution)/shard_map/ppermute | solution.py:317
  86.6 16.0 %collective-permute-start.21 = (bf16[400,128]{1,0:T(8,128)(2,1)S(1)}, bf16[400,128]{1,0:T(8,128)(2,1)S(1)}, u32[]{:S(2)}, u32[]{:S(2)}) collective-permute-start(bf16[400,128]{1,0:T(8,128)(2,1)S(1)} %get-tuple-element.28), channel_id=1, source_target_pairs={{0,12},{2,14},{4,8},{6,10},{8,4},{10,6},{12,0},{14,2},{16,28},{18,... | collective-permute-start | bytes 307208 | tf_op jit(solution)/shard_map/ppermute | solution.py:317
  88.1 19.1 %collective-permute-start.22 = (bf16[400,128]{1,0:T(8,128)(2,1)S(1)}, bf16[400,128]{1,0:T(8,128)(2,1)S(1)}, u32[]{:S(2)}, u32[]{:S(2)}) collective-permute-start(bf16[400,128]{1,0:T(8,128)(2,1)S(1)} %get-tuple-element.29), channel_id=1, source_target_pairs={{0,14},{2,12},{4,10},{6,8},{8,6},{10,4},{12,2},{14,0},{16,30},{18,... | collective-permute-start | bytes 307208 | tf_op jit(solution)/shard_map/ppermute | solution.py:317
  90.4 17.6 %collective-permute-start.23 = (bf16[400,128]{1,0:T(8,128)(2,1)S(1)}, bf16[400,128]{1,0:T(8,128)(2,1)S(1)}, u32[]{:S(2)}, u32[]{:S(2)}) collective-permute-start(bf16[400,128]{1,0:T(8,128)(2,1)S(1)} %get-tuple-element.30), channel_id=1, source_target_pairs={{0,2},{2,0},{4,6},{6,4},{8,10},{10,8},{12,14},{14,12},{16,18},{18,... | collective-permute-start | bytes 307208 | tf_op jit(solution)/shard_map/ppermute | solution.py:317
  96.2 13.9 %collective-permute-start.24 = (bf16[400,128]{1,0:T(8,128)(2,1)S(1)}, bf16[400,128]{1,0:T(8,128)(2,1)S(1)}, u32[]{:S(2)}, u32[]{:S(2)}) collective-permute-start(bf16[400,128]{1,0:T(8,128)(2,1)S(1)} %get-tuple-element.31), channel_id=1, source_target_pairs={{0,4},{2,6},{4,0},{6,2},{8,12},{10,14},{12,8},{14,10},{16,20},{18,... | collective-permute-start | bytes 307208 | tf_op jit(solution)/shard_map/ppermute | solution.py:317
  98.5 14.2 %collective-permute-start.25 = (bf16[400,128]{1,0:T(8,128)(2,1)}, bf16[400,128]{1,0:T(8,128)(2,1)S(1)}, u32[]{:S(2)}, u32[]{:S(2)}) collective-permute-start(bf16[400,128]{1,0:T(8,128)(2,1)} %get-tuple-element.32), channel_id=1, source_target_pairs={{0,6},{2,4},{4,2},{6,0},{8,14},{10,12},{12,10},{14,8},{16,22},{18,... | collective-permute-start | bytes 307208 | tf_op jit(solution)/shard_map/ppermute | solution.py:317
  102.6 17.9 %collective-permute-start.26 = (bf16[400,128]{1,0:T(8,128)(2,1)S(1)}, bf16[400,128]{1,0:T(8,128)(2,1)S(1)}, u32[]{:S(2)}, u32[]{:S(2)}) collective-permute-start(bf16[400,128]{1,0:T(8,128)(2,1)S(1)} %get-tuple-element.33), channel_id=1, source_target_pairs={{0,16},{2,18},{4,20},{6,22},{8,24},{10,26},{12,28},{14,30},{16,0},... | collective-permute-start | bytes 307208 | tf_op jit(solution)/shard_map/ppermute | solution.py:317
  107.3 15.4 %collective-permute-start.27 = (bf16[400,128]{1,0:T(8,128)(2,1)S(1)}, bf16[400,128]{1,0:T(8,128)(2,1)S(1)}, u32[]{:S(2)}, u32[]{:S(2)}) collective-permute-start(bf16[400,128]{1,0:T(8,128)(2,1)S(1)} %get-tuple-element.34), channel_id=1, source_target_pairs={{0,24},{2,26},{4,28},{6,30},{8,16},{10,18},{12,20},{14,22},{16,8},... | collective-permute-start | bytes 307208 | tf_op jit(solution)/shard_map/ppermute | solution.py:317
  108.1 17.9 %collective-permute-start.28 = (bf16[400,128]{1,0:T(8,128)(2,1)S(1)}, bf16[400,128]{1,0:T(8,128)(2,1)S(1)}, u32[]{:S(2)}, u32[]{:S(2)}) collective-permute-start(bf16[400,128]{1,0:T(8,128)(2,1)S(1)} %get-tuple-element.35), channel_id=1, source_target_pairs={{0,18},{2,16},{4,22},{6,20},{8,26},{10,24},{12,30},{14,28},{16,2},... | collective-permute-start | bytes 307208 | tf_op jit(solution)/shard_map/ppermute | solution.py:317
  110.1 21.6 %collective-permute-start.29 = (bf16[400,128]{1,0:T(8,128)(2,1)}, bf16[400,128]{1,0:T(8,128)(2,1)S(1)}, u32[]{:S(2)}, u32[]{:S(2)}) collective-permute-start(bf16[400,128]{1,0:T(8,128)(2,1)} %get-tuple-element.36), channel_id=1, source_target_pairs={{0,26},{2,24},{4,30},{6,28},{8,18},{10,16},{12,22},{14,20},{16,10}... | collective-permute-start | bytes 307208 | tf_op jit(solution)/shard_map/ppermute | solution.py:317
  112.6 22.2 %collective-permute-start.30 = (bf16[400,128]{1,0:T(8,128)(2,1)}, bf16[400,128]{1,0:T(8,128)(2,1)S(1)}, u32[]{:S(2)}, u32[]{:S(2)}) collective-permute-start(bf16[400,128]{1,0:T(8,128)(2,1)} %get-tuple-element.37), channel_id=1, source_target_pairs={{0,20},{2,22},{4,16},{6,18},{8,28},{10,30},{12,24},{14,26},{16,4},... | collective-permute-start | bytes 307208 | tf_op jit(solution)/shard_map/ppermute | solution.py:317
  120.5 16.6 %collective-permute-start.31 = (bf16[400,128]{1,0:T(8,128)(2,1)}, bf16[400,128]{1,0:T(8,128)(2,1)S(1)}, u32[]{:S(2)}, u32[]{:S(2)}) collective-permute-start(bf16[400,128]{1,0:T(8,128)(2,1)} %get-tuple-element.38), channel_id=1, source_target_pairs={{0,28},{2,30},{4,24},{6,26},{8,20},{10,22},{12,16},{14,18},{16,12}... | collective-permute-start | bytes 307208 | tf_op jit(solution)/shard_map/ppermute | solution.py:317
  122.7 16.5 %collective-permute-start.32 = (bf16[400,128]{1,0:T(8,128)(2,1)S(1)}, bf16[400,128]{1,0:T(8,128)(2,1)S(1)}, u32[]{:S(2)}, u32[]{:S(2)}) collective-permute-start(bf16[400,128]{1,0:T(8,128)(2,1)S(1)} %get-tuple-element.39), channel_id=1, source_target_pairs={{0,22},{2,20},{4,18},{6,16},{8,30},{10,28},{12,26},{14,24},{16,6},... | collective-permute-start | bytes 307208 | tf_op jit(solution)/shard_map/ppermute | solution.py:317
  126.0 16.1 %collective-permute-start.33 = (bf16[400,128]{1,0:T(8,128)(2,1)S(1)}, bf16[400,128]{1,0:T(8,128)(2,1)S(1)}, u32[]{:S(2)}, u32[]{:S(2)}) collective-permute-start(bf16[400,128]{1,0:T(8,128)(2,1)S(1)} %get-tuple-element.40), channel_id=1, source_target_pairs={{0,30},{2,28},{4,26},{6,24},{8,22},{10,20},{12,18},{14,16},{16,14}... | collective-permute-start | bytes 307208 | tf_op jit(solution)/shard_map/ppermute | solution.py:317
  (16 other events, 121.6 us)

commit v6 on v5

--- a/solution.py
+++ b/solution.py
@@ -36,7 +36,7 @@
         out_shape=jax.ShapeDtypeStruct((4 * rows, columns), blocks[0].dtype),
         in_specs=[VMEM] * len(blocks) + [ANY] * len(earlier),
         out_specs=VMEM,
-        compiler_params=kernel_params(16),
+        compiler_params=kernel_params(10),
         cost_estimate=pl.CostEstimate(
             flops=0, bytes_accessed=16 * rows * columns, transcendentals=0
         ),
@@ -89,7 +89,7 @@
         in_specs=[SMEM] + [VMEM] * len(logits) + [ANY] * len(earlier),
         out_specs=VMEM,
         scratch_shapes=[pltpu.VMEM((2 * TILE, TILE), jnp.float32)],
-        compiler_params=kernel_params(32),
+        compiler_params=kernel_params(20),
         cost_estimate=pl.CostEstimate(
             flops=4 * rows * columns, bytes_accessed=10 * rows * columns, transcendentals=rows * columns
         ),
@@ -132,7 +132,7 @@
         in_specs=[SMEM, SMEM, VMEM, VMEM],
         out_specs=VMEM,
         scratch_shapes=[pltpu.SMEM((owners,), jnp.int32)],
-        compiler_params=kernel_params(32),
+        compiler_params=kernel_params(20),
         cost_estimate=pl.CostEstimate(
             flops=2 * entries * rows * TILE * TILE,
             bytes_accessed=4 * owners * size * TILE,
@@ -182,7 +182,7 @@
         in_specs=[SMEM, SMEM, VMEM, VMEM],
         out_specs=[VMEM] * owners,
         scratch_shapes=[pltpu.SMEM((owners,), jnp.int32)],
-        compiler_params=kernel_params(32),
+        compiler_params=kernel_params(20),
     )(me, pairs, tiles, focus_blocks)
 
 
@@ -267,7 +267,7 @@
                 pltpu.SemaphoreType.DMA,
             ],
         ),
-        compiler_params=kernel_params(40),
+        compiler_params=kernel_params(24),
         cost_estimate=pl.CostEstimate(
             flops=2 * senders * chunks * CAP * rows * TILE,
             bytes_accessed=4 * rows * chunks * STILES_DEV * TILE,
@@ -286,7 +286,7 @@
         out_shape=jax.ShapeDtypeStruct(x.shape, x.dtype),
         in_specs=[VMEM, ANY],
         out_specs=VMEM,
-        compiler_params=kernel_params(16),
+        compiler_params=kernel_params(10),
     )(x, earlier)
 
 
@@ -304,7 +304,7 @@
         out_shape=[jax.ShapeDtypeStruct((rows, columns // 2), left.dtype)] * 2,
         in_specs=[VMEM] * 2 + [ANY] * len(earlier),
         out_specs=[VMEM] * 2,
-        compiler_params=kernel_params(16),
+        compiler_params=kernel_params(10),
     )(left, right, *earlier)
 
 

time: 149 us -> 147 us (0.987)
  starting transfers between devices: 50.5 us -> 52.1 us
    ppermute x31, waiting for transfers between devices: 54.8 us -> 52.9 us  [swap(): return lax.ppermute(x, 'vocab', [(i, i ^ k) for i in range(vocab)])]
  transfers between devices with their start and end apart: 35 -> 35, of which waited for: 17 -> 19; matrix products, arithmetic and copies ran while one was open for 16% -> 16% of each run, Pallas kernels for 6% -> 6%
where the time goes in v6:
time: 147 us
  waiting for transfers between devices  53.4 us (36%)
  starting transfers between devices  52.1 us (35%)
  matrix products  17.7 us (12%)
  Pallas kernels  14.2 us (10%)
  local copies, waits for them, and re-layouts  8.45 us (6%)
    ppermute x31, waiting for transfers between devices, swap(): return lax.ppermute(x, 'vocab', [(i, i ^ k) for i in range(vocab)])  52.9 us
    ppermute x31, starting transfers between devices, swap(): return lax.ppermute(x, 'vocab', [(i, i ^ k) for i in range(vocab)])  42.1 us
    dot_general x4, matrix products, dot(): return jnp.dot(x, head_weight, preferred_element_type=jnp.float32)  17.7 us
    all_to_all x1, starting transfers between devices, exchange(): lax.all_to_all(sent, 'vocab', split_axis=0, concat_axis=0, tiled=True)  6.66 us
    unnamed x33, local copies, waits for them, and re-layouts  6.58 us
    pallas_call x1, Pallas kernels, sum_slots(): pl.pallas_call(functools.partial(sum_kernel, senders, place), out_shape=j...  5.36 us
    pallas_call x1, Pallas kernels, focus_each(): pl.pallas_call(functools.partial(focus_each_kernel, rows), out_shape=[jax...  4.5 us
    ppermute x2, starting transfers between devices, product(): return (logits, lax.ppermute(logits, ('vocab', 'hid'), pairs))  3.24 us
  transfers between devices with their start and end apart: 35, of which 19 were waited for; matrix products, arithmetic and copies ran while one was open for 16% of the time, Pallas kernels for 6%

profile of v6, /device:TPU:10, one launch (start us, length us, event | category | flops | bytes accessed | tf_op | source)
XLA Modules:
  0.0 146.5 jit_solution(11880947182800651120)
XLA Ops:
  1.5 2.6 %collective-permute-start = (bf16[48,4096]{1,0:T(8,128)(2,1)}, bf16[48,4096]{1,0:T(8,128)(2,1)S(1)}, u32[]{:S(2)}, u32[]{:S(2)}) collective-permute-start(bf16[48,4096]{1,0:T(8,128)(2,1)} %x_ref.3), channel_id=1, source_target_pairs={{0,16},{2,18},{4,20},{6,22},{8,24},{10,26},{12,28},{14,30},{16,0},... | collective-permute-start | bytes 1179656 | tf_op jit(solution)/shard_map/ppermute | solution.py:317
  6.8 4.3 %collective-permute-done.4.refs_2_ = bf16[48,4096]{1,0:T(8,128)(2,1)S(1)} collective-permute-done((bf16[48,4096]{1,0:T(8,128)(2,1)}, bf16[48,4096]{1,0:T(8,128)(2,1)S(1)}, u32[]{:S(2)}, u32[]{:S(2)}) %collective-permute-start.4) | collective-permute-done | bytes 393248 | tf_op jit(solution)/shard_map/ppermute | solution.py:317
  12.5 8.3 %collective-permute-done.earlier_ref.refs_0_ = bf16[48,4096]{1,0:T(8,128)(2,1)S(1)} collective-permute-done((bf16[48,4096]{1,0:T(8,128)(2,1)}, bf16[48,4096]{1,0:T(8,128)(2,1)S(1)}, u32[]{:S(2)}, u32[]{:S(2)}) %collective-permute-start) | collective-permute-done | bytes 393248 | tf_op jit(solution)/shard_map/ppermute | solution.py:317
  24.0 2.2 %collective-permute-done.5.refs_3_ = bf16[48,4096]{1,0:T(8,128)(2,1)S(1)} collective-permute-done((bf16[48,4096]{1,0:T(8,128)(2,1)S(1)}, bf16[48,4096]{1,0:T(8,128)(2,1)S(1)}, u32[]{:S(2)}, u32[]{:S(2)}) %collective-permute-start.5) | collective-permute-done | bytes 393248 | tf_op jit(solution)/shard_map/ppermute | solution.py:317
  26.4 6.3 %fusion.6.refs_0_.refs_2_ = f32[192,1280]{1,0:T(8,128)S(1)} fusion(bf16[192,4096]{1,0:T(8,128)(2,1)S(1)} %shard_map.47, bf16[4096,1280]{1,0:T(8,128)(2,1)} %param.5), kind=kOutput, calls=%fused_computation.17 | convolution fusion | flops 2013265920 | bytes 13041664 | tf_op jit(solution)/shard_map/dot_general | solution.py:320
  36.7 3.7 %collective-permute-done.9.refs_6_ = bf16[48,4096]{1,0:T(8,128)(2,1)S(1)} collective-permute-done((bf16[48,4096]{1,0:T(8,128)(2,1)S(1)}, bf16[48,4096]{1,0:T(8,128)(2,1)S(1)}, u32[]{:S(2)}, u32[]{:S(2)}) %collective-permute-start.9) | collective-permute-done | bytes 393248 | tf_op jit(solution)/shard_map/ppermute | solution.py:317
  43.1 2.2 %fusion.7.refs_0_ = f32[192,1280]{1,0:T(8,128)S(1)} fusion(bf16[192,4096]{1,0:T(8,128)(2,1)S(1)} %shard_map.50, bf16[4096,1280]{1,0:T(8,128)(2,1)S(1)} %bitcast.11), kind=kOutput, calls=%fused_computation.18 | convolution fusion | flops 2013265920 | bytes 13041664 | tf_op jit(solution)/shard_map/dot_general | solution.py:320
  45.4 5.5 %collective-permute-done.12 = bf16[48,4096]{1,0:T(8,128)(2,1)S(1)} collective-permute-done((bf16[48,4096]{1,0:T(8,128)(2,1)S(1)}, bf16[48,4096]{1,0:T(8,128)(2,1)S(1)}, u32[]{:S(2)}, u32[]{:S(2)}) %collective-permute-start.12) | collective-permute-done | bytes 393248 | tf_op jit(solution)/shard_map/ppermute | solution.py:317
  50.8 1.9 %collective-permute-start.10 = (f32[192,1280]{1,0:T(8,128)S(1)}, f32[192,1280]{1,0:T(8,128)S(1)}, u32[]{:S(2)}, u32[]{:S(2)}) collective-permute-start(f32[192,1280]{1,0:T(8,128)S(1)} %fusion.7.refs_0_), channel_id=1, source_target_pairs={{0,1},{2,3},{4,5},{6,7},{8,9},{10,11},{12,13},{14,15},{17,16},{19,... | collective-permute-start | bytes 2949128 | tf_op jit(solution)/shard_map/ppermute | solution.py:340
  56.0 2.1 %shard_map.52 = bf16[16,400,128]{2,1,0:T(8,128)(2,1)} custom-call(s32[1]{0:T(128)} %bitcast.me_ref, s32[32]{0:T(128)S(1)} %reshape.3.pair_ref, bf16[1936,128]{1,0:T(8,128)(2,1)S(1)} %shard_map.51.tiles_ref, bf16[16,128,128]{2,1,0:T(8,128)(2,1)S(1)} %copy-done.1), custom_call_target="tpu_custom_call" | custom-call | flops 100663296 | bytes 3276800 | tf_op jit(solution)/shard_map/pallas_call | solution.py:129
  58.1 6.7 %all-to-all-start = ((bf16[16,400,128]{2,1,0:T(8,128)(2,1)}), bf16[16,400,128]{2,1,0:T(8,128)(2,1)S(1)}, u32[]{:S(2)}, u32[]{:S(2)}) async-start(bf16[16,400,128]{2,1,0:T(8,128)(2,1)} %shard_map.52), calls=%async_computation | async-start | bytes 3276800 | tf_op jit(solution)/shard_map/all_to_all | solution.py:324
  65.5 1.9 %constant_dynamic-update-slice_fusion.5 = bf16[192,4096]{1,0:T(8,128)(2,1)} fusion(bf16[192,4096]{1,0:T(8,128)(2,1)} %constant_dynamic-update-slice_fusion.6, bf16[48,4096]{1,0:T(8,128)(2,1)} %collective-permute-done.16), kind=kLoop, calls=%fused_computation.12 | loop fusion | bytes 786432
  67.5 1.8 %constant_dynamic-update-slice_fusion.4 = bf16[192,4096]{1,0:T(8,128)(2,1)} fusion(bf16[192,4096]{1,0:T(8,128)(2,1)} %constant_dynamic-update-slice_fusion.5, bf16[48,4096]{1,0:T(8,128)(2,1)} %collective-permute-done.17), kind=kLoop, calls=%fused_computation.11 | loop fusion | bytes 786432 | tf_op jit(solution)/shard_map/concatenate | solution.py:343
  69.2 6.9 %fusion = f32[192,1280]{1,0:T(8,128)S(1)} fusion(bf16[4096,1280]{1,0:T(8,128)(2,1)} %param.5, bf16[192,4096]{1,0:T(8,128)(2,1)} %constant_dynamic-update-slice_fusion.4, bf16[192,4096]{1,0:T(8,128)(2,1)S(1)} %copy-done.6, pred[]{:T(512)S(6)} %eq.3), kind=kOutput, calls=%fused_computation | convolution fusion | flops 2014052352 | bytes 14614529 | tf_op jit(solution)/shard_map/dot_general | solution.py:320
  76.2 2.3 %fusion.2.refs_0_.refs_2_ = f32[192,1280]{1,0:T(8,128)S(1)} fusion(bf16[4096,1280]{1,0:T(8,128)(2,1)S(1)} %bitcast.13, bf16[192,4096]{1,0:T(8,128)(2,1)S(1)} %copy-done.6, bf16[192,4096]{1,0:T(8,128)(2,1)S(1)} %copy-done.4, pred[]{:T(512)S(6)} %eq.3), kind=kOutput, calls=%fused_computation.2 | convolution fusion | flops 2014052352 | bytes 14614529 | tf_op jit(solution)/shard_map/dot_general | solution.py:320
  79.9 4.5 %shard_map.54 = (bf16[400,128]{1,0:T(8,128)(2,1)S(1)}, bf16[400,128]{1,0:T(8,128)(2,1)S(1)}, bf16[400,128]{1,0:T(8,128)(2,1)S(1)}, bf16[400,128]{1,0:T(8,128)(2,...) custom-call(s32[1]{0:T(128)} %bitcast.me_ref, ...), custom_call_target="tpu_custom_call" | custom-call | tf_op jit(solution)/shard_map/pallas_call | solution.py:179
  87.7 2.5 %collective-permute-start.22 = (bf16[400,128]{1,0:T(8,128)(2,1)S(1)}, bf16[400,128]{1,0:T(8,128)(2,1)S(1)}, u32[]{:S(2)}, u32[]{:S(2)}) collective-permute-start(bf16[400,128]{1,0:T(8,128)(2,1)S(1)} %get-tuple-element.29), channel_id=1, source_target_pairs={{0,14},{2,12},{4,10},{6,8},{8,6},{10,4},{12,2},{14,0},{16,30},{18,... | collective-permute-start | bytes 307208 | tf_op jit(solution)/shard_map/ppermute | solution.py:317
  90.7 5.0 %collective-permute-done.19.refs_2_ = bf16[400,128]{1,0:T(8,128)(2,1)S(1)} collective-permute-done((bf16[400,128]{1,0:T(8,128)(2,1)S(1)}, bf16[400,128]{1,0:T(8,128)(2,1)S(1)}, u32[]{:S(2)}, u32[]{:S(2)}) %collective-permute-start.19) | collective-permute-done | bytes 102432 | tf_op jit(solution)/shard_map/ppermute | solution.py:317
  97.7 2.6 %collective-permute-start.25 = (bf16[400,128]{1,0:T(8,128)(2,1)}, bf16[400,128]{1,0:T(8,128)(2,1)S(1)}, u32[]{:S(2)}, u32[]{:S(2)}) collective-permute-start(bf16[400,128]{1,0:T(8,128)(2,1)} %get-tuple-element.32), channel_id=1, source_target_pairs={{0,6},{2,4},{4,2},{6,0},{8,14},{10,12},{12,10},{14,8},{16,22},{18,... | collective-permute-start | bytes 307208 | tf_op jit(solution)/shard_map/ppermute | solution.py:317
  101.8 3.8 %collective-permute-start.26 = (bf16[400,128]{1,0:T(8,128)(2,1)S(1)}, bf16[400,128]{1,0:T(8,128)(2,1)S(1)}, u32[]{:S(2)}, u32[]{:S(2)}) collective-permute-start(bf16[400,128]{1,0:T(8,128)(2,1)S(1)} %get-tuple-element.33), channel_id=1, source_target_pairs={{0,16},{2,18},{4,20},{6,22},{8,24},{10,26},{12,28},{14,30},{16,0},... | collective-permute-start | bytes 307208 | tf_op jit(solution)/shard_map/ppermute | solution.py:317
  105.6 1.9 %collective-permute-start.27 = (bf16[400,128]{1,0:T(8,128)(2,1)S(1)}, bf16[400,128]{1,0:T(8,128)(2,1)S(1)}, u32[]{:S(2)}, u32[]{:S(2)}) collective-permute-start(bf16[400,128]{1,0:T(8,128)(2,1)S(1)} %get-tuple-element.34), channel_id=1, source_target_pairs={{0,24},{2,26},{4,28},{6,30},{8,16},{10,18},{12,20},{14,22},{16,8},... | collective-permute-start | bytes 307208 | tf_op jit(solution)/shard_map/ppermute | solution.py:317
  107.5 2.5 %collective-permute-start.28 = (bf16[400,128]{1,0:T(8,128)(2,1)S(1)}, bf16[400,128]{1,0:T(8,128)(2,1)S(1)}, u32[]{:S(2)}, u32[]{:S(2)}) collective-permute-start(bf16[400,128]{1,0:T(8,128)(2,1)S(1)} %get-tuple-element.35), channel_id=1, source_target_pairs={{0,18},{2,16},{4,22},{6,20},{8,26},{10,24},{12,30},{14,28},{16,2},... | collective-permute-start | bytes 307208 | tf_op jit(solution)/shard_map/ppermute | solution.py:317
  111.4 2.1 %collective-permute-start.30 = (bf16[400,128]{1,0:T(8,128)(2,1)}, bf16[400,128]{1,0:T(8,128)(2,1)S(1)}, u32[]{:S(2)}, u32[]{:S(2)}) collective-permute-start(bf16[400,128]{1,0:T(8,128)(2,1)} %get-tuple-element.37), channel_id=1, source_target_pairs={{0,20},{2,22},{4,16},{6,18},{8,28},{10,30},{12,24},{14,26},{16,4},... | collective-permute-start | bytes 307208 | tf_op jit(solution)/shard_map/ppermute | solution.py:317
  113.5 6.2 %collective-permute-done.26.refs_9_ = bf16[400,128]{1,0:T(8,128)(2,1)S(1)} collective-permute-done((bf16[400,128]{1,0:T(8,128)(2,1)S(1)}, bf16[400,128]{1,0:T(8,128)(2,1)S(1)}, u32[]{:S(2)}, u32[]{:S(2)}) %collective-permute-start.26) | collective-permute-done | bytes 102432 | tf_op jit(solution)/shard_map/ppermute | solution.py:317
  119.8 2.2 %collective-permute-done.27.refs_10_ = bf16[400,128]{1,0:T(8,128)(2,1)S(1)} collective-permute-done((bf16[400,128]{1,0:T(8,128)(2,1)S(1)}, bf16[400,128]{1,0:T(8,128)(2,1)S(1)}, u32[]{:S(2)}, u32[]{:S(2)}) %collective-permute-start.27) | collective-permute-done | bytes 102432 | tf_op jit(solution)/shard_map/ppermute | solution.py:317
  122.0 2.7 %collective-permute-start.32 = (bf16[400,128]{1,0:T(8,128)(2,1)S(1)}, bf16[400,128]{1,0:T(8,128)(2,1)S(1)}, u32[]{:S(2)}, u32[]{:S(2)}) collective-permute-start(bf16[400,128]{1,0:T(8,128)(2,1)S(1)} %get-tuple-element.39), channel_id=1, source_target_pairs={{0,22},{2,20},{4,18},{6,16},{8,30},{10,28},{12,26},{14,24},{16,6},... | collective-permute-start | bytes 307208 | tf_op jit(solution)/shard_map/ppermute | solution.py:317
  125.2 3.3 %collective-permute-start.33 = (bf16[400,128]{1,0:T(8,128)(2,1)S(1)}, bf16[400,128]{1,0:T(8,128)(2,1)S(1)}, u32[]{:S(2)}, u32[]{:S(2)}) collective-permute-start(bf16[400,128]{1,0:T(8,128)(2,1)S(1)} %get-tuple-element.40), channel_id=1, source_target_pairs={{0,30},{2,28},{4,26},{6,24},{8,22},{10,20},{12,18},{14,16},{16,14}... | collective-permute-start | bytes 307208 | tf_op jit(solution)/shard_map/ppermute | solution.py:317
  128.6 2.3 %collective-permute-done.29.refs_12_ = bf16[400,128]{1,0:T(8,128)(2,1)S(1)} collective-permute-done((bf16[400,128]{1,0:T(8,128)(2,1)}, bf16[400,128]{1,0:T(8,128)(2,1)S(1)}, u32[]{:S(2)}, u32[]{:S(2)}) %collective-permute-start.29) | collective-permute-done | bytes 102432 | tf_op jit(solution)/shard_map/ppermute | solution.py:317
  130.9 3.3 %collective-permute-done.30.refs_13_ = bf16[400,128]{1,0:T(8,128)(2,1)S(1)} collective-permute-done((bf16[400,128]{1,0:T(8,128)(2,1)}, bf16[400,128]{1,0:T(8,128)(2,1)S(1)}, u32[]{:S(2)}, u32[]{:S(2)}) %collective-permute-start.30) | collective-permute-done | bytes 102432 | tf_op jit(solution)/shard_map/ppermute | solution.py:317
  134.1 2.4 %collective-permute-done.31.refs_14_ = bf16[400,128]{1,0:T(8,128)(2,1)S(1)} collective-permute-done((bf16[400,128]{1,0:T(8,128)(2,1)}, bf16[400,128]{1,0:T(8,128)(2,1)S(1)}, u32[]{:S(2)}, u32[]{:S(2)}) %collective-permute-start.31) | collective-permute-done | bytes 102432 | tf_op jit(solution)/shard_map/ppermute | solution.py:317
  138.1 2.9 %collective-permute-done.33.refs_16_ = bf16[400,128]{1,0:T(8,128)(2,1)S(1)} collective-permute-done((bf16[400,128]{1,0:T(8,128)(2,1)S(1)}, bf16[400,128]{1,0:T(8,128)(2,1)S(1)}, u32[]{:S(2)}, u32[]{:S(2)}) %collective-permute-start.33) | collective-permute-done | bytes 102432 | tf_op jit(solution)/shard_map/ppermute | solution.py:317
  141.0 5.4 %shard_map.55 = f32[384,1536]{1,0:T(8,128)} custom-call(s32[2]{0:T(128)S(1)} %pad_add_fusion.me_ref, bf16[16,400,128]{2,1,0:T(8,128)(2,1)S(1)} %all-to-all-done.refs_0_, bf16[400,128]{1,0:T(8,128)(2,1)S(1)} %get-tuple-element.25.refs_1_, bf16[400,128]{1,0:T(8,128)(2,1)S(1)} %collective-permute-done.19.refs_2_, ...), custom_call_target="tpu_custom_call" | custom-call | flops 3145728 | bytes 2359296 | tf_op jit(solution)/shard_map/pallas_call | solution.py:254
  (93 shorter events, 32.0 us)
Async XLA Ops:
  0.0 11.1 %collective-permute-start.4 = (bf16[48,4096]{1,0:T(8,128)(2,1)}, bf16[48,4096]{1,0:T(8,128)(2,1)S(1)}, u32[]{:S(2)}, u32[]{:S(2)}) collective-permute-start(bf16[48,4096]{1,0:T(8,128)(2,1)} %x_ref.3), channel_id=1, source_target_pairs={{0,4},{2,6},{4,0},{6,2},{8,12},{10,14},{12,8},{14,10},{16,20},{18,... | collective-permute-start | bytes 1179656 | tf_op jit(solution)/shard_map/ppermute | solution.py:317
  1.5 19.3 %collective-permute-start = (bf16[48,4096]{1,0:T(8,128)(2,1)}, bf16[48,4096]{1,0:T(8,128)(2,1)S(1)}, u32[]{:S(2)}, u32[]{:S(2)}) collective-permute-start(bf16[48,4096]{1,0:T(8,128)(2,1)} %x_ref.3), channel_id=1, source_target_pairs={{0,16},{2,18},{4,20},{6,22},{8,24},{10,26},{12,28},{14,30},{16,0},... | collective-permute-start | bytes 1179656 | tf_op jit(solution)/shard_map/ppermute | solution.py:317
  6.2 17.0 %collective-permute-start.3 = (bf16[48,4096]{1,0:T(8,128)(2,1)S(1)}, bf16[48,4096]{1,0:T(8,128)(2,1)S(1)}, u32[]{:S(2)}, u32[]{:S(2)}) collective-permute-start(bf16[48,4096]{1,0:T(8,128)(2,1)S(1)} %shard_map.46), channel_id=1, source_target_pairs={{0,2},{2,0},{4,6},{6,4},{8,10},{10,8},{12,14},{14,12},{16,18},{18,... | collective-permute-start | bytes 1179656 | tf_op jit(solution)/shard_map/ppermute | solution.py:317
  11.1 15.2 %collective-permute-start.5 = (bf16[48,4096]{1,0:T(8,128)(2,1)S(1)}, bf16[48,4096]{1,0:T(8,128)(2,1)S(1)}, u32[]{:S(2)}, u32[]{:S(2)}) collective-permute-start(bf16[48,4096]{1,0:T(8,128)(2,1)S(1)} %collective-permute-done.4.refs_2_), channel_id=1, source_target_pairs={{0,2},{2,0},{4,6},{6,4},{8,10},{10,8},{12,14},{14,12},{16,18},{18,... | collective-permute-start | bytes 1179656 | tf_op jit(solution)/shard_map/ppermute | solution.py:317
  20.9 14.3 %collective-permute-start.8 = (bf16[48,4096]{1,0:T(8,128)(2,1)S(1)}, bf16[48,4096]{1,0:T(8,128)(2,1)S(1)}, u32[]{:S(2)}, u32[]{:S(2)}) collective-permute-start(bf16[48,4096]{1,0:T(8,128)(2,1)S(1)} %shard_map.49), channel_id=1, source_target_pairs={{0,8},{2,10},{4,12},{6,14},{8,0},{10,2},{12,4},{14,6},{16,24},{18,... | collective-permute-start | bytes 1179656 | tf_op jit(solution)/shard_map/ppermute | solution.py:317
  22.2 11.8 %collective-permute-start.1 = (bf16[48,4096]{1,0:T(8,128)(2,1)S(1)}, bf16[48,4096]{1,0:T(8,128)(2,1)S(1)}, u32[]{:S(2)}, u32[]{:S(2)}) collective-permute-start(bf16[48,4096]{1,0:T(8,128)(2,1)S(1)} %collective-permute-done.earlier_ref.refs_0_), channel_id=1, source_target_pairs={{0,2},{2,0},{4,6},{6,4},{8,10},{10,8},{12,14},{14,12},{16,18},{18,... | collective-permute-start | bytes 1179656 | tf_op jit(solution)/shard_map/ppermute | solution.py:317
  22.7 11.3 %collective-permute-start.2 = (bf16[48,4096]{1,0:T(8,128)(2,1)S(1)}, bf16[48,4096]{1,0:T(8,128)(2,1)S(1)}, u32[]{:S(2)}, u32[]{:S(2)}) collective-permute-start(bf16[48,4096]{1,0:T(8,128)(2,1)S(1)} %collective-permute-done.earlier_ref.refs_0_), channel_id=1, source_target_pairs={{0,4},{2,6},{4,0},{6,2},{8,12},{10,14},{12,8},{14,10},{16,20},{18,... | collective-permute-start | bytes 1179656 | tf_op jit(solution)/shard_map/ppermute | solution.py:317
  23.2 17.2 %collective-permute-start.9 = (bf16[48,4096]{1,0:T(8,128)(2,1)S(1)}, bf16[48,4096]{1,0:T(8,128)(2,1)S(1)}, u32[]{:S(2)}, u32[]{:S(2)}) collective-permute-start(bf16[48,4096]{1,0:T(8,128)(2,1)S(1)} %collective-permute-done.earlier_ref.refs_0_), channel_id=1, source_target_pairs={{0,8},{2,10},{4,12},{6,14},{8,0},{10,2},{12,4},{14,6},{16,24},{18,... | collective-permute-start | bytes 1179656 | tf_op jit(solution)/shard_map/ppermute | solution.py:317
  32.7 21.9 %collective-permute-start.11 = (f32[192,1280]{1,0:T(8,128)S(1)}, f32[192,1280]{1,0:T(8,128)S(1)}, u32[]{:S(2)}, u32[]{:S(2)}) collective-permute-start(f32[192,1280]{1,0:T(8,128)S(1)} %fusion.6.refs_0_.refs_2_), channel_id=1, source_target_pairs={{1,0},{3,2},{5,4},{7,6},{9,8},{11,10},{13,12},{15,14},{16,17},{18,... | collective-permute-start | bytes 2949128 | tf_op jit(solution)/shard_map/ppermute | solution.py:340
  34.6 7.8 %collective-permute-start.7 = (bf16[48,2048]{1,0:T(8,128)(2,1)S(1)}, bf16[48,2048]{1,0:T(8,128)(2,1)S(1)}, u32[]{:S(2)}, u32[]{:S(2)}) collective-permute-start(bf16[48,2048]{1,0:T(8,128)(2,1)S(1)} %get-tuple-element.24), channel_id=1, source_target_pairs={{0,2},{2,0},{4,6},{6,4},{8,10},{10,8},{12,14},{14,12},{16,18},{18,... | collective-permute-start | bytes 589832 | tf_op jit(solution)/shard_map/ppermute | solution.py:317
  35.2 15.7 %collective-permute-start.12 = (bf16[48,4096]{1,0:T(8,128)(2,1)S(1)}, bf16[48,4096]{1,0:T(8,128)(2,1)S(1)}, u32[]{:S(2)}, u32[]{:S(2)}) collective-permute-start(bf16[48,4096]{1,0:T(8,128)(2,1)S(1)} %collective-permute-done.8.refs_5_), channel_id=1, source_target_pairs={{0,2},{2,0},{4,6},{6,4},{8,10},{10,8},{12,14},{14,12},{16,18},{18,... | collective-permute-start | bytes 1179656 | tf_op jit(solution)/shard_map/ppermute | solution.py:317
  40.4 12.4 %collective-permute-start.13 = (bf16[48,4096]{1,0:T(8,128)(2,1)S(1)}, bf16[48,4096]{1,0:T(8,128)(2,1)S(1)}, u32[]{:S(2)}, u32[]{:S(2)}) collective-permute-start(bf16[48,4096]{1,0:T(8,128)(2,1)S(1)} %collective-permute-done.8.refs_5_), channel_id=1, source_target_pairs={{0,4},{2,6},{4,0},{6,2},{8,12},{10,14},{12,8},{14,10},{16,20},{18,... | collective-permute-start | bytes 1179656 | tf_op jit(solution)/shard_map/ppermute | solution.py:317
  41.7 12.8 %collective-permute-start.14 = (bf16[48,4096]{1,0:T(8,128)(2,1)S(1)}, bf16[48,4096]{1,0:T(8,128)(2,1)S(1)}, u32[]{:S(2)}, u32[]{:S(2)}) collective-permute-start(bf16[48,4096]{1,0:T(8,128)(2,1)S(1)} %collective-permute-done.5.refs_3_), channel_id=1, source_target_pairs={{0,8},{2,10},{4,12},{6,14},{8,0},{10,2},{12,4},{14,6},{16,24},{18,... | collective-permute-start | bytes 1179656 | tf_op jit(solution)/shard_map/ppermute | solution.py:317
  42.4 22.3 %collective-permute-start.15 = (bf16[48,4096]{1,0:T(8,128)(2,1)S(1)}, bf16[48,4096]{1,0:T(8,128)(2,1)S(1)}, u32[]{:S(2)}, u32[]{:S(2)}) collective-permute-start(bf16[48,4096]{1,0:T(8,128)(2,1)S(1)} %collective-permute-done.9.refs_6_), channel_id=1, source_target_pairs={{0,2},{2,0},{4,6},{6,4},{8,10},{10,8},{12,14},{14,12},{16,18},{18,... | collective-permute-start | bytes 1179656 | tf_op jit(solution)/shard_map/ppermute | solution.py:317
  52.8 12.7 %collective-permute-start.16 = (bf16[48,4096]{1,0:T(8,128)(2,1)S(1)}, bf16[48,4096]{1,0:T(8,128)(2,1)}, u32[]{:S(2)}, u32[]{:S(2)}) collective-permute-start(bf16[48,4096]{1,0:T(8,128)(2,1)S(1)} %collective-permute-done.9.refs_6_), channel_id=1, source_target_pairs={{0,4},{2,6},{4,0},{6,2},{8,12},{10,14},{12,8},{14,10},{16,20},{18,... | collective-permute-start | bytes 1179656 | tf_op jit(solution)/shard_map/ppermute | solution.py:317
  54.5 13.0 %collective-permute-start.17 = (bf16[48,4096]{1,0:T(8,128)(2,1)S(1)}, bf16[48,4096]{1,0:T(8,128)(2,1)}, u32[]{:S(2)}, u32[]{:S(2)}) collective-permute-start(bf16[48,4096]{1,0:T(8,128)(2,1)S(1)} %pad_maximum_fusion), channel_id=1, source_target_pairs={{0,8},{2,10},{4,12},{6,14},{8,0},{10,2},{12,4},{14,6},{16,24},{18,... | collective-permute-start | bytes 1179656 | tf_op jit(solution)/shard_map/ppermute | solution.py:317
  58.1 82.9 %all-to-all-start = ((bf16[16,400,128]{2,1,0:T(8,128)(2,1)}), bf16[16,400,128]{2,1,0:T(8,128)(2,1)S(1)}, u32[]{:S(2)}, u32[]{:S(2)}) async-start(bf16[16,400,128]{2,1,0:T(8,128)(2,1)} %shard_map.52), calls=%async_computation | async-start | bytes 3276800 | tf_op jit(solution)/shard_map/all_to_all | solution.py:324
  84.3 11.4 %collective-permute-start.19 = (bf16[400,128]{1,0:T(8,128)(2,1)S(1)}, bf16[400,128]{1,0:T(8,128)(2,1)S(1)}, u32[]{:S(2)}, u32[]{:S(2)}) collective-permute-start(bf16[400,128]{1,0:T(8,128)(2,1)S(1)} %get-tuple-element.26), channel_id=1, source_target_pairs={{0,8},{2,10},{4,12},{6,14},{8,0},{10,2},{12,4},{14,6},{16,24},{18,... | collective-permute-start | bytes 307208 | tf_op jit(solution)/shard_map/ppermute | solution.py:317
  84.8 12.9 %collective-permute-start.20 = (bf16[400,128]{1,0:T(8,128)(2,1)S(1)}, bf16[400,128]{1,0:T(8,128)(2,1)S(1)}, u32[]{:S(2)}, u32[]{:S(2)}) collective-permute-start(bf16[400,128]{1,0:T(8,128)(2,1)S(1)} %get-tuple-element.27), channel_id=1, source_target_pairs={{0,10},{2,8},{4,14},{6,12},{8,2},{10,0},{12,6},{14,4},{16,26},{18,... | collective-permute-start | bytes 307208 | tf_op jit(solution)/shard_map/ppermute | solution.py:317
  86.4 15.5 %collective-permute-start.21 = (bf16[400,128]{1,0:T(8,128)(2,1)S(1)}, bf16[400,128]{1,0:T(8,128)(2,1)S(1)}, u32[]{:S(2)}, u32[]{:S(2)}) collective-permute-start(bf16[400,128]{1,0:T(8,128)(2,1)S(1)} %get-tuple-element.28), channel_id=1, source_target_pairs={{0,12},{2,14},{4,8},{6,10},{8,4},{10,6},{12,0},{14,2},{16,28},{18,... | collective-permute-start | bytes 307208 | tf_op jit(solution)/shard_map/ppermute | solution.py:317
  87.7 17.9 %collective-permute-start.22 = (bf16[400,128]{1,0:T(8,128)(2,1)S(1)}, bf16[400,128]{1,0:T(8,128)(2,1)S(1)}, u32[]{:S(2)}, u32[]{:S(2)}) collective-permute-start(bf16[400,128]{1,0:T(8,128)(2,1)S(1)} %get-tuple-element.29), channel_id=1, source_target_pairs={{0,14},{2,12},{4,10},{6,8},{8,6},{10,4},{12,2},{14,0},{16,30},{18,... | collective-permute-start | bytes 307208 | tf_op jit(solution)/shard_map/ppermute | solution.py:317
  90.2 17.3 %collective-permute-start.23 = (bf16[400,128]{1,0:T(8,128)(2,1)S(1)}, bf16[400,128]{1,0:T(8,128)(2,1)S(1)}, u32[]{:S(2)}, u32[]{:S(2)}) collective-permute-start(bf16[400,128]{1,0:T(8,128)(2,1)S(1)} %get-tuple-element.30), channel_id=1, source_target_pairs={{0,2},{2,0},{4,6},{6,4},{8,10},{10,8},{12,14},{14,12},{16,18},{18,... | collective-permute-start | bytes 307208 | tf_op jit(solution)/shard_map/ppermute | solution.py:317
  95.7 14.3 %collective-permute-start.24 = (bf16[400,128]{1,0:T(8,128)(2,1)S(1)}, bf16[400,128]{1,0:T(8,128)(2,1)S(1)}, u32[]{:S(2)}, u32[]{:S(2)}) collective-permute-start(bf16[400,128]{1,0:T(8,128)(2,1)S(1)} %get-tuple-element.31), channel_id=1, source_target_pairs={{0,4},{2,6},{4,0},{6,2},{8,12},{10,14},{12,8},{14,10},{16,20},{18,... | collective-permute-start | bytes 307208 | tf_op jit(solution)/shard_map/ppermute | solution.py:317
  97.7 13.7 %collective-permute-start.25 = (bf16[400,128]{1,0:T(8,128)(2,1)}, bf16[400,128]{1,0:T(8,128)(2,1)S(1)}, u32[]{:S(2)}, u32[]{:S(2)}) collective-permute-start(bf16[400,128]{1,0:T(8,128)(2,1)} %get-tuple-element.32), channel_id=1, source_target_pairs={{0,6},{2,4},{4,2},{6,0},{8,14},{10,12},{12,10},{14,8},{16,22},{18,... | collective-permute-start | bytes 307208 | tf_op jit(solution)/shard_map/ppermute | solution.py:317
  101.8 17.9 %collective-permute-start.26 = (bf16[400,128]{1,0:T(8,128)(2,1)S(1)}, bf16[400,128]{1,0:T(8,128)(2,1)S(1)}, u32[]{:S(2)}, u32[]{:S(2)}) collective-permute-start(bf16[400,128]{1,0:T(8,128)(2,1)S(1)} %get-tuple-element.33), channel_id=1, source_target_pairs={{0,16},{2,18},{4,20},{6,22},{8,24},{10,26},{12,28},{14,30},{16,0},... | collective-permute-start | bytes 307208 | tf_op jit(solution)/shard_map/ppermute | solution.py:317
  105.6 16.3 %collective-permute-start.27 = (bf16[400,128]{1,0:T(8,128)(2,1)S(1)}, bf16[400,128]{1,0:T(8,128)(2,1)S(1)}, u32[]{:S(2)}, u32[]{:S(2)}) collective-permute-start(bf16[400,128]{1,0:T(8,128)(2,1)S(1)} %get-tuple-element.34), channel_id=1, source_target_pairs={{0,24},{2,26},{4,28},{6,30},{8,16},{10,18},{12,20},{14,22},{16,8},... | collective-permute-start | bytes 307208 | tf_op jit(solution)/shard_map/ppermute | solution.py:317
  107.5 17.7 %collective-permute-start.28 = (bf16[400,128]{1,0:T(8,128)(2,1)S(1)}, bf16[400,128]{1,0:T(8,128)(2,1)S(1)}, u32[]{:S(2)}, u32[]{:S(2)}) collective-permute-start(bf16[400,128]{1,0:T(8,128)(2,1)S(1)} %get-tuple-element.35), channel_id=1, source_target_pairs={{0,18},{2,16},{4,22},{6,20},{8,26},{10,24},{12,30},{14,28},{16,2},... | collective-permute-start | bytes 307208 | tf_op jit(solution)/shard_map/ppermute | solution.py:317
  110.0 20.8 %collective-permute-start.29 = (bf16[400,128]{1,0:T(8,128)(2,1)}, bf16[400,128]{1,0:T(8,128)(2,1)S(1)}, u32[]{:S(2)}, u32[]{:S(2)}) collective-permute-start(bf16[400,128]{1,0:T(8,128)(2,1)} %get-tuple-element.36), channel_id=1, source_target_pairs={{0,26},{2,24},{4,30},{6,28},{8,18},{10,16},{12,22},{14,20},{16,10}... | collective-permute-start | bytes 307208 | tf_op jit(solution)/shard_map/ppermute | solution.py:317
  111.4 22.7 %collective-permute-start.30 = (bf16[400,128]{1,0:T(8,128)(2,1)}, bf16[400,128]{1,0:T(8,128)(2,1)S(1)}, u32[]{:S(2)}, u32[]{:S(2)}) collective-permute-start(bf16[400,128]{1,0:T(8,128)(2,1)} %get-tuple-element.37), channel_id=1, source_target_pairs={{0,20},{2,22},{4,16},{6,18},{8,28},{10,30},{12,24},{14,26},{16,4},... | collective-permute-start | bytes 307208 | tf_op jit(solution)/shard_map/ppermute | solution.py:317
  119.8 16.8 %collective-permute-start.31 = (bf16[400,128]{1,0:T(8,128)(2,1)}, bf16[400,128]{1,0:T(8,128)(2,1)S(1)}, u32[]{:S(2)}, u32[]{:S(2)}) collective-permute-start(bf16[400,128]{1,0:T(8,128)(2,1)} %get-tuple-element.38), channel_id=1, source_target_pairs={{0,28},{2,30},{4,24},{6,26},{8,20},{10,22},{12,16},{14,18},{16,12}... | collective-permute-start | bytes 307208 | tf_op jit(solution)/shard_map/ppermute | solution.py:317
  122.0 16.2 %collective-permute-start.32 = (bf16[400,128]{1,0:T(8,128)(2,1)S(1)}, bf16[400,128]{1,0:T(8,128)(2,1)S(1)}, u32[]{:S(2)}, u32[]{:S(2)}) collective-permute-start(bf16[400,128]{1,0:T(8,128)(2,1)S(1)} %get-tuple-element.39), channel_id=1, source_target_pairs={{0,22},{2,20},{4,18},{6,16},{8,30},{10,28},{12,26},{14,24},{16,6},... | collective-permute-start | bytes 307208 | tf_op jit(solution)/shard_map/ppermute | solution.py:317
  125.2 15.8 %collective-permute-start.33 = (bf16[400,128]{1,0:T(8,128)(2,1)S(1)}, bf16[400,128]{1,0:T(8,128)(2,1)S(1)}, u32[]{:S(2)}, u32[]{:S(2)}) collective-permute-start(bf16[400,128]{1,0:T(8,128)(2,1)S(1)} %get-tuple-element.40), channel_id=1, source_target_pairs={{0,30},{2,28},{4,26},{6,24},{8,22},{10,20},{12,18},{14,16},{16,14}... | collective-permute-start | bytes 307208 | tf_op jit(solution)/shard_map/ppermute | solution.py:317
  (16 other events, 120.1 us)

commit v7 on v6

--- a/solution.py
+++ b/solution.py
@@ -12,7 +12,7 @@
 CAP = 2
 STATS = 16
 LABEL_ROW = 6
-SENT = (0, 4, 5, 6, 7, 1, 2, 3, 8, 12, 9, 13, 10, 14, 11, 15)
+SENT = (0, 4, 5, 6, 7, 1, 8, 12, 2, 9, 13, 3, 10, 14, 11, 15)
 VMEM = pl.BlockSpec(memory_space=pltpu.VMEM)
 SMEM = pl.BlockSpec(memory_space=pltpu.SMEM)
 ANY = pl.BlockSpec(memory_space=pl.ANY)

time: 147 us -> 147 us (level)
  starting transfers between devices: 52.1 us -> 59.3 us
  waiting for transfers between devices: 53.4 us -> 46.3 us
    ppermute x31, starting transfers between devices: 42.1 us -> 49.3 us  [swap(): return lax.ppermute(x, 'vocab', [(i, i ^ k) for i in range(vocab)])]
    ppermute x31, waiting for transfers between devices: 52.9 us -> 45.8 us  [swap(): return lax.ppermute(x, 'vocab', [(i, i ^ k) for i in range(vocab)])]
  transfers between devices with their start and end apart: 35 -> 35, of which waited for: 19 -> 16; matrix products, arithmetic and copies ran while one was open for 16% -> 16% of each run, Pallas kernels for 6% -> 6%
where the time goes in v7:
time: 147 us; the launch traced here: 146 us
  starting transfers between devices  59.3 us (40%)
  waiting for transfers between devices  46.3 us (31%)
  matrix products  17.7 us (12%)
  Pallas kernels  13.5 us (9%)
  local copies, waits for them, and re-layouts  8.45 us (6%)
    ppermute x31, starting transfers between devices, swap(): return lax.ppermute(x, 'vocab', [(i, i ^ k) for i in range(vocab)])  49.3 us
    ppermute x31, waiting for transfers between devices, swap(): return lax.ppermute(x, 'vocab', [(i, i ^ k) for i in range(vocab)])  45.8 us
    dot_general x4, matrix products, dot(): return jnp.dot(x, head_weight, preferred_element_type=jnp.float32)  17.7 us
    all_to_all x1, starting transfers between devices, exchange(): lax.all_to_all(sent, 'vocab', split_axis=0, concat_axis=0, tiled=True)  6.66 us
    unnamed x33, local copies, waits for them, and re-layouts  6.58 us
    pallas_call x1, Pallas kernels, sum_slots(): pl.pallas_call(functools.partial(sum_kernel, senders, place), out_shape=j...  4.93 us
    pallas_call x1, Pallas kernels, focus_each(): pl.pallas_call(functools.partial(focus_each_kernel, rows), out_shape=[jax...  4.21 us
    ppermute x2, starting transfers between devices, product(): return (logits, lax.ppermute(logits, ('vocab', 'hid'), pairs))  3.24 us
  transfers between devices with their start and end apart: 35, of which 16 were waited for; matrix products, arithmetic and copies ran while one was open for 16% of the time, Pallas kernels for 6%

profile of v7, /device:TPU:10, one launch (start us, length us, event | category | flops | bytes accessed | tf_op | source)
XLA Modules:
  0.0 145.9 jit_solution(14845882097815429185)
XLA Ops:
  1.5 2.6 %collective-permute-start = (bf16[48,4096]{1,0:T(8,128)(2,1)}, bf16[48,4096]{1,0:T(8,128)(2,1)S(1)}, u32[]{:S(2)}, u32[]{:S(2)}) collective-permute-start(bf16[48,4096]{1,0:T(8,128)(2,1)} %x_ref.3), channel_id=1, source_target_pairs={{0,16},{2,18},{4,20},{6,22},{8,24},{10,26},{12,28},{14,30},{16,0},... | collective-permute-start | bytes 1179656 | tf_op jit(solution)/shard_map/ppermute | solution.py:317
  6.8 4.3 %collective-permute-done.4.refs_2_ = bf16[48,4096]{1,0:T(8,128)(2,1)S(1)} collective-permute-done((bf16[48,4096]{1,0:T(8,128)(2,1)}, bf16[48,4096]{1,0:T(8,128)(2,1)S(1)}, u32[]{:S(2)}, u32[]{:S(2)}) %collective-permute-start.4) | collective-permute-done | bytes 393248 | tf_op jit(solution)/shard_map/ppermute | solution.py:317
  12.5 8.3 %collective-permute-done.earlier_ref.refs_0_ = bf16[48,4096]{1,0:T(8,128)(2,1)S(1)} collective-permute-done((bf16[48,4096]{1,0:T(8,128)(2,1)}, bf16[48,4096]{1,0:T(8,128)(2,1)S(1)}, u32[]{:S(2)}, u32[]{:S(2)}) %collective-permute-start) | collective-permute-done | bytes 393248 | tf_op jit(solution)/shard_map/ppermute | solution.py:317
  24.0 2.2 %collective-permute-done.5.refs_3_ = bf16[48,4096]{1,0:T(8,128)(2,1)S(1)} collective-permute-done((bf16[48,4096]{1,0:T(8,128)(2,1)S(1)}, bf16[48,4096]{1,0:T(8,128)(2,1)S(1)}, u32[]{:S(2)}, u32[]{:S(2)}) %collective-permute-start.5) | collective-permute-done | bytes 393248 | tf_op jit(solution)/shard_map/ppermute | solution.py:317
  26.4 6.3 %fusion.6.refs_0_.refs_2_ = f32[192,1280]{1,0:T(8,128)S(1)} fusion(bf16[192,4096]{1,0:T(8,128)(2,1)S(1)} %shard_map.47, bf16[4096,1280]{1,0:T(8,128)(2,1)} %param.5), kind=kOutput, calls=%fused_computation.17 | convolution fusion | flops 2013265920 | bytes 13041664 | tf_op jit(solution)/shard_map/dot_general | solution.py:320
  36.7 3.7 %collective-permute-done.9.refs_6_ = bf16[48,4096]{1,0:T(8,128)(2,1)S(1)} collective-permute-done((bf16[48,4096]{1,0:T(8,128)(2,1)S(1)}, bf16[48,4096]{1,0:T(8,128)(2,1)S(1)}, u32[]{:S(2)}, u32[]{:S(2)}) %collective-permute-start.9) | collective-permute-done | bytes 393248 | tf_op jit(solution)/shard_map/ppermute | solution.py:317
  43.1 2.2 %fusion.7.refs_0_ = f32[192,1280]{1,0:T(8,128)S(1)} fusion(bf16[192,4096]{1,0:T(8,128)(2,1)S(1)} %shard_map.50, bf16[4096,1280]{1,0:T(8,128)(2,1)S(1)} %bitcast.11), kind=kOutput, calls=%fused_computation.18 | convolution fusion | flops 2013265920 | bytes 13041664 | tf_op jit(solution)/shard_map/dot_general | solution.py:320
  45.4 5.5 %collective-permute-done.12 = bf16[48,4096]{1,0:T(8,128)(2,1)S(1)} collective-permute-done((bf16[48,4096]{1,0:T(8,128)(2,1)S(1)}, bf16[48,4096]{1,0:T(8,128)(2,1)S(1)}, u32[]{:S(2)}, u32[]{:S(2)}) %collective-permute-start.12) | collective-permute-done | bytes 393248 | tf_op jit(solution)/shard_map/ppermute | solution.py:317
  50.8 1.9 %collective-permute-start.10 = (f32[192,1280]{1,0:T(8,128)S(1)}, f32[192,1280]{1,0:T(8,128)S(1)}, u32[]{:S(2)}, u32[]{:S(2)}) collective-permute-start(f32[192,1280]{1,0:T(8,128)S(1)} %fusion.7.refs_0_), channel_id=1, source_target_pairs={{0,1},{2,3},{4,5},{6,7},{8,9},{10,11},{12,13},{14,15},{17,16},{19,... | collective-permute-start | bytes 2949128 | tf_op jit(solution)/shard_map/ppermute | solution.py:340
  52.8 1.6 %collective-permute-start.16 = (bf16[48,4096]{1,0:T(8,128)(2,1)S(1)}, bf16[48,4096]{1,0:T(8,128)(2,1)}, u32[]{:S(2)}, u32[]{:S(2)}) collective-permute-start(bf16[48,4096]{1,0:T(8,128)(2,1)S(1)} %collective-permute-done.9.refs_6_), channel_id=1, source_target_pairs={{0,4},{2,6},{4,0},{6,2},{8,12},{10,14},{12,8},{14,10},{16,20},{18,... | collective-permute-start | bytes 1179656 | tf_op jit(solution)/shard_map/ppermute | solution.py:317
  56.0 2.1 %shard_map.52 = bf16[16,400,128]{2,1,0:T(8,128)(2,1)} custom-call(s32[1]{0:T(128)} %bitcast.me_ref, s32[32]{0:T(128)S(1)} %reshape.3.pair_ref, bf16[1936,128]{1,0:T(8,128)(2,1)S(1)} %shard_map.51.tiles_ref, bf16[16,128,128]{2,1,0:T(8,128)(2,1)S(1)} %copy-done.1), custom_call_target="tpu_custom_call" | custom-call | flops 100663296 | bytes 3276800 | tf_op jit(solution)/shard_map/pallas_call | solution.py:129
  58.1 6.7 %all-to-all-start = ((bf16[16,400,128]{2,1,0:T(8,128)(2,1)}), bf16[16,400,128]{2,1,0:T(8,128)(2,1)S(1)}, u32[]{:S(2)}, u32[]{:S(2)}) async-start(bf16[16,400,128]{2,1,0:T(8,128)(2,1)} %shard_map.52), calls=%async_computation | async-start | bytes 3276800 | tf_op jit(solution)/shard_map/all_to_all | solution.py:324
  65.5 1.9 %constant_dynamic-update-slice_fusion.5 = bf16[192,4096]{1,0:T(8,128)(2,1)} fusion(bf16[192,4096]{1,0:T(8,128)(2,1)} %constant_dynamic-update-slice_fusion.6, bf16[48,4096]{1,0:T(8,128)(2,1)} %collective-permute-done.16), kind=kLoop, calls=%fused_computation.12 | loop fusion | bytes 786432
  67.5 1.8 %constant_dynamic-update-slice_fusion.4 = bf16[192,4096]{1,0:T(8,128)(2,1)} fusion(bf16[192,4096]{1,0:T(8,128)(2,1)} %constant_dynamic-update-slice_fusion.5, bf16[48,4096]{1,0:T(8,128)(2,1)} %collective-permute-done.17), kind=kLoop, calls=%fused_computation.11 | loop fusion | bytes 786432 | tf_op jit(solution)/shard_map/concatenate | solution.py:343
  69.2 6.9 %fusion = f32[192,1280]{1,0:T(8,128)S(1)} fusion(bf16[4096,1280]{1,0:T(8,128)(2,1)} %param.5, bf16[192,4096]{1,0:T(8,128)(2,1)} %constant_dynamic-update-slice_fusion.4, bf16[192,4096]{1,0:T(8,128)(2,1)S(1)} %copy-done.6, pred[]{:T(512)S(6)} %eq.3), kind=kOutput, calls=%fused_computation | convolution fusion | flops 2014052352 | bytes 14614529 | tf_op jit(solution)/shard_map/dot_general | solution.py:320
  76.2 2.3 %fusion.2.refs_0_.refs_2_ = f32[192,1280]{1,0:T(8,128)S(1)} fusion(bf16[4096,1280]{1,0:T(8,128)(2,1)S(1)} %bitcast.13, bf16[192,4096]{1,0:T(8,128)(2,1)S(1)} %copy-done.6, bf16[192,4096]{1,0:T(8,128)(2,1)S(1)} %copy-done.4, pred[]{:T(512)S(6)} %eq.3), kind=kOutput, calls=%fused_computation.2 | convolution fusion | flops 2014052352 | bytes 14614529 | tf_op jit(solution)/shard_map/dot_general | solution.py:320
  79.9 4.2 %shard_map.54 = (bf16[400,128]{1,0:T(8,128)(2,1)S(1)}, bf16[400,128]{1,0:T(8,128)(2,1)S(1)}, bf16[400,128]{1,0:T(8,128)(2,1)S(1)}, bf16[400,128]{1,0:T(8,128)(2,...) custom-call(s32[1]{0:T(128)} %bitcast.me_ref, ...), custom_call_target="tpu_custom_call" | custom-call | tf_op jit(solution)/shard_map/pallas_call | solution.py:179
  84.8 1.7 %collective-permute-start.20 = (bf16[400,128]{1,0:T(8,128)(2,1)S(1)}, bf16[400,128]{1,0:T(8,128)(2,1)S(1)}, u32[]{:S(2)}, u32[]{:S(2)}) collective-permute-start(bf16[400,128]{1,0:T(8,128)(2,1)S(1)} %get-tuple-element.27), channel_id=1, source_target_pairs={{0,10},{2,8},{4,14},{6,12},{8,2},{10,0},{12,6},{14,4},{16,26},{18,... | collective-permute-start | bytes 307208 | tf_op jit(solution)/shard_map/ppermute | solution.py:317
  87.9 2.0 %collective-permute-start.22 = (bf16[400,128]{1,0:T(8,128)(2,1)S(1)}, bf16[400,128]{1,0:T(8,128)(2,1)S(1)}, u32[]{:S(2)}, u32[]{:S(2)}) collective-permute-start(bf16[400,128]{1,0:T(8,128)(2,1)S(1)} %get-tuple-element.29), channel_id=1, source_target_pairs={{0,14},{2,12},{4,10},{6,8},{8,6},{10,4},{12,2},{14,0},{16,30},{18,... | collective-permute-start | bytes 307208 | tf_op jit(solution)/shard_map/ppermute | solution.py:317
  90.8 4.9 %collective-permute-done.19.refs_2_ = bf16[400,128]{1,0:T(8,128)(2,1)S(1)} collective-permute-done((bf16[400,128]{1,0:T(8,128)(2,1)S(1)}, bf16[400,128]{1,0:T(8,128)(2,1)S(1)}, u32[]{:S(2)}, u32[]{:S(2)}) %collective-permute-start.19) | collective-permute-done | bytes 102432 | tf_op jit(solution)/shard_map/ppermute | solution.py:317
  97.7 3.3 %collective-permute-start.25 = (bf16[400,128]{1,0:T(8,128)(2,1)}, bf16[400,128]{1,0:T(8,128)(2,1)S(1)}, u32[]{:S(2)}, u32[]{:S(2)}) collective-permute-start(bf16[400,128]{1,0:T(8,128)(2,1)} %get-tuple-element.32), channel_id=1, source_target_pairs={{0,24},{2,26},{4,28},{6,30},{8,16},{10,18},{12,20},{14,22},{16,8},... | collective-permute-start | bytes 307208 | tf_op jit(solution)/shard_map/ppermute | solution.py:317
  102.9 1.5 %collective-permute-done.22.refs_5_ = bf16[400,128]{1,0:T(8,128)(2,1)S(1)} collective-permute-done((bf16[400,128]{1,0:T(8,128)(2,1)S(1)}, bf16[400,128]{1,0:T(8,128)(2,1)S(1)}, u32[]{:S(2)}, u32[]{:S(2)}) %collective-permute-start.22) | collective-permute-done | bytes 102432 | tf_op jit(solution)/shard_map/ppermute | solution.py:317
  104.4 6.1 %collective-permute-start.27 = (bf16[400,128]{1,0:T(8,128)(2,1)S(1)}, bf16[400,128]{1,0:T(8,128)(2,1)S(1)}, u32[]{:S(2)}, u32[]{:S(2)}) collective-permute-start(bf16[400,128]{1,0:T(8,128)(2,1)S(1)} %get-tuple-element.34), channel_id=1, source_target_pairs={{0,18},{2,16},{4,22},{6,20},{8,26},{10,24},{12,30},{14,28},{16,2},... | collective-permute-start | bytes 307208 | tf_op jit(solution)/shard_map/ppermute | solution.py:317
  110.5 3.5 %collective-permute-start.29 = (bf16[400,128]{1,0:T(8,128)(2,1)}, bf16[400,128]{1,0:T(8,128)(2,1)S(1)}, u32[]{:S(2)}, u32[]{:S(2)}) collective-permute-start(bf16[400,128]{1,0:T(8,128)(2,1)} %get-tuple-element.36), channel_id=1, source_target_pairs={{0,6},{2,4},{4,2},{6,0},{8,14},{10,12},{12,10},{14,8},{16,22},{18,... | collective-permute-start | bytes 307208 | tf_op jit(solution)/shard_map/ppermute | solution.py:317
  114.0 3.2 %collective-permute-done.25.refs_8_ = bf16[400,128]{1,0:T(8,128)(2,1)S(1)} collective-permute-done((bf16[400,128]{1,0:T(8,128)(2,1)}, bf16[400,128]{1,0:T(8,128)(2,1)S(1)}, u32[]{:S(2)}, u32[]{:S(2)}) %collective-permute-start.25) | collective-permute-done | bytes 102432 | tf_op jit(solution)/shard_map/ppermute | solution.py:317
  117.2 4.8 %collective-permute-start.31 = (bf16[400,128]{1,0:T(8,128)(2,1)}, bf16[400,128]{1,0:T(8,128)(2,1)S(1)}, u32[]{:S(2)}, u32[]{:S(2)}) collective-permute-start(bf16[400,128]{1,0:T(8,128)(2,1)} %get-tuple-element.38), channel_id=1, source_target_pairs={{0,28},{2,30},{4,24},{6,26},{8,20},{10,22},{12,16},{14,18},{16,12}... | collective-permute-start | bytes 307208 | tf_op jit(solution)/shard_map/ppermute | solution.py:317
  122.0 3.1 %collective-permute-start.32 = (bf16[400,128]{1,0:T(8,128)(2,1)S(1)}, bf16[400,128]{1,0:T(8,128)(2,1)S(1)}, u32[]{:S(2)}, u32[]{:S(2)}) collective-permute-start(bf16[400,128]{1,0:T(8,128)(2,1)S(1)} %get-tuple-element.39), channel_id=1, source_target_pairs={{0,22},{2,20},{4,18},{6,16},{8,30},{10,28},{12,26},{14,24},{16,6},... | collective-permute-start | bytes 307208 | tf_op jit(solution)/shard_map/ppermute | solution.py:317
  125.1 1.9 %collective-permute-done.28.refs_11_ = bf16[400,128]{1,0:T(8,128)(2,1)S(1)} collective-permute-done((bf16[400,128]{1,0:T(8,128)(2,1)S(1)}, bf16[400,128]{1,0:T(8,128)(2,1)S(1)}, u32[]{:S(2)}, u32[]{:S(2)}) %collective-permute-start.28) | collective-permute-done | bytes 102432 | tf_op jit(solution)/shard_map/ppermute | solution.py:317
  127.0 5.5 %collective-permute-start.33 = (bf16[400,128]{1,0:T(8,128)(2,1)S(1)}, bf16[400,128]{1,0:T(8,128)(2,1)S(1)}, u32[]{:S(2)}, u32[]{:S(2)}) collective-permute-start(bf16[400,128]{1,0:T(8,128)(2,1)S(1)} %get-tuple-element.40), channel_id=1, source_target_pairs={{0,30},{2,28},{4,26},{6,24},{8,22},{10,20},{12,18},{14,16},{16,14}... | collective-permute-start | bytes 307208 | tf_op jit(solution)/shard_map/ppermute | solution.py:317
  132.6 3.6 %collective-permute-done.31.refs_14_ = bf16[400,128]{1,0:T(8,128)(2,1)S(1)} collective-permute-done((bf16[400,128]{1,0:T(8,128)(2,1)}, bf16[400,128]{1,0:T(8,128)(2,1)S(1)}, u32[]{:S(2)}, u32[]{:S(2)}) %collective-permute-start.31) | collective-permute-done | bytes 102432 | tf_op jit(solution)/shard_map/ppermute | solution.py:317
  136.2 4.5 %collective-permute-done.33.refs_16_ = bf16[400,128]{1,0:T(8,128)(2,1)S(1)} collective-permute-done((bf16[400,128]{1,0:T(8,128)(2,1)S(1)}, bf16[400,128]{1,0:T(8,128)(2,1)S(1)}, u32[]{:S(2)}, u32[]{:S(2)}) %collective-permute-start.33) | collective-permute-done | bytes 102432 | tf_op jit(solution)/shard_map/ppermute | solution.py:317
  140.8 4.9 %shard_map.55 = f32[384,1536]{1,0:T(8,128)} custom-call(s32[2]{0:T(128)S(1)} %pad_add_fusion.me_ref, bf16[16,400,128]{2,1,0:T(8,128)(2,1)S(1)} %all-to-all-done.refs_0_, bf16[400,128]{1,0:T(8,128)(2,1)S(1)} %get-tuple-element.25.refs_1_, bf16[400,128]{1,0:T(8,128)(2,1)S(1)} %collective-permute-done.19.refs_2_, ...), custom_call_target="tpu_custom_call" | custom-call | flops 3145728 | bytes 2359296 | tf_op jit(solution)/shard_map/pallas_call | solution.py:254
  (93 shorter events, 26.3 us)
Async XLA Ops:
  0.0 11.1 %collective-permute-start.4 = (bf16[48,4096]{1,0:T(8,128)(2,1)}, bf16[48,4096]{1,0:T(8,128)(2,1)S(1)}, u32[]{:S(2)}, u32[]{:S(2)}) collective-permute-start(bf16[48,4096]{1,0:T(8,128)(2,1)} %x_ref.3), channel_id=1, source_target_pairs={{0,4},{2,6},{4,0},{6,2},{8,12},{10,14},{12,8},{14,10},{16,20},{18,... | collective-permute-start | bytes 1179656 | tf_op jit(solution)/shard_map/ppermute | solution.py:317
  1.5 19.3 %collective-permute-start = (bf16[48,4096]{1,0:T(8,128)(2,1)}, bf16[48,4096]{1,0:T(8,128)(2,1)S(1)}, u32[]{:S(2)}, u32[]{:S(2)}) collective-permute-start(bf16[48,4096]{1,0:T(8,128)(2,1)} %x_ref.3), channel_id=1, source_target_pairs={{0,16},{2,18},{4,20},{6,22},{8,24},{10,26},{12,28},{14,30},{16,0},... | collective-permute-start | bytes 1179656 | tf_op jit(solution)/shard_map/ppermute | solution.py:317
  6.2 17.0 %collective-permute-start.3 = (bf16[48,4096]{1,0:T(8,128)(2,1)S(1)}, bf16[48,4096]{1,0:T(8,128)(2,1)S(1)}, u32[]{:S(2)}, u32[]{:S(2)}) collective-permute-start(bf16[48,4096]{1,0:T(8,128)(2,1)S(1)} %shard_map.46), channel_id=1, source_target_pairs={{0,2},{2,0},{4,6},{6,4},{8,10},{10,8},{12,14},{14,12},{16,18},{18,... | collective-permute-start | bytes 1179656 | tf_op jit(solution)/shard_map/ppermute | solution.py:317
  11.1 15.2 %collective-permute-start.5 = (bf16[48,4096]{1,0:T(8,128)(2,1)S(1)}, bf16[48,4096]{1,0:T(8,128)(2,1)S(1)}, u32[]{:S(2)}, u32[]{:S(2)}) collective-permute-start(bf16[48,4096]{1,0:T(8,128)(2,1)S(1)} %collective-permute-done.4.refs_2_), channel_id=1, source_target_pairs={{0,2},{2,0},{4,6},{6,4},{8,10},{10,8},{12,14},{14,12},{16,18},{18,... | collective-permute-start | bytes 1179656 | tf_op jit(solution)/shard_map/ppermute | solution.py:317
  20.9 14.3 %collective-permute-start.8 = (bf16[48,4096]{1,0:T(8,128)(2,1)S(1)}, bf16[48,4096]{1,0:T(8,128)(2,1)S(1)}, u32[]{:S(2)}, u32[]{:S(2)}) collective-permute-start(bf16[48,4096]{1,0:T(8,128)(2,1)S(1)} %shard_map.49), channel_id=1, source_target_pairs={{0,8},{2,10},{4,12},{6,14},{8,0},{10,2},{12,4},{14,6},{16,24},{18,... | collective-permute-start | bytes 1179656 | tf_op jit(solution)/shard_map/ppermute | solution.py:317
  22.2 11.8 %collective-permute-start.1 = (bf16[48,4096]{1,0:T(8,128)(2,1)S(1)}, bf16[48,4096]{1,0:T(8,128)(2,1)S(1)}, u32[]{:S(2)}, u32[]{:S(2)}) collective-permute-start(bf16[48,4096]{1,0:T(8,128)(2,1)S(1)} %collective-permute-done.earlier_ref.refs_0_), channel_id=1, source_target_pairs={{0,2},{2,0},{4,6},{6,4},{8,10},{10,8},{12,14},{14,12},{16,18},{18,... | collective-permute-start | bytes 1179656 | tf_op jit(solution)/shard_map/ppermute | solution.py:317
  22.7 11.3 %collective-permute-start.2 = (bf16[48,4096]{1,0:T(8,128)(2,1)S(1)}, bf16[48,4096]{1,0:T(8,128)(2,1)S(1)}, u32[]{:S(2)}, u32[]{:S(2)}) collective-permute-start(bf16[48,4096]{1,0:T(8,128)(2,1)S(1)} %collective-permute-done.earlier_ref.refs_0_), channel_id=1, source_target_pairs={{0,4},{2,6},{4,0},{6,2},{8,12},{10,14},{12,8},{14,10},{16,20},{18,... | collective-permute-start | bytes 1179656 | tf_op jit(solution)/shard_map/ppermute | solution.py:317
  23.2 17.2 %collective-permute-start.9 = (bf16[48,4096]{1,0:T(8,128)(2,1)S(1)}, bf16[48,4096]{1,0:T(8,128)(2,1)S(1)}, u32[]{:S(2)}, u32[]{:S(2)}) collective-permute-start(bf16[48,4096]{1,0:T(8,128)(2,1)S(1)} %collective-permute-done.earlier_ref.refs_0_), channel_id=1, source_target_pairs={{0,8},{2,10},{4,12},{6,14},{8,0},{10,2},{12,4},{14,6},{16,24},{18,... | collective-permute-start | bytes 1179656 | tf_op jit(solution)/shard_map/ppermute | solution.py:317
  32.7 21.9 %collective-permute-start.11 = (f32[192,1280]{1,0:T(8,128)S(1)}, f32[192,1280]{1,0:T(8,128)S(1)}, u32[]{:S(2)}, u32[]{:S(2)}) collective-permute-start(f32[192,1280]{1,0:T(8,128)S(1)} %fusion.6.refs_0_.refs_2_), channel_id=1, source_target_pairs={{1,0},{3,2},{5,4},{7,6},{9,8},{11,10},{13,12},{15,14},{16,17},{18,... | collective-permute-start | bytes 2949128 | tf_op jit(solution)/shard_map/ppermute | solution.py:340
  34.6 7.8 %collective-permute-start.7 = (bf16[48,2048]{1,0:T(8,128)(2,1)S(1)}, bf16[48,2048]{1,0:T(8,128)(2,1)S(1)}, u32[]{:S(2)}, u32[]{:S(2)}) collective-permute-start(bf16[48,2048]{1,0:T(8,128)(2,1)S(1)} %get-tuple-element.24), channel_id=1, source_target_pairs={{0,2},{2,0},{4,6},{6,4},{8,10},{10,8},{12,14},{14,12},{16,18},{18,... | collective-permute-start | bytes 589832 | tf_op jit(solution)/shard_map/ppermute | solution.py:317
  35.2 15.7 %collective-permute-start.12 = (bf16[48,4096]{1,0:T(8,128)(2,1)S(1)}, bf16[48,4096]{1,0:T(8,128)(2,1)S(1)}, u32[]{:S(2)}, u32[]{:S(2)}) collective-permute-start(bf16[48,4096]{1,0:T(8,128)(2,1)S(1)} %collective-permute-done.8.refs_5_), channel_id=1, source_target_pairs={{0,2},{2,0},{4,6},{6,4},{8,10},{10,8},{12,14},{14,12},{16,18},{18,... | collective-permute-start | bytes 1179656 | tf_op jit(solution)/shard_map/ppermute | solution.py:317
  40.4 12.4 %collective-permute-start.13 = (bf16[48,4096]{1,0:T(8,128)(2,1)S(1)}, bf16[48,4096]{1,0:T(8,128)(2,1)S(1)}, u32[]{:S(2)}, u32[]{:S(2)}) collective-permute-start(bf16[48,4096]{1,0:T(8,128)(2,1)S(1)} %collective-permute-done.8.refs_5_), channel_id=1, source_target_pairs={{0,4},{2,6},{4,0},{6,2},{8,12},{10,14},{12,8},{14,10},{16,20},{18,... | collective-permute-start | bytes 1179656 | tf_op jit(solution)/shard_map/ppermute | solution.py:317
  41.7 12.8 %collective-permute-start.14 = (bf16[48,4096]{1,0:T(8,128)(2,1)S(1)}, bf16[48,4096]{1,0:T(8,128)(2,1)S(1)}, u32[]{:S(2)}, u32[]{:S(2)}) collective-permute-start(bf16[48,4096]{1,0:T(8,128)(2,1)S(1)} %collective-permute-done.5.refs_3_), channel_id=1, source_target_pairs={{0,8},{2,10},{4,12},{6,14},{8,0},{10,2},{12,4},{14,6},{16,24},{18,... | collective-permute-start | bytes 1179656 | tf_op jit(solution)/shard_map/ppermute | solution.py:317
  42.4 22.3 %collective-permute-start.15 = (bf16[48,4096]{1,0:T(8,128)(2,1)S(1)}, bf16[48,4096]{1,0:T(8,128)(2,1)S(1)}, u32[]{:S(2)}, u32[]{:S(2)}) collective-permute-start(bf16[48,4096]{1,0:T(8,128)(2,1)S(1)} %collective-permute-done.9.refs_6_), channel_id=1, source_target_pairs={{0,2},{2,0},{4,6},{6,4},{8,10},{10,8},{12,14},{14,12},{16,18},{18,... | collective-permute-start | bytes 1179656 | tf_op jit(solution)/shard_map/ppermute | solution.py:317
  52.8 12.7 %collective-permute-start.16 = (bf16[48,4096]{1,0:T(8,128)(2,1)S(1)}, bf16[48,4096]{1,0:T(8,128)(2,1)}, u32[]{:S(2)}, u32[]{:S(2)}) collective-permute-start(bf16[48,4096]{1,0:T(8,128)(2,1)S(1)} %collective-permute-done.9.refs_6_), channel_id=1, source_target_pairs={{0,4},{2,6},{4,0},{6,2},{8,12},{10,14},{12,8},{14,10},{16,20},{18,... | collective-permute-start | bytes 1179656 | tf_op jit(solution)/shard_map/ppermute | solution.py:317
  54.5 13.0 %collective-permute-start.17 = (bf16[48,4096]{1,0:T(8,128)(2,1)S(1)}, bf16[48,4096]{1,0:T(8,128)(2,1)}, u32[]{:S(2)}, u32[]{:S(2)}) collective-permute-start(bf16[48,4096]{1,0:T(8,128)(2,1)S(1)} %pad_maximum_fusion), channel_id=1, source_target_pairs={{0,8},{2,10},{4,12},{6,14},{8,0},{10,2},{12,4},{14,6},{16,24},{18,... | collective-permute-start | bytes 1179656 | tf_op jit(solution)/shard_map/ppermute | solution.py:317
  58.1 82.7 %all-to-all-start = ((bf16[16,400,128]{2,1,0:T(8,128)(2,1)}), bf16[16,400,128]{2,1,0:T(8,128)(2,1)S(1)}, u32[]{:S(2)}, u32[]{:S(2)}) async-start(bf16[16,400,128]{2,1,0:T(8,128)(2,1)} %shard_map.52), calls=%async_computation | async-start | bytes 3276800 | tf_op jit(solution)/shard_map/all_to_all | solution.py:324
  84.1 11.7 %collective-permute-start.19 = (bf16[400,128]{1,0:T(8,128)(2,1)S(1)}, bf16[400,128]{1,0:T(8,128)(2,1)S(1)}, u32[]{:S(2)}, u32[]{:S(2)}) collective-permute-start(bf16[400,128]{1,0:T(8,128)(2,1)S(1)} %get-tuple-element.26), channel_id=1, source_target_pairs={{0,8},{2,10},{4,12},{6,14},{8,0},{10,2},{12,4},{14,6},{16,24},{18,... | collective-permute-start | bytes 307208 | tf_op jit(solution)/shard_map/ppermute | solution.py:317
  84.8 12.9 %collective-permute-start.20 = (bf16[400,128]{1,0:T(8,128)(2,1)S(1)}, bf16[400,128]{1,0:T(8,128)(2,1)S(1)}, u32[]{:S(2)}, u32[]{:S(2)}) collective-permute-start(bf16[400,128]{1,0:T(8,128)(2,1)S(1)} %get-tuple-element.27), channel_id=1, source_target_pairs={{0,10},{2,8},{4,14},{6,12},{8,2},{10,0},{12,6},{14,4},{16,26},{18,... | collective-permute-start | bytes 307208 | tf_op jit(solution)/shard_map/ppermute | solution.py:317
  86.5 15.5 %collective-permute-start.21 = (bf16[400,128]{1,0:T(8,128)(2,1)S(1)}, bf16[400,128]{1,0:T(8,128)(2,1)S(1)}, u32[]{:S(2)}, u32[]{:S(2)}) collective-permute-start(bf16[400,128]{1,0:T(8,128)(2,1)S(1)} %get-tuple-element.28), channel_id=1, source_target_pairs={{0,12},{2,14},{4,8},{6,10},{8,4},{10,6},{12,0},{14,2},{16,28},{18,... | collective-permute-start | bytes 307208 | tf_op jit(solution)/shard_map/ppermute | solution.py:317
  87.9 16.5 %collective-permute-start.22 = (bf16[400,128]{1,0:T(8,128)(2,1)S(1)}, bf16[400,128]{1,0:T(8,128)(2,1)S(1)}, u32[]{:S(2)}, u32[]{:S(2)}) collective-permute-start(bf16[400,128]{1,0:T(8,128)(2,1)S(1)} %get-tuple-element.29), channel_id=1, source_target_pairs={{0,14},{2,12},{4,10},{6,8},{8,6},{10,4},{12,2},{14,0},{16,30},{18,... | collective-permute-start | bytes 307208 | tf_op jit(solution)/shard_map/ppermute | solution.py:317
  89.9 20.6 %collective-permute-start.23 = (bf16[400,128]{1,0:T(8,128)(2,1)S(1)}, bf16[400,128]{1,0:T(8,128)(2,1)S(1)}, u32[]{:S(2)}, u32[]{:S(2)}) collective-permute-start(bf16[400,128]{1,0:T(8,128)(2,1)S(1)} %get-tuple-element.30), channel_id=1, source_target_pairs={{0,2},{2,0},{4,6},{6,4},{8,10},{10,8},{12,14},{14,12},{16,18},{18,... | collective-permute-start | bytes 307208 | tf_op jit(solution)/shard_map/ppermute | solution.py:317
  95.8 14.8 %collective-permute-start.24 = (bf16[400,128]{1,0:T(8,128)(2,1)S(1)}, bf16[400,128]{1,0:T(8,128)(2,1)S(1)}, u32[]{:S(2)}, u32[]{:S(2)}) collective-permute-start(bf16[400,128]{1,0:T(8,128)(2,1)S(1)} %get-tuple-element.31), channel_id=1, source_target_pairs={{0,16},{2,18},{4,20},{6,22},{8,24},{10,26},{12,28},{14,30},{16,0},... | collective-permute-start | bytes 307208 | tf_op jit(solution)/shard_map/ppermute | solution.py:317
  97.7 19.5 %collective-permute-start.25 = (bf16[400,128]{1,0:T(8,128)(2,1)}, bf16[400,128]{1,0:T(8,128)(2,1)S(1)}, u32[]{:S(2)}, u32[]{:S(2)}) collective-permute-start(bf16[400,128]{1,0:T(8,128)(2,1)} %get-tuple-element.32), channel_id=1, source_target_pairs={{0,24},{2,26},{4,28},{6,30},{8,16},{10,18},{12,20},{14,22},{16,8},... | collective-permute-start | bytes 307208 | tf_op jit(solution)/shard_map/ppermute | solution.py:317
  102.0 15.2 %collective-permute-start.26 = (bf16[400,128]{1,0:T(8,128)(2,1)S(1)}, bf16[400,128]{1,0:T(8,128)(2,1)S(1)}, u32[]{:S(2)}, u32[]{:S(2)}) collective-permute-start(bf16[400,128]{1,0:T(8,128)(2,1)S(1)} %get-tuple-element.33), channel_id=1, source_target_pairs={{0,4},{2,6},{4,0},{6,2},{8,12},{10,14},{12,8},{14,10},{16,20},{18,... | collective-permute-start | bytes 307208 | tf_op jit(solution)/shard_map/ppermute | solution.py:317
  104.4 17.6 %collective-permute-start.27 = (bf16[400,128]{1,0:T(8,128)(2,1)S(1)}, bf16[400,128]{1,0:T(8,128)(2,1)S(1)}, u32[]{:S(2)}, u32[]{:S(2)}) collective-permute-start(bf16[400,128]{1,0:T(8,128)(2,1)S(1)} %get-tuple-element.34), channel_id=1, source_target_pairs={{0,18},{2,16},{4,22},{6,20},{8,26},{10,24},{12,30},{14,28},{16,2},... | collective-permute-start | bytes 307208 | tf_op jit(solution)/shard_map/ppermute | solution.py:317
  110.5 16.5 %collective-permute-start.28 = (bf16[400,128]{1,0:T(8,128)(2,1)S(1)}, bf16[400,128]{1,0:T(8,128)(2,1)S(1)}, u32[]{:S(2)}, u32[]{:S(2)}) collective-permute-start(bf16[400,128]{1,0:T(8,128)(2,1)S(1)} %get-tuple-element.35), channel_id=1, source_target_pairs={{0,26},{2,24},{4,30},{6,28},{8,18},{10,16},{12,22},{14,20},{16,10}... | collective-permute-start | bytes 307208 | tf_op jit(solution)/shard_map/ppermute | solution.py:317
  110.5 22.1 %collective-permute-start.29 = (bf16[400,128]{1,0:T(8,128)(2,1)}, bf16[400,128]{1,0:T(8,128)(2,1)S(1)}, u32[]{:S(2)}, u32[]{:S(2)}) collective-permute-start(bf16[400,128]{1,0:T(8,128)(2,1)} %get-tuple-element.36), channel_id=1, source_target_pairs={{0,6},{2,4},{4,2},{6,0},{8,14},{10,12},{12,10},{14,8},{16,22},{18,... | collective-permute-start | bytes 307208 | tf_op jit(solution)/shard_map/ppermute | solution.py:317
  117.2 15.4 %collective-permute-start.30 = (bf16[400,128]{1,0:T(8,128)(2,1)}, bf16[400,128]{1,0:T(8,128)(2,1)S(1)}, u32[]{:S(2)}, u32[]{:S(2)}) collective-permute-start(bf16[400,128]{1,0:T(8,128)(2,1)} %get-tuple-element.37), channel_id=1, source_target_pairs={{0,20},{2,22},{4,16},{6,18},{8,28},{10,30},{12,24},{14,26},{16,4},... | collective-permute-start | bytes 307208 | tf_op jit(solution)/shard_map/ppermute | solution.py:317
  117.2 19.0 %collective-permute-start.31 = (bf16[400,128]{1,0:T(8,128)(2,1)}, bf16[400,128]{1,0:T(8,128)(2,1)S(1)}, u32[]{:S(2)}, u32[]{:S(2)}) collective-permute-start(bf16[400,128]{1,0:T(8,128)(2,1)} %get-tuple-element.38), channel_id=1, source_target_pairs={{0,28},{2,30},{4,24},{6,26},{8,20},{10,22},{12,16},{14,18},{16,12}... | collective-permute-start | bytes 307208 | tf_op jit(solution)/shard_map/ppermute | solution.py:317
  122.0 14.2 %collective-permute-start.32 = (bf16[400,128]{1,0:T(8,128)(2,1)S(1)}, bf16[400,128]{1,0:T(8,128)(2,1)S(1)}, u32[]{:S(2)}, u32[]{:S(2)}) collective-permute-start(bf16[400,128]{1,0:T(8,128)(2,1)S(1)} %get-tuple-element.39), channel_id=1, source_target_pairs={{0,22},{2,20},{4,18},{6,16},{8,30},{10,28},{12,26},{14,24},{16,6},... | collective-permute-start | bytes 307208 | tf_op jit(solution)/shard_map/ppermute | solution.py:317
  127.0 13.8 %collective-permute-start.33 = (bf16[400,128]{1,0:T(8,128)(2,1)S(1)}, bf16[400,128]{1,0:T(8,128)(2,1)S(1)}, u32[]{:S(2)}, u32[]{:S(2)}) collective-permute-start(bf16[400,128]{1,0:T(8,128)(2,1)S(1)} %get-tuple-element.40), channel_id=1, source_target_pairs={{0,30},{2,28},{4,26},{6,24},{8,22},{10,20},{12,18},{14,16},{16,14}... | collective-permute-start | bytes 307208 | tf_op jit(solution)/shard_map/ppermute | solution.py:317
  (16 other events, 120.1 us)
